TPU v7x, 128 devices: a whole 4x4x4 slice. The times are simulated.
128 devices in a mesh: seq: 4 (over x), head: 32 (over z, y, core).
Axes of the slice: x: 4, y: 4, z: 4, core: 2. Of those that a mesh axis runs over, the one named last changes fastest.
Arguments:
- tokens: bfloat16 [2048, 2048], P('seq'), may hold values from -40 to 40
- attention_gain: float32 [2048], replicated, may hold values from 0.1 to 1.9
- head_weights: bfloat16 [3, 2048, 2048], P(None, None, 'head'), may hold values from -1 to 1
- carried_state: float32 [8256, 2048], P(None, 'head'), may hold values from -384 to 384
- output_weight: bfloat16 [2048, 2048], P('head'), may hold values from -0.125 to 0.125
- expert_gain: float32 [2048], replicated, may hold values from 0.1 to 1.9
- router_weight: bfloat16 [2048, 64], replicated, may hold values from -0.125 to 0.125
- expert_index: int32 [2048, 8], P(('seq', 'head')), may hold values from 0 to 63, all different within a row; in each aligned block of 16 rows (0 to 15, 16 to 31, ...) at most 3 rows name the same one
- expert_first: bfloat16 [2, 2048, 65536], P(None, None, ('seq', 'head')), may hold values from -0.125 to 0.125
- expert_second: bfloat16 [65536, 2048], P(('seq', 'head')), may hold values from -0.1875 to 0.1875
Outputs:
- layer_out: bfloat16 [2048, 2048], P(('seq', 'head'))
Inputs may be any that keep to these rules, and one draw needn't show every extreme that they name: `expert_index`: each row names 8 different experts; within each aligned block of 16 rows (the rows of one device) no expert is named by more than 3 rows.
All inputs are finite; a program needn't handle non-finite values.
Results may differ from a plain program's by a relative error of at most 0.019.
Values may be sent and summed in bfloat16 or wider, within the bound.
No kernel may reach another device: no remote copies, remote signals or barrier semaphores. Data moves between devices by JAX's collectives and lax.ppermute only.
A program may use at most 128 MiB of HBM per device.

v0:
```python
import math

import jax
import jax.numpy as jnp
import numpy as np
from jax import lax
from jax.sharding import PartitionSpec as P

HD = 128
EXPERTS = 64
TOP = 8


def partner_2(array, axis, apart):
    return lax.ppermute(array, axis, [(i, i ^ 1 << apart) for i in range(lax.axis_size(axis))])


def entering(array, axis, combine, identity):
    count, position = (lax.axis_size(axis), lax.axis_index(axis))
    everything = lax.all_gather(
        array.astype(jnp.bfloat16 if array.dtype == jnp.float32 else array.dtype), axis
    )
    start = jnp.broadcast_to(jnp.asarray(identity, array.dtype), array.shape)

    def hop(k, before):
        reached = k < position
        new = combine(before, everything[k].astype(array.dtype))
        return jnp.where(reached, new, before)

    return lax.fori_loop(0, count, hop, start)


def pair_tables(breadth):
    pair_rows = []
    pair_factor = []
    for first in range(breadth):
        for second in range(first, breadth):
            pair_rows.append(first * breadth + second)
            pair_factor.append(1.0 if first == second else math.sqrt(2.0))
    lookup = np.zeros((breadth, breadth), np.int32)
    spread = np.zeros((breadth, breadth), np.float32)
    place = 0
    for first in range(breadth):
        for second in range(first, breadth):
            lookup[first, second] = place
            lookup[second, first] = place
            spread[first, second] = 1.0 if first == second else math.sqrt(2.0) / 2.0
            spread[second, first] = spread[first, second]
            place += 1
    return (
        np.array(pair_rows, np.int32),
        np.array(pair_factor, np.float32),
        lookup.reshape(-1),
        spread.reshape(-1),
    )


def norm_scaled(values, gain):
    return values * lax.rsqrt(jnp.mean(values * values, axis=-1, keepdims=True) + 1e-06) * gain


def within_shard(query_rows, key_rows, value_rows):
    scores = lax.dot_general(
        query_rows, key_rows, (((1,), (1,)), ((), ())), preferred_element_type=jnp.float32
    )
    places = jnp.arange(query_rows.shape[0], dtype=jnp.int32)
    weights = jnp.where(places[None, :] <= places[:, None], scores * scores, 0.0)
    return jnp.dot(weights, value_rows.astype(jnp.float32), precision=lax.Precision.HIGHEST)


def build_state(key_rows, value_rows, block_rows):
    breadth = key_rows.shape[1]
    columns = value_rows.shape[1]

    def add_block(block_num, running):
        key_block = key_rows.astype(jnp.float32)
        value_block = value_rows.astype(jnp.float32)
        products = (key_block[:, :, None] * value_block[:, None, :]).reshape(
            block_rows, breadth * columns
        )
        return running + lax.dot_general(
            key_block, products, (((0,), (0,)), ((), ())), precision=lax.Precision.HIGHEST
        )

    initial = jnp.zeros((breadth, breadth * columns), jnp.float32)
    full_state = lax.fori_loop(0, key_rows.shape[0] // block_rows, add_block, initial).reshape(
        breadth * breadth, columns
    )
    pair_rows, pair_factor, lookup, spread = pair_tables(breadth)
    return jnp.take(full_state, jnp.asarray(pair_rows), axis=0) * jnp.asarray(pair_factor)[:, None]


def apply_state(query_rows, memory, block_rows):
    breadth = query_rows.shape[1]
    columns = memory.shape[1]
    pair_rows, pair_factor, lookup, spread = pair_tables(breadth)
    symmetric = (
        jnp.take(memory, jnp.asarray(lookup), axis=0) * jnp.asarray(spread)[:, None]
    ).reshape(breadth, breadth * columns)

    def one_block(block_num):
        query_block = query_rows.astype(jnp.float32)
        inner = jnp.dot(query_block, symmetric, precision=lax.Precision.HIGHEST).reshape(
            block_rows, breadth, columns
        )
        return jnp.sum(inner * query_block[:, :, None], axis=1)

    blocks = lax.map(one_block, jnp.arange(query_rows.shape[0] // block_rows, dtype=jnp.int32))
    return blocks.reshape(query_rows.shape[0], columns)


def add_pair(earlier, later):
    return earlier + later


def body(
    tokens,
    attention_gain,
    head_weights,
    carried_state,
    output_weight,
    expert_gain,
    router_weight,
    expert_index,
    expert_first,
    expert_second,
):
    shard_rows = tokens.shape[0]
    model_width = tokens.shape[1]
    block_rows = min(shard_rows, 512)
    floats = tokens.astype(jnp.float32)
    normed = norm_scaled(floats, attention_gain).astype(jnp.bfloat16)
    projected = jnp.einsum(
        "td,adc->atc", normed, head_weights, preferred_element_type=jnp.float32
    ).astype(jnp.bfloat16)
    query_rows, key_rows, value_rows = (projected[0], projected[1], projected[2])
    share = value_rows.shape[1]
    mine = jnp.stack([query_rows, key_rows])
    partner = partner_2(mine, "head", 0)
    lower = lax.axis_index("head") % 2 == 0
    joined = jnp.where(
        lower, jnp.concatenate([mine, partner], axis=2), jnp.concatenate([partner, mine], axis=2)
    )
    query_rows, key_rows = (joined[0], joined[1])
    memories = jnp.stack([build_state(key_rows, value_rows, block_rows)])
    prefix = entering(memories, "seq", add_pair, jnp.zeros_like(memories))
    nearby = within_shard(query_rows, key_rows, value_rows)
    carried = apply_state(query_rows, carried_state + prefix[0], block_rows)
    raw_heads = [(nearby + carried) / HD]
    raw_stack = jnp.stack(raw_heads)
    squares = jnp.sum(raw_stack * raw_stack, axis=2, keepdims=True)
    squares = squares + partner_2(squares, "head", 0)
    scaled_heads = (raw_stack * lax.rsqrt(squares / HD + 1e-06)).astype(jnp.bfloat16)
    attended = scaled_heads.transpose(1, 0, 2).reshape(shard_rows, share)
    slab_rows = expert_index.shape[0]
    attention_sum = lax.psum_scatter(
        jnp.dot(attended, output_weight, preferred_element_type=jnp.float32).astype(jnp.bfloat16),
        "head",
        scatter_dimension=0,
        tiled=True,
    ).astype(jnp.float32)
    token_slab = lax.dynamic_slice_in_dim(floats, lax.axis_index("head") * slab_rows, slab_rows, 0)
    residual = token_slab + attention_sum
    expert_input = norm_scaled(residual, expert_gain).astype(jnp.bfloat16)
    logits = jnp.dot(expert_input, router_weight, preferred_element_type=jnp.float32)
    matches = expert_index[:, :, None] == jnp.arange(EXPERTS, dtype=jnp.int32)
    gate_values = jax.nn.sigmoid(jnp.sum(jnp.where(matches, logits[:, None, :], 0.0), axis=2))
    flat_matches = matches.reshape(slab_rows * TOP, EXPERTS).astype(jnp.int32)
    earlier = jnp.cumsum(flat_matches, axis=0) - flat_matches
    slots = jnp.sum(earlier * flat_matches, axis=1).reshape(slab_rows, TOP)
    devices = lax.axis_size("seq") * lax.axis_size("head")
    piece_count = max(1, devices // EXPERTS)
    local_experts = max(1, EXPERTS // devices)
    capacity = max(2, 3 * slab_rows * TOP // (2 * EXPERTS))
    groups = EXPERTS * piece_count
    targets = (slots * groups + expert_index * piece_count)[:, :, None] + jnp.arange(
        piece_count, dtype=jnp.int32
    )
    send_map = jnp.sum(
        (
            targets.reshape(slab_rows, TOP * piece_count, 1)
            == jnp.arange(capacity * groups, dtype=jnp.int32)
        ).astype(jnp.bfloat16),
        axis=1,
    )
    outgoing = (
        lax.dot_general(
            send_map, expert_input, (((0,), (0,)), ((), ())), preferred_element_type=jnp.float32
        )
        .astype(jnp.bfloat16)
        .reshape(capacity, groups, model_width)
    )
    cells = capacity * EXPERTS
    combine_map = jnp.sum(
        jnp.where(
            (slots * EXPERTS + expert_index)[:, :, None] == jnp.arange(cells, dtype=jnp.int32),
            gate_values[:, :, None],
            0.0,
        ),
        axis=1,
    )
    piece_width = expert_first.shape[2] // local_experts
    first_local = expert_first.reshape(2, model_width, local_experts, piece_width)
    second_local = expert_second.reshape(local_experts, piece_width, model_width)
    arrived = lax.all_to_all(outgoing, ("seq", "head"), split_axis=1, concat_axis=1, tiled=True)
    slot_count = arrived.shape[0]
    grouped = arrived.reshape(slot_count, devices, local_experts, model_width)
    paired = jnp.einsum(
        "ksed,gdef->gksef", grouped, first_local, preferred_element_type=jnp.float32
    )
    hidden = (jax.nn.silu(paired[0]) * paired[1]).astype(jnp.bfloat16)
    produced = jnp.einsum(
        "ksef,efd->ksed", hidden, second_local, preferred_element_type=jnp.float32
    ).astype(jnp.bfloat16)
    returned = lax.all_to_all(
        produced.reshape(slot_count, devices * local_experts, model_width),
        ("seq", "head"),
        split_axis=1,
        concat_axis=1,
        tiled=True,
    )
    summed = jnp.sum(
        returned.reshape(capacity, EXPERTS, piece_count, model_width).astype(jnp.float32), axis=2
    )
    expert_sum = jnp.dot(
        combine_map, summed.reshape(cells, model_width), precision=lax.Precision.HIGHEST
    )
    return (residual + expert_sum).astype(jnp.bfloat16)


def solution(mesh):
    in_specs = (
        P("seq", None),
        P(),
        P(None, None, "head"),
        P(None, "head"),
        P("head", None),
        P(),
        P(),
        P(("seq", "head"), None),
        P(None, None, ("seq", "head")),
        P(("seq", "head"), None),
    )
    out_specs = P(("seq", "head"), None)
    return jax.shard_map(body, mesh=mesh, in_specs=in_specs, out_specs=out_specs, check_vma=False)
```

profile of v0, /device:TPU:0, one launch (start us, length us, event | category | flops | bytes accessed | tf_op | source)
XLA Modules:
  0.0 436.3 jit_solution(13381711311372783268)
XLA Ops:
  6.5 2.2 multiply_reduce_fusion.1
  8.8 2.7 fusion.5
  11.6 0.1 collective-permute-start
  11.7 1.3 collective-permute-done
  13.1 0.8 fusion.25
  13.8 8.2 %broadcast_multiply_fusion = f32[512,128,64]{0,2,1:T(8,128)} fusion(f32[512,64]{0,1:T(8,128)S(1)} %fusion.30, f32[512,128]{0,1:T(8,128)S(1)} %get-tuple-element.152), kind=kLoop, calls=%fused_computation.5 | loop fusion | flops 4194304 | bytes 17170432 | tf_op jit(solution)/shard_map/while/body/eval_jaxpr/mul | solution.py:78
  22.1 14.5 %fusion.24 = f32[128,8192]{1,0:T(8,128)} fusion(f32[512,8192]{0,1:T(8,128)} %bitcast.79, bf16[2,512,128]{1,2,0:T(8,128)(2,1)S(1)} %maximum_select_fusion), kind=kOutput, calls=%fused_computation.51 | convolution fusion | flops 6442450944 | bytes 21102592 | tf_op jit(solution)/shard_map/while/body/eval_jaxpr/dot_general | solution.py:81
  36.5 7.9 %reshape.225 = f32[16384,64]{1,0:T(8,128)} reshape(f32[128,8192]{1,0:T(8,128)} %fusion.24) | data formatting | bytes 8388608 | tf_op jit(solution)/shard_map/reshape | solution.py:86
  44.4 19.6 %gather_fusion = f32[8256,64]{1,0:T(8,128)} fusion(f32[16384,64]{1,0:T(8,128)} %reshape.225, s32[9216]{0:T(1024)S(1)} %pad_clamp_fusion), kind=kCustom, calls=%fused_computation | custom fusion | bytes 4260096 | tf_op jit(solution)/shard_map/jit(_take)/gather | solution.py:90
  64.0 6.0 %fusion = bf16[1,1,8256,64]{3,2,1,0:T(8,128)(2,1)} fusion(f32[8256,64]{1,0:T(8,128)} %gather_fusion, f32[8256]{0:T(1024)S(1)} %copy-done.10), kind=kLoop, calls=%fused_computation.8 | loop fusion | flops 1056768 | bytes 3203328 | tf_op jit(solution)/shard_map/convert_element_type | solution.py:21
  70.1 3.7 copy.100
  73.8 0.2 reduce-scatter.2.cloned.1.call-start
  74.1 4.7 %copy.102 = f32[8256,64]{1,0:T(8,128)} copy(f32[8256,64]{0,1:T(8,128)} %param.19) | data formatting | bytes 4227072 | tf_op args[3]
  78.7 2.2 mul.188
  81.0 5.7 %copy.103 = f32[128,8192]{1,0:T(8,128)} copy(f32[128,8192]{0,1:T(8,128)} %bitcast.80) | data formatting | bytes 8388608 | tf_op jit(solution)/shard_map/mul | solution.py:98
  86.7 1.3 fusion.16
  88.0 37.2 %all-gather.2.cloned.1.call-done = bf16[4,1,8256,64]{2,3,1,0:T(8,128)(2,1)} async-done(((bf16[1,1,8256,64]{2,3,1,0:T(8,128)(2,1)}), bf16[4,1,8256,64]{2,3,1,0:T(8,128)(2,1)}) %all-gather.2.cloned.1.call-update) | async-done | bytes 4227088 | tf_op jit(solution)/shard_map/all_gather | solution.py:20
  125.2 31.5 %while.9 = (s32[]{:T(128)}, f32[1,8256,64]{2,1,0:T(8,128)}, s32[]{:T(128)}, bf16[4,1,8256,64]{2,3,1,0:T(8,128)(2,1)}, s32[]{:T(128)}, /*index=5*/s32[]{:T(128)}) while((s32[]{:T(128)}, f32[1,8256,64]{2,1,0:T(8,128)}, s32[]{:T(128)}, bf16[4,1,8256,64]{2,3,1,0:T(8,128)(2,1)}, s32[]{:T(128)}, /*index=5*/s32[]{:T(128)}) %tuple.44), condition=%wide.region_2.3_spmd.clone, body=%wide.region_1.2_spmd.clone.sunk | while | flops 2113540 | bytes 9511005 | solution.py:30
  125.2 1.3 constant_dynamic-slice_fusion.2
  126.5 2.4 copy.129
  128.9 3.5 add_select_fusion.2
  132.4 1.3 constant_dynamic-slice_fusion.2
  133.7 2.4 copy.129
  136.1 4.4 %add_select_fusion.2 = f32[1,8256,64]{2,1,0:T(8,128)} fusion(f32[1,8256,64]{2,1,0:T(8,128)} %get-tuple-element.190, bf16[1,1,8256,64]{3,2,1,0:T(8,128)(2,1)} %copy.129, pred[]{:T(512)S(6)} %compare.4, pred[]{:T(512)S(6)} %lt.54), kind=kLoop, calls=%fused_computation.2.clone.1 | loop fusion | flops 2113536 | bytes 5283842 | tf_op jit(solution)/shard_map/while/body/eval_jaxpr/jit(_where)/select_n | solution.py:28
  140.5 1.3 constant_dynamic-slice_fusion.2
  141.8 2.4 copy.129
  144.2 4.4 %add_select_fusion.2 = f32[1,8256,64]{2,1,0:T(8,128)} fusion(f32[1,8256,64]{2,1,0:T(8,128)} %get-tuple-element.190, bf16[1,1,8256,64]{3,2,1,0:T(8,128)(2,1)} %copy.129, pred[]{:T(512)S(6)} %compare.4, pred[]{:T(512)S(6)} %lt.54), kind=kLoop, calls=%fused_computation.2.clone.1 | loop fusion | flops 2113536 | bytes 5283842 | tf_op jit(solution)/shard_map/while/body/eval_jaxpr/jit(_where)/select_n | solution.py:28
  148.6 1.3 constant_dynamic-slice_fusion.2
  149.9 2.4 copy.129
  152.3 4.4 %add_select_fusion.2 = f32[1,8256,64]{2,1,0:T(8,128)} fusion(f32[1,8256,64]{2,1,0:T(8,128)} %get-tuple-element.190, bf16[1,1,8256,64]{3,2,1,0:T(8,128)(2,1)} %copy.129, pred[]{:T(512)S(6)} %compare.4, pred[]{:T(512)S(6)} %lt.54), kind=kLoop, calls=%fused_computation.2.clone.1 | loop fusion | flops 2113536 | bytes 5283842 | tf_op jit(solution)/shard_map/while/body/eval_jaxpr/jit(_where)/select_n | solution.py:28
  156.7 5.1 %bitcast_add_fusion = f32[8256,64]{1,0:T(8,128)} fusion(f32[8256,64]{1,0:T(8,128)} %copy.102, f32[1,8256,64]{2,1,0:T(8,128)} %get-tuple-element.108), kind=kLoop, calls=%fused_computation.6 | loop fusion | flops 528384 | bytes 6340608 | tf_op jit(solution)/shard_map/add | solution.py:148
  161.8 56.6 %gather_fusion.1 = f32[16384,64]{1,0:T(8,128)} fusion(f32[8256,64]{1,0:T(8,128)} %bitcast_add_fusion, s32[16384]{0:T(1024)S(1)} %broadcast_clamp_fusion), kind=kCustom, calls=%fused_computation.1 | custom fusion | bytes 8454144 | tf_op jit(solution)/shard_map/jit(_take)/gather | solution.py:98
  218.4 7.9 %gather.15 = f32[128,8192]{1,0:T(8,128)} reshape(f32[16384,64]{1,0:T(8,128)} %gather_fusion.1) | data formatting | bytes 8388608 | tf_op jit(solution)/shard_map/jit(_take)/gather | solution.py:98
  226.3 6.0 %multiply_bitcast_fusion = f32[8192,128]{0,1:T(8,128)} fusion(f32[128,8192]{1,0:T(8,128)} %gather.15, f32[128,8192]{1,0:T(8,128)} %copy.103), kind=kLoop, calls=%fused_computation.13 | loop fusion | flops 1048576 | bytes 12582912 | tf_op jit(solution)/shard_map/while/body/eval_jaxpr/dot_general | solution.py:103
  232.2 5.6 %copy.104 = f32[8192,128]{1,0:T(8,128)} copy(f32[8192,128]{0,1:T(8,128)} %multiply_bitcast_fusion) | data formatting | bytes 8388608 | tf_op jit(solution)/shard_map/while/body/eval_jaxpr/dot_general | solution.py:103
  237.9 15.6 %multiply_reduce_fusion = f32[512,64]{0,1:T(8,128)S(1)} fusion(f32[512,128]{0,1:T(8,128)S(1)} %copy-done.4, f32[128,64,128]{2,1,0:T(8,128)} %bitcast.83, bf16[2,512,128]{1,2,0:T(8,128)(2,1)S(1)} %maximum_select_fusion), kind=kOutput, calls=%fused_computation.4 | convolution fusion | flops 6450806784 | bytes 4718592 | tf_op jit(solution)/shard_map/while/body/eval_jaxpr/dot_general | solution.py:103
  253.5 1.5 multiply_reduce_fusion.3
  255.0 0.3 collective-permute-start.1
  255.3 1.1 collective-permute-done.1
  256.5 2.1 convolution_convert_fusion
  258.6 4.0 convert_element_type.115
  262.7 0.1 eq.54
  262.8 0.1 fusion.28
  262.9 0.2 reduce_window_sum.11
  263.0 0.2 select_reduce_fusion.2
  263.4 0.1 add.164
  263.6 0.2 fusion.21
  263.8 74.3 %reduce-scatter.2.cloned.1.call-done = bf16[16,2048]{1,0:T(8,128)(2,1)} async-done(((bf16[512,2048]{1,0:T(8,128)(2,1)}), bf16[16,2048]{1,0:T(8,128)(2,1)}) %reduce-scatter.2.cloned.1.call-update) | async-done | bytes 65552 | tf_op jit(solution)/shard_map/reduce_scatter | solution.py:156
  338.1 1.1 multiply_reduce_fusion.2
  339.2 1.0 multiply_convert_fusion.2
  340.2 0.6 convolution_convert_fusion.1
  340.8 1.4 copy.112
  342.2 38.1 %all_to_all.10 = bf16[3,128,2048]{2,0,1:T(4,128)(2,1)S(1)} all-to-all(bf16[3,128,2048]{2,0,1:T(4,128)(2,1)S(1)} %copy.112), channel_id=1, replica_groups=mesh['seq'=4,'head'=32] {'seq','head'}, dimensions={1} | all-to-all | bytes 3145728 | tf_op jit(solution)/shard_map/all_to_all | solution.py:205
  380.3 2.9 fusion.11
  383.2 1.0 convolution_convert_fusion.2
  384.3 2.7 copy.114
  387.0 6.0 %all-to-all-start.1 = ((bf16[3,128,2048]{2,0,1:T(4,128)(2,1)}), bf16[3,128,2048]{2,0,1:T(4,128)(2,1)}, u32[]{:S(2)}, u32[]{:S(2)}) async-start(bf16[3,128,2048]{2,0,1:T(4,128)(2,1)} %copy.114), calls=%async_computation.2 | async-start | bytes 4194304 | tf_op jit(solution)/shard_map/all_to_all | solution.py:215
  393.1 0.2 fusion.32
  393.3 0.2 select_reduce_fusion.1
  393.5 0.1 select_reduce_fusion
  393.6 29.1 %all-to-all-done.1 = bf16[3,128,2048]{2,0,1:T(4,128)(2,1)} async-done(((bf16[3,128,2048]{2,0,1:T(4,128)(2,1)}), bf16[3,128,2048]{2,0,1:T(4,128)(2,1)}, u32[]{:S(2)}, u32[]{:S(2)}) %all-to-all-start.1) | async-done | bytes 1572896 | tf_op jit(solution)/shard_map/all_to_all | solution.py:215
  422.8 3.4 convert_reduce_fusion
  426.2 0.9 copy.115
  427.1 2.4 fusion.4
  (53 shorter events, 0.7 us)
Async XLA Ops:
  6.5 376.7 %copy-start = (bf16[512,2048]{1,0:T(8,128)(2,1)S(1)}, bf16[512,2048]{1,0:T(8,128)(2,1)}, u32[]{:S(2)}) copy-start(bf16[512,2048]{1,0:T(8,128)(2,1)} %param.25) | copy-start | bytes 6291460
  6.5 118.7 %all-gather.2.cloned.1.call-start = ((), (), s32[]{:S(2)}) async-start(), calls=%async_computation.3 | async-start | bytes 5324800 | tf_op jit(solution)/shard_map/all_gather | solution.py:20
  8.8 2.9 copy-start.9
  11.5 10.6 %copy-start.1 = (bf16[3,512,64]{1,2,0:T(8,128)(2,1)}, bf16[3,512,64]{1,2,0:T(8,128)(2,1)S(1)}, u32[]{:S(2)}) copy-start(bf16[3,512,64]{1,2,0:T(8,128)(2,1)S(1)} %convert_bitcast_fusion) | copy-start | bytes 589828
  11.6 1.4 collective-permute-start
  44.4 19.6 %copy-start.10 = (f32[8256]{0:T(1024)S(1)}, f32[8256]{0:T(1024)}, u32[]{:S(2)}) copy-start(f32[8256]{0:T(1024)} %constant.132.clone) | copy-start | bytes 99076
  73.8 5.0 %copy-start.7 = (f32[128,128]{0,1:T(8,128)S(1)}, f32[128,128]{0,1:T(8,128)}, u32[]{:S(2)}) copy-start(f32[128,128]{0,1:T(8,128)} %constant.151) | copy-start | bytes 196612
  73.8 264.3 %reduce-scatter.2.cloned.1.call-start = ((), (), s32[]{:S(2)}) async-start(), calls=%async_computation.4 | async-start | bytes 2162688 | tf_op jit(solution)/shard_map/reduce_scatter | solution.py:156
  81.0 5.7 %copy-start.8 = (s32[16384]{0:T(1024)S(1)}, s32[16384]{0:T(1024)}, u32[]{:S(2)}) copy-start(s32[16384]{0:T(1024)} %constant.155) | copy-start | bytes 196612
  232.2 5.6 %copy-start.4 = (f32[512,128]{0,1:T(8,128)S(1)}, f32[512,128]{0,1:T(8,128)}, u32[]{:S(2)}) copy-start(f32[512,128]{0,1:T(8,128)} %get-tuple-element.153) | copy-start | bytes 786436
  237.9 15.6 %copy-start.2 = (f32[512,512]{1,0:T(8,128)S(1)}, f32[512,512]{1,0:T(8,128)}, u32[]{:S(2)}) copy-start(f32[512,512]{1,0:T(8,128)} %fusion.16) | copy-start | bytes 3145732
  237.9 18.6 %copy-start.6 = (bf16[64,2048]{1,0:T(8,128)(2,1)S(1)}, bf16[64,2048]{1,0:T(8,128)(2,1)}, u32[]{:S(2)}) copy-start(bf16[64,2048]{1,0:T(8,128)(2,1)} %param.20) | copy-start | bytes 786436
  255.0 1.5 collective-permute-start.1
  258.5 4.1 copy-start.11
  258.5 80.6 %copy-start.12 = (f32[2048]{0:T(1024)S(1)}, f32[2048]{0:T(1024)}, u32[]{:S(2)}) copy-start(f32[2048]{0:T(1024)} %param.21) | copy-start | bytes 24580
  340.8 39.5 %copy-start.13 = (bf16[2,2048,512]{2,1,0:T(8,128)(2,1)S(1)}, bf16[2,2048,512]{2,1,0:T(8,128)(2,1)}, u32[]{:S(2)}) copy-start(bf16[2,2048,512]{2,1,0:T(8,128)(2,1)} %param.24) | copy-start | bytes 12582916
  384.3 8.9 %copy-start.5 = (bf16[2048,64]{0,1:T(8,128)(2,1)S(1)}, bf16[2048,64]{0,1:T(8,128)(2,1)}, u32[]{:S(2)}) copy-start(bf16[2048,64]{0,1:T(8,128)(2,1)} %param.22) | copy-start | bytes 786436
  387.0 35.8 %all-to-all-start.1 = ((bf16[3,128,2048]{2,0,1:T(4,128)(2,1)}), bf16[3,128,2048]{2,0,1:T(4,128)(2,1)}, u32[]{:S(2)}, u32[]{:S(2)}) async-start(bf16[3,128,2048]{2,0,1:T(4,128)(2,1)} %copy.114), calls=%async_computation.2 | async-start | bytes 4194304 | tf_op jit(solution)/shard_map/all_to_all | solution.py:215
  393.0 34.1 %copy-start.3 = (bf16[16,2048]{1,0:T(8,128)(2,1)S(1)}, bf16[16,2048]{1,0:T(8,128)(2,1)}, u32[]{:S(2)}) copy-start(bf16[16,2048]{1,0:T(8,128)(2,1)} %reduce-scatter.2.cloned.1.call-done) | copy-start | bytes 196612
Sparse Core Ops, SparseCore 0:
  73.9 51.2 all-gather.1
  258.7 79.3 reduce-scatter.1
where the time goes:
time: 438 us; the launch traced here: 436 us
  waiting for transfers between devices  143 us (33%)
  local copies, waits for them, and re-layouts  134 us (31%)
  other arithmetic  55.6 us (13%)
  matrix products  44.7 us (10%)
  blocking collectives  38.1 us (9%)
  between operations  13.8 us (3%)
  starting transfers between devices  6.65 us (2%)
    reduce_scatter x1, waiting for transfers between devices, body(): lax.psum_scatter(jnp.dot(attended, output_weight, preferred_element_type=...  74.3 us
    gather x2, local copies, waits for them, and re-layouts, apply_state(): jnp.take(memory, jnp.asarray(lookup), axis=0) * jnp.asarray(spread)[:, None]  64.5 us
    all_to_all x1, blocking collectives, body(): lax.all_to_all(outgoing, ('seq', 'head'), split_axis=1, concat_axis=1, ti...  38.1 us
    all_gather x1, waiting for transfers between devices, entering(): lax.all_gather(array.astype(jnp.bfloat16 if array.dtype == jnp.float32 el...  37.2 us
    all_to_all x1, waiting for transfers between devices, body(): lax.all_to_all(produced.reshape(slot_count, devices * local_experts, mode...  29.1 us
    gather x1, local copies, waits for them, and re-layouts, build_state(): jnp.take(full_state, jnp.asarray(pair_rows), axis=0)  19.6 us
    select_n x4, other arithmetic, hop(): return jnp.where(reached, new, before)  16.7 us
    dot_general x1, matrix products, one_block(): jnp.dot(query_block, symmetric, precision=lax.Precision.HIGHEST)  15.6 us
  transfers between devices with their start and end apart: 5, of which 5 were waited for; matrix products, arithmetic and copies ran while one was open for 5% of the time, Pallas kernels for 0%

commit v1 on v0

v1 whole, which is shorter than its diff:
```python
import functools
import math

import jax
import jax.numpy as jnp
from jax import lax
from jax.experimental import pallas as pl
from jax.experimental.pallas import tpu as pltpu
from jax.sharding import Mesh
from jax.sharding import PartitionSpec as P

HD = 128
D = 2048
STATE = 8256
EXPERTS = 64
TOP = 8
CAP = 3
SLAB = 16
HALF = 256
SHARD = 512
CHIP_AXES = ("x", "z", "y")


def swap_core(array):
    return lax.ppermute(array, "c", [(0, 1), (1, 0)])


def shift(array, axis, step):
    return lax.ppermute(array, axis, [(i, (i + step) % 4) for i in range(4)])


def norm_scaled(values, gain):
    return values * lax.rsqrt(jnp.mean(values * values, axis=-1, keepdims=True) + 1e-06) * gain


GROUP = 8
LOOPED = 112
TAIL_AT = 8064


def carried_kernel(m_ref, q_own_ref, q_other_ref, out_ref, q_ref, w_ref, tail_ref):
    q_ref[:, :HALF] = q_own_ref[...].astype(jnp.float32)
    q_ref[:, HALF:] = q_other_ref[...].astype(jnp.float32)
    tail_ref[:, : STATE - TAIL_AT] = m_ref[:, TAIL_AT:]
    q_cols = jnp.concatenate([q_own_ref[...], q_other_ref[...]], axis=1)
    lane = lax.broadcasted_iota(jnp.int32, (64, 128), 1)
    root = math.sqrt(2.0)

    def piece(first, second, turn, i):
        joined = jnp.where(
            lane < 128 - turn,
            pltpu.roll(first, (128 - turn) % 128, 1),
            pltpu.roll(second, (128 - turn) % 128, 1),
        )
        return jnp.where(lane > i, joined * root, jnp.where(lane == i, joined, 0.0)).astype(
            jnp.bfloat16
        )

    def finish(rows):
        spread = jnp.dot(w_ref[...], q_cols, preferred_element_type=jnp.float32)
        total = spread[0:64] * rows[0]
        for k in range(1, GROUP):
            total = total + spread[64 * k : 64 * k + 64] * rows[k]
        return total

    out_ref[...] = jnp.zeros_like(out_ref)

    def group(g, carry):
        base = g * GROUP
        for k in range(GROUP):
            i = base + k
            offset = 127 * i - (i * (i - 1)) // 2
            tile = pl.multiple_of((offset // 128) * 128, 128)
            w_ref[64 * k : 64 * k + 64, :] = piece(
                m_ref[:, pl.ds(tile, 128)],
                m_ref[:, pl.ds(pl.multiple_of(tile + 128, 128), 128)],
                offset - tile,
                i,
            )
        out_ref[...] += finish([q_ref[pl.ds(base + k, 1), :] for k in range(GROUP)])
        return carry

    lax.fori_loop(0, LOOPED // GROUP, group, 0)
    for base in range(LOOPED, HD, GROUP):
        for k in range(GROUP):
            i = base + k
            offset = 127 * i - (i * (i - 1)) // 2
            tile = (offset // 128) * 128
            if tile < TAIL_AT:
                first, second = m_ref[:, tile : tile + 128], m_ref[:, tile + 128 : tile + 256]
            else:
                first, second = tail_ref[:, :128], tail_ref[:, 128:]
            w_ref[64 * k : 64 * k + 64, :] = piece(first, second, offset - tile, i)
        out_ref[...] += finish([q_ref[base + k : base + k + 1, :] for k in range(GROUP)])


def carried_part(state_cols, q_own, q_other):
    return pl.pallas_call(
        carried_kernel,
        out_shape=jax.ShapeDtypeStruct((64, SHARD), jnp.float32),
        in_specs=[pl.BlockSpec(memory_space=pltpu.VMEM)] * 3,
        out_specs=pl.BlockSpec(memory_space=pltpu.VMEM),
        scratch_shapes=[
            pltpu.VMEM((HD, SHARD), jnp.float32),
            pltpu.VMEM((64 * GROUP, HD), jnp.bfloat16),
            pltpu.VMEM((64, 256), jnp.float32),
        ],
        compiler_params=pltpu.CompilerParams(vmem_limit_bytes=32 * 1024 * 1024),
        cost_estimate=pl.CostEstimate(
            flops=8192 * 512 * 128 * 4, bytes_accessed=64 * STATE * 4, transcendentals=0
        ),
        name="carried",
    )(state_cols, q_own, q_other)


def window_kernel(core_ref, q_own_ref, q_other_ref, kv0, kv1, kv2, kv3, carried_ref, mine_ref, send_ref):
    core = core_ref[0]
    q_cols = jnp.concatenate([q_own_ref[...], q_other_ref[...]], axis=1)
    key = lax.broadcasted_iota(jnp.int32, (HALF, SHARD), 0)
    query = lax.broadcasted_iota(jnp.int32, (HALF, SHARD), 1)
    key_place = (key // 16) * 32 + key % 16 + core * 16
    inside = query % HALF
    query_place = (inside // 16) * 32 + inside % 16 + jnp.where(query < HALF, core, 1 - core) * 16
    allowed = key_place <= query_place
    total = jnp.zeros((HD, SHARD), jnp.float32)
    for number, kv in enumerate((kv0, kv1, kv2, kv3)):
        scores = lax.dot_general(
            kv[:HD, :], q_cols, (((0,), (0,)), ((), ())), preferred_element_type=jnp.float32
        )
        weights = scores * scores
        if number == 0:
            weights = jnp.where(allowed, weights, 0.0)
        total = total + jnp.dot(
            kv[HD:, :], weights.astype(jnp.bfloat16), preferred_element_type=jnp.float32
        )
    upper = total[:64] + carried_ref[...]
    lower = total[64:]
    mine_ref[...] = jnp.concatenate([upper[:, :HALF], lower[:, :HALF]], axis=0).T
    send_ref[...] = jnp.concatenate([lower[:, HALF:], upper[:, HALF:]], axis=0).T.astype(jnp.bfloat16)


def window_part(core, q_own, q_other, kvs, carried):
    return pl.pallas_call(
        window_kernel,
        out_shape=(
            jax.ShapeDtypeStruct((HALF, HD), jnp.float32),
            jax.ShapeDtypeStruct((HALF, HD), jnp.bfloat16),
        ),
        in_specs=[pl.BlockSpec(memory_space=pltpu.SMEM)]
        + [pl.BlockSpec(memory_space=pltpu.VMEM)] * 7,
        out_specs=(pl.BlockSpec(memory_space=pltpu.VMEM),) * 2,
        compiler_params=pltpu.CompilerParams(vmem_limit_bytes=32 * 1024 * 1024),
        name="window",
    )(core, q_own, q_other, *kvs, carried)


def body(
    tokens,
    attention_gain,
    head_weights,
    carried_state,
    output_weight,
    expert_gain,
    router_weight,
    expert_index,
    expert_first,
    expert_second,
):
    z, y, c = (lax.axis_index(name) for name in ("z", "y", "c"))
    own_weights = head_weights.transpose(0, 2, 1)
    other_weights = swap_core(own_weights)
    output_own = lax.all_gather(output_weight, "y")
    output_other = swap_core(output_own)

    half_tokens = lax.dynamic_index_in_dim(
        tokens.reshape(16, 2, 16, D), c, axis=1, keepdims=False
    ).reshape(HALF, D)
    normed = norm_scaled(half_tokens.astype(jnp.float32), attention_gain).astype(jnp.bfloat16)

    def project(weights):
        return jnp.einsum("afd,td->aft", weights, normed, preferred_element_type=jnp.float32).astype(
            jnp.bfloat16
        )

    own, other = project(own_weights), project(other_weights)
    lower = jnp.where(c == 0, own[:2], other[:2])
    upper = jnp.where(c == 0, other[:2], own[:2])
    q_own = jnp.concatenate([lower[0], upper[0]])
    kv = jnp.concatenate([lower[1], upper[1], own[2], other[2]])
    q_other = swap_core(q_own)
    kvs = [kv] + [
        lax.ppermute(kv, "x", [(i, i + step) for i in range(4 - step)]) for step in (1, 2, 3)
    ]
    carried = carried_part(carried_state.T, q_own, q_other)
    mine, send = window_part(c.reshape(1), q_own, q_other, kvs, carried)
    raw = (mine + swap_core(send).astype(jnp.float32)) / HD
    attended = norm_scaled(raw, 1.0).astype(jnp.bfloat16)

    by_y = attended.reshape(4, 4, SLAB, HD).transpose(1, 0, 2, 3).reshape(4, 64, HD)

    def block(array, at):
        return lax.dynamic_index_in_dim(array, at % 4, axis=0, keepdims=False)

    pieces = [block(by_y, y)] + [shift(block(by_y, y + step), "y", step) for step in (1, 2, 3)]
    partial = jnp.zeros((64, D), jnp.float32)
    for step in range(4):
        for columns, weights in ((slice(0, 64), output_own), (slice(64, 128), output_other)):
            partial = partial + jnp.dot(
                pieces[step][:, columns],
                block(weights, y - step + 4),
                preferred_element_type=jnp.float32,
            )
    by_z = partial.reshape(4, SLAB, D)
    attention_sum = block(by_z, z)
    by_z = by_z.astype(jnp.bfloat16)
    for step in (1, 2, 3):
        attention_sum = attention_sum + shift(block(by_z, z + step), "z", step).astype(jnp.float32)
    slab = lax.dynamic_slice_in_dim(tokens, ((z * 4 + y) * 2 + c) * SLAB, SLAB, 0)
    residual = slab.astype(jnp.float32) + attention_sum
    expert_input = norm_scaled(residual, expert_gain).astype(jnp.bfloat16)
    logits = jnp.dot(expert_input, router_weight, preferred_element_type=jnp.float32)
    matches = expert_index[:, :, None] == jnp.arange(EXPERTS, dtype=jnp.int32)
    gate_values = jax.nn.sigmoid(jnp.sum(jnp.where(matches, logits[:, None, :], 0.0), axis=2))
    flat_matches = matches.reshape(SLAB * TOP, EXPERTS).astype(jnp.int32)
    earlier = jnp.cumsum(flat_matches, axis=0) - flat_matches
    slots = jnp.sum(earlier * flat_matches, axis=1).reshape(SLAB, TOP)
    cells = EXPERTS * CAP
    hits = (expert_index * CAP + slots)[:, :, None] == jnp.arange(cells, dtype=jnp.int32)
    send_map = jnp.sum(hits.astype(jnp.bfloat16), axis=1)
    combine_map = jnp.sum(jnp.where(hits, gate_values[:, :, None], 0.0), axis=1)
    outgoing = (
        lax.dot_general(
            send_map, expert_input, (((0,), (0,)), ((), ())), preferred_element_type=jnp.float32
        )
        .astype(jnp.bfloat16)
        .reshape(EXPERTS, CAP, D)
    )
    arrived = lax.all_to_all(outgoing, CHIP_AXES, split_axis=0, concat_axis=0, tiled=True).reshape(cells, D)
    arrived_other = swap_core(arrived)

    def expert(rows):
        gate = jnp.dot(rows, expert_first[0], preferred_element_type=jnp.float32)
        up = jnp.dot(rows, expert_first[1], preferred_element_type=jnp.float32)
        hidden = (jax.nn.silu(gate) * up).astype(jnp.bfloat16)
        return jnp.dot(hidden, expert_second, preferred_element_type=jnp.float32)

    back = swap_core(expert(arrived_other).astype(jnp.bfloat16))
    produced = (expert(arrived) + back.astype(jnp.float32)).astype(jnp.bfloat16)
    returned = lax.all_to_all(
        produced.reshape(EXPERTS, CAP, D), CHIP_AXES, split_axis=0, concat_axis=0, tiled=True
    ).reshape(cells, D)
    expert_sum = jnp.dot(
        combine_map.astype(jnp.bfloat16), returned, preferred_element_type=jnp.float32
    )
    return (residual + expert_sum).astype(jnp.bfloat16)


def solution(mesh):
    fine = Mesh(mesh.devices.reshape(4, 4, 4, 2), ("x", "z", "y", "c"))
    head = ("z", "y", "c")
    every = ("x", "z", "y", "c")
    in_specs = (
        P("x", None),
        P(),
        P(None, None, head),
        P(None, head),
        P(head, None),
        P(),
        P(),
        P(every, None),
        P(None, None, every),
        P(every, None),
    )
    return jax.shard_map(body, mesh=fine, in_specs=in_specs, out_specs=P(every, None), check_vma=False)
```

time: 438 us -> 143 us (0.33)
  local copies, waits for them, and re-layouts: 134 us -> 10.9 us
  waiting for transfers between devices: 143 us -> 27.4 us
  other arithmetic: 55.6 us -> 7.25 us
  matrix products: 44.7 us -> 24.2 us
  starting transfers between devices: 6.65 us -> 26.3 us
  blocking collectives: 38.1 us -> 24.7 us
  Pallas kernels: 0 us -> 7.44 us
    gather x3 -> x0, local copies, waits for them, and re-layouts: 84.1 us -> none  [the longest x2 64.5 us: apply_state(): jnp.take(memory, jnp.asarray(lookup), axis=0) * jnp.asarray(spread)[:, None]]
    reduce_scatter x1 -> x0, waiting for transfers between devices: 74.3 us -> none  [body(): lax.psum_scatter(jnp.dot(attended, output_weight, preferred_element_type=...]
    all_gather x1, waiting for transfers between devices: 37.2 us -> 1.36 us  [body(): output_own = lax.all_gather(output_weight, 'y')]
    ppermute x2 -> x15, starting transfers between devices: 0.39 us -> 21.4 us  [the longest x6 11.4 us: shift(): return lax.ppermute(array, axis, [(i, (i + step) % 4) for i in range(4)])]
    dot_general x8 -> x15, matrix products: 41.2 us -> 21.7 us  [the longest x2 7.76 us: expert(): return jnp.dot(hidden, expert_second, preferred_element_type=jnp.float32)]
    select_n x5 -> x1, other arithmetic: 16.7 us -> 0.02 us  [body(): lower = jnp.where(c == 0, own[:2], other[:2])]
    dynamic_slice x8 -> x0, local copies, waits for them, and re-layouts: 14.8 us -> none  [hop(): new = combine(before, everything[k].astype(array.dtype))]
    all_to_all x1, blocking collectives: 38.1 us -> 24.7 us  [body(): lax.all_to_all(outgoing, CHIP_AXES, split_axis=0, concat_axis=0, tiled=True)]
  transfers between devices with their start and end apart: 5 -> 17, of which waited for: 5 -> 8; matrix products, arithmetic and copies ran while one was open for 5% -> 11% of each run, Pallas kernels for 0% -> 5%
where the time goes in v1:
time: 143 us; the launch traced here: 142 us
  waiting for transfers between devices  27.4 us (19%)
  starting transfers between devices  26.3 us (18%)
  blocking collectives  24.7 us (17%)
  matrix products  24.2 us (17%)
  between operations  14 us (10%)
  local copies, waits for them, and re-layouts  10.9 us (8%)
  Pallas kernels  7.44 us (5%)
  other arithmetic  7.25 us (5%)
    all_to_all x1, blocking collectives, body(): lax.all_to_all(outgoing, CHIP_AXES, split_axis=0, concat_axis=0, tiled=True)  24.7 us
    all_to_all x1, waiting for transfers between devices, body(): lax.all_to_all(produced.reshape(EXPERTS, CAP, D), CHIP_AXES, split_axis=0...  17.6 us
    ppermute x6, starting transfers between devices, shift(): return lax.ppermute(array, axis, [(i, (i + step) % 4) for i in range(4)])  11.4 us
    ppermute x3, starting transfers between devices, body(): lax.ppermute(kv, 'x', [(i, i + step) for i in range(4 - step)])  9.42 us
    dot_general x2, matrix products, expert(): return jnp.dot(hidden, expert_second, preferred_element_type=jnp.float32)  7.76 us
    pallas_call x1, Pallas kernels, carried_part(): pl.pallas_call(carried_kernel, out_shape=jax.ShapeDtypeStruct((64, SHARD)...  6.35 us
    all_to_all x1, starting transfers between devices, body(): lax.all_to_all(produced.reshape(EXPERTS, CAP, D), CHIP_AXES, split_axis=0...  4.9 us
    ppermute x6, waiting for transfers between devices, shift(): return lax.ppermute(array, axis, [(i, (i + step) % 4) for i in range(4)])  4.36 us
  transfers between devices with their start and end apart: 17, of which 8 were waited for; matrix products, arithmetic and copies ran while one was open for 11% of the time, Pallas kernels for 5%

profile of v1, /device:TPU:0, one launch (start us, length us, event | category | flops | bytes accessed | tf_op | source)
XLA Modules:
  0.0 142.2 jit_solution(18161855394439093732)
XLA Ops:
  6.5 0.7 all-gather.3.cloned.1.call-update
  7.3 3.0 %dynamic-slice_convert_fusion = f32[16,1,16,2048]{3,2,1,0:T(8,128)} fusion(bf16[16,2,16,2048]{3,2,1,0:T(8,128)(2,1)} %bitcast.122, s32[]{:T(128)S(6)} %select_n.120), kind=kLoop, calls=%fused_computation.37 | loop fusion | flops 524288 | bytes 3145732 | tf_op jit(solution)/shard_map/convert_element_type | solution.py:178
  10.3 0.3 multiply_reduce_fusion
  10.5 0.1 rsqrt.28
  10.6 0.1 copy.19
  10.7 0.1 eq.57
  10.8 0.1 fusion.73
  10.9 0.2 reduce_window_sum.11
  11.1 0.2 select_reduce_fusion.2
  11.3 0.1 reshape.88
  11.3 1.8 %fusion.15 = bf16[256,2048]{1,0:T(8,128)(2,1)S(1)} fusion(f32[16,1,16,2048]{3,2,1,0:T(8,128)} %dynamic-slice_convert_fusion, f32[2048]{0:T(1024)S(1)} %copy-done.5, f32[256]{0:T(256)S(1)} %rsqrt.28), kind=kLoop, calls=%fused_computation.21 | loop fusion | flops 1572864 | bytes 3154944 | tf_op jit(solution)/shard_map/convert_element_type | solution.py:178
  13.2 0.5 fusion.31
  13.7 1.8 %fusion.32 = bf16[3,64,256]{2,1,0:T(8,128)(2,1)S(1)} fusion(bf16[3,64,2048]{2,1,0:T(8,128)(2,1)} %collective-permute-done, bf16[256,2048]{1,0:T(8,128)(2,1)S(1)} %fusion.15), kind=kOutput, calls=%fused_computation.34 | convolution fusion | flops 201375744 | bytes 1933312 | tf_op jit(solution)/shard_map/afd,td->aft/dot_general | solution.py:181
  15.6 0.1 collective-permute-start.1
  15.7 3.5 %collective-permute-start.2 = (bf16[256,256]{1,0:T(8,128)(2,1)S(1)}, bf16[256,256]{1,0:T(8,128)(2,1)S(1)}, u32[]{:S(2)}, u32[]{:S(2)}) collective-permute-start(bf16[256,256]{1,0:T(8,128)(2,1)S(1)} %pad_maximum_fusion.kv0), channel_id=1, source_target_pairs={{0,32},{32,64},{64,96},{1,33},{33,65},{65,97},{2,34},{34,66},{66,9... | collective-permute-start | bytes 393224 | tf_op jit(solution)/shard_map/ppermute | solution.py:192
  19.2 4.6 %collective-permute-start.3 = (bf16[256,256]{1,0:T(8,128)(2,1)S(1)}, bf16[256,256]{1,0:T(8,128)(2,1)S(1)}, u32[]{:S(2)}, u32[]{:S(2)}) collective-permute-start(bf16[256,256]{1,0:T(8,128)(2,1)S(1)} %pad_maximum_fusion.kv0), channel_id=1, source_target_pairs={{0,64},{32,96},{1,65},{33,97},{2,66},{34,98},{3,67},{35,99},{4,68}... | collective-permute-start | bytes 393224 | tf_op jit(solution)/shard_map/ppermute | solution.py:192
  23.9 1.3 collective-permute-start.4
  25.2 6.4 %carried.1.carried_ref = f32[64,512]{1,0:T(8,128)S(1)} custom-call(f32[64,8256]{1,0:T(8,128)S(1)} %bitcast.120, bf16[128,256]{1,0:T(8,128)(2,1)S(1)} %pad_maximum_fusion.1.q_own_ref, bf16[128,256]{1,0:T(8,128)(2,1)S(1)} %collective-permute-done.1.q_other_ref), custom_call_target="tpu_custom_call" | custom-call | flops 2147483648 | bytes 2113536 | tf_op jit(solution)/shard_map/carried/pallas_call | solution.py:98
  31.6 1.1 window.1
  32.7 0.1 collective-permute-start.5
  32.9 1.1 collective-permute-done.5
  34.0 0.1 multiply_reduce_fusion.2
  34.1 1.4 all-gather.3.cloned.1.call-done
  35.5 0.1 multiply_convert_fusion.3
  35.7 0.6 collective-permute-start.7
  36.3 2.8 %collective-permute-start.8 = (bf16[64,128]{1,0:T(8,128)(2,1)S(1)}, bf16[64,128]{1,0:T(8,128)(2,1)S(1)}, u32[]{:S(2)}, u32[]{:S(2)}) collective-permute-start(bf16[64,128]{1,0:T(8,128)(2,1)S(1)} %get-tuple-element.18), channel_id=1, source_target_pairs={{0,4},{2,6},{4,0},{6,2},{1,5},{3,7},{5,1},{7,3},{8,12},{10,14},{12... | collective-permute-start | bytes 49160 | tf_op jit(solution)/shard_map/ppermute | solution.py:29
  39.1 1.3 collective-permute-start.9
  40.5 1.2 fusion.52
  41.6 1.2 collective-permute-done.9
  42.9 1.2 fusion.42
  44.0 0.2 fusion.46
  44.3 0.3 fusion.44
  44.5 0.3 convolution_add_fusion.1
  44.8 0.3 fusion.40
  45.1 0.3 fusion.48
  45.4 0.3 fusion.4
  45.7 2.0 %collective-permute-start.10 = (bf16[16,2048]{1,0:T(8,128)(2,1)S(1)}, bf16[16,2048]{1,0:T(8,128)(2,1)S(1)}, u32[]{:S(2)}, u32[]{:S(2)}) collective-permute-start(bf16[16,2048]{1,0:T(8,128)(2,1)S(1)} %get-tuple-element.11), channel_id=1, source_target_pairs={{0,8},{8,16},{16,24},{24,0},{1,9},{9,17},{17,25},{25,1},{2,10},{10... | collective-permute-start | bytes 196616 | tf_op jit(solution)/shard_map/ppermute | solution.py:29
  47.7 3.6 %collective-permute-start.11 = (bf16[16,2048]{1,0:T(8,128)(2,1)S(1)}, bf16[16,2048]{1,0:T(8,128)(2,1)S(1)}, u32[]{:S(2)}, u32[]{:S(2)}) collective-permute-start(bf16[16,2048]{1,0:T(8,128)(2,1)S(1)} %get-tuple-element.13), channel_id=1, source_target_pairs={{0,16},{8,24},{16,0},{24,8},{1,17},{9,25},{17,1},{25,9},{2,18},{10... | collective-permute-start | bytes 196616 | tf_op jit(solution)/shard_map/ppermute | solution.py:29
  51.3 1.0 collective-permute-start.12
  52.3 0.1 fusion.72
  52.4 0.3 collective-permute-done.10
  52.7 1.5 %collective-permute-done.11 = bf16[16,2048]{1,0:T(8,128)(2,1)S(1)} collective-permute-done((bf16[16,2048]{1,0:T(8,128)(2,1)S(1)}, bf16[16,2048]{1,0:T(8,128)(2,1)S(1)}, u32[]{:S(2)}, u32[]{:S(2)}) %collective-permute-start.11) | collective-permute-done | bytes 65568 | tf_op jit(solution)/shard_map/ppermute | solution.py:29
  54.2 1.3 collective-permute-done.12
  55.6 1.0 multiply_reduce_fusion.1
  56.6 1.3 convolution_convert_fusion.1
  57.9 2.4 %reshape.89 = bf16[64,3,2048]{2,1,0:T(4,128)(2,1)S(1)} reshape(bf16[192,2048]{1,0:T(8,128)(2,1)} %convolution_convert_fusion.1) | data formatting | bytes 1572864 | tf_op jit(solution)/shard_map/reshape | solution.py:236
  60.3 24.7 %all_to_all.10 = bf16[64,3,2048]{2,1,0:T(4,128)(2,1)} all-to-all(bf16[64,3,2048]{2,1,0:T(4,128)(2,1)S(1)} %reshape.89), channel_id=1, replica_groups=mesh['x'=4,'z'=4,'y'=4,'c'=2] {'x','z','y'}, dimensions={0} | all-to-all | bytes 1572864 | tf_op jit(solution)/shard_map/all_to_all | solution.py:238
  85.1 2.4 %reshape.90 = bf16[192,2048]{1,0:T(8,128)(2,1)S(1)} reshape(bf16[64,3,2048]{2,1,0:T(4,128)(2,1)} %all_to_all.10) | data formatting | bytes 1572864 | tf_op jit(solution)/shard_map/reshape | solution.py:238
  87.5 0.3 collective-permute-start.13
  87.8 2.3 %collective-permute-done.13 = bf16[192,2048]{1,0:T(8,128)(2,1)S(1)} collective-permute-done((bf16[192,2048]{1,0:T(8,128)(2,1)S(1)}, bf16[192,2048]{1,0:T(8,128)(2,1)S(1)}, u32[]{:S(2)}, u32[]{:S(2)}) %collective-permute-start.13) | collective-permute-done | bytes 786464 | tf_op jit(solution)/shard_map/ppermute | solution.py:25
  90.0 0.9 copy-done.8
  90.9 2.9 %fusion.6 = f32[192,512]{1,0:T(8,128)} fusion(bf16[192,2048]{1,0:T(8,128)(2,1)S(1)} %collective-permute-done.13, bf16[2,2048,512]{2,1,0:T(8,128)(2,1)} %param.18), kind=kOutput, calls=%fused_computation.11 | convolution fusion | flops 402653184 | bytes 3276800 | tf_op jit(solution)/shard_map/dot_general | solution.py:243
  93.9 3.9 %convolution_convert_fusion = bf16[192,2048]{1,0:T(8,128)(2,1)} fusion(bf16[512,2048]{1,0:T(8,128)(2,1)S(1)} %copy-done, f32[192,512]{1,0:T(8,128)} %fusion.6, bf16[192,2048]{1,0:T(8,128)(2,1)} %copy-done.8, bf16[2,2048,512]{2,1,0:T(8,128)(2,1)} %param.18), kind=kOutput, calls=%fused_computation | convolution fusion | flops 806289408 | bytes 6160384 | tf_op jit(solution)/shard_map/dot_general | solution.py:245
  97.8 0.1 collective-permute-start.14
  97.9 2.9 %fusion.12 = f32[192,512]{1,0:T(8,128)} fusion(bf16[192,2048]{1,0:T(8,128)(2,1)S(1)} %reshape.90, bf16[2,2048,512]{2,1,0:T(8,128)(2,1)} %param.18), kind=kOutput, calls=%fused_computation.17 | convolution fusion | flops 402653184 | bytes 3276800 | tf_op jit(solution)/shard_map/dot_general | solution.py:242
  100.8 3.9 %add_convert_fusion = bf16[192,2048]{1,0:T(8,128)(2,1)} fusion(bf16[192,2048]{1,0:T(8,128)(2,1)} %collective-permute-done.14, bf16[512,2048]{1,0:T(8,128)(2,1)S(1)} %copy-done, bf16[192,2048]{1,0:T(8,128)(2,1)S(1)} %reshape.90, bf16[2,2048,512]{2,1,0:T(8,128)(2,1)} %param.18, f32[192,512]{1,0:T(8,128)} %fusion.12), kind=kOutput, calls=%fused_computation.27 | convolution fusion | flops 807075840 | bytes 6946816 | tf_op jit(solution)/shard_map/dot_general | solution.py:245
  104.7 3.3 %reshape.91 = bf16[64,3,2048]{2,1,0:T(4,128)(2,1)} reshape(bf16[192,2048]{1,0:T(8,128)(2,1)} %add_convert_fusion) | data formatting | bytes 1572864 | tf_op jit(solution)/shard_map/reshape | solution.py:250
  107.9 4.9 %all-to-all-start.1 = ((bf16[64,3,2048]{2,1,0:T(4,128)(2,1)}), bf16[64,3,2048]{2,1,0:T(4,128)(2,1)S(1)}, u32[]{:S(2)}, u32[]{:S(2)}) async-start(bf16[64,3,2048]{2,1,0:T(4,128)(2,1)} %reshape.91), calls=%async_computation.1 | async-start | bytes 2097152 | tf_op jit(solution)/shard_map/all_to_all | solution.py:249
  112.9 1.2 fusion.94
  114.0 0.2 select_reduce_fusion.1
  114.2 0.1 select_reduce_fusion
  114.4 17.6 %all-to-all-done.1 = bf16[64,3,2048]{2,1,0:T(4,128)(2,1)S(1)} async-done(((bf16[64,3,2048]{2,1,0:T(4,128)(2,1)}), bf16[64,3,2048]{2,1,0:T(4,128)(2,1)S(1)}, u32[]{:S(2)}, u32[]{:S(2)}) %all-to-all-start.1) | async-done | bytes 786464 | tf_op jit(solution)/shard_map/all_to_all | solution.py:249
  132.0 1.4 reshape.92
  133.4 2.0 %fusion.5 = bf16[16,2048]{1,0:T(8,128)(2,1)} fusion(f32[16,2048]{1,0:T(8,128)S(1)} %get-tuple-element.10, bf16[192,2048]{1,0:T(8,128)(2,1)} %reshape.92, bf16[16,192]{1,0:T(8,128)(2,1)S(1)} %select_reduce_fusion), kind=kOutput, calls=%fused_computation.10 | convolution fusion | flops 12648448 | bytes 989184 | tf_op jit(solution)/shard_map/dot_general | solution.py:252
  (44 shorter events, 0.2 us)
Async XLA Ops:
  6.5 87.3 %copy-start = (bf16[512,2048]{1,0:T(8,128)(2,1)S(1)}, bf16[512,2048]{1,0:T(8,128)(2,1)}, u32[]{:S(2)}) copy-start(bf16[512,2048]{1,0:T(8,128)(2,1)} %param.19) | copy-start | bytes 6291460
  6.5 29.0 %all-gather.3.cloned.1.call-start = ((), (), s32[]{:S(2)}) async-start(), calls=%async_computation.2 | async-start | bytes 1310720 | tf_op jit(solution)/shard_map/all_gather | solution.py:172
  6.5 7.2 %collective-permute-start = (bf16[3,64,2048]{2,1,0:T(8,128)(2,1)}, bf16[3,64,2048]{2,1,0:T(8,128)(2,1)}, u32[]{:S(2)}, u32[]{:S(2)}) collective-permute-start(bf16[3,64,2048]{2,1,0:T(8,128)(2,1)} %bitcast.131), channel_id=1, source_target_pairs={{0,1},{1,0},{2,3},{3,2},{4,5},{5,4},{6,7},{7,6},{8,9},{9,8},{10,11... | collective-permute-start | bytes 2359304 | tf_op jit(solution)/shard_map/ppermute | solution.py:25
  7.3 3.0 %copy-start.2 = (bf16[512,2048]{1,0:T(8,128)(2,1)S(1)}, bf16[512,2048]{1,0:T(8,128)(2,1)}, u32[]{:S(2)}) copy-start(bf16[512,2048]{1,0:T(8,128)(2,1)} %param.10) | copy-start | bytes 6291460
  7.3 3.3 %copy-start.6 = (s32[16,8]{0,1:T(8,128)S(1)}, s32[16,8]{0,1:T(8,128)}, u32[]{:S(2)}) copy-start(s32[16,8]{0,1:T(8,128)} %param.17) | copy-start | bytes 1540
  7.3 4.1 %copy-start.5 = (f32[2048]{0:T(1024)S(1)}, f32[2048]{0:T(1024)}, u32[]{:S(2)}) copy-start(f32[2048]{0:T(1024)} %param.11) | copy-start | bytes 24580
  10.3 2.9 %copy-start.7 = (bf16[3,2048,64]{1,2,0:T(8,128)(2,1)S(1)}, bf16[3,2048,64]{1,2,0:T(8,128)(2,1)}, u32[]{:S(2)}) copy-start(bf16[3,2048,64]{1,2,0:T(8,128)(2,1)} %param.12) | copy-start | bytes 2359300
  13.7 11.5 %copy-start.1 = (f32[8256,64]{0,1:T(8,128)S(1)}, f32[8256,64]{0,1:T(8,128)}, u32[]{:S(2)}) copy-start(f32[8256,64]{0,1:T(8,128)} %param.13) | copy-start | bytes 6340612
  15.6 9.6 %collective-permute-start.1 = (bf16[128,256]{1,0:T(8,128)(2,1)S(1)}, bf16[128,256]{1,0:T(8,128)(2,1)S(1)}, u32[]{:S(2)}, u32[]{:S(2)}) collective-permute-start(bf16[128,256]{1,0:T(8,128)(2,1)S(1)} %pad_maximum_fusion.1.q_own_ref), channel_id=1, source_target_pairs={{0,1},{1,0},{2,3},{3,2},{4,5},{5,4},{6,7},{7,6},{8,9},{9,8},{10,11... | collective-permute-start | bytes 196616 | tf_op jit(solution)/shard_map/ppermute | solution.py:25
  15.7 15.8 %collective-permute-start.2 = (bf16[256,256]{1,0:T(8,128)(2,1)S(1)}, bf16[256,256]{1,0:T(8,128)(2,1)S(1)}, u32[]{:S(2)}, u32[]{:S(2)}) collective-permute-start(bf16[256,256]{1,0:T(8,128)(2,1)S(1)} %pad_maximum_fusion.kv0), channel_id=1, source_target_pairs={{0,32},{32,64},{64,96},{1,33},{33,65},{65,97},{2,34},{34,66},{66,9... | collective-permute-start | bytes 393224 | tf_op jit(solution)/shard_map/ppermute | solution.py:192
  19.2 12.3 %collective-permute-start.3 = (bf16[256,256]{1,0:T(8,128)(2,1)S(1)}, bf16[256,256]{1,0:T(8,128)(2,1)S(1)}, u32[]{:S(2)}, u32[]{:S(2)}) collective-permute-start(bf16[256,256]{1,0:T(8,128)(2,1)S(1)} %pad_maximum_fusion.kv0), channel_id=1, source_target_pairs={{0,64},{32,96},{1,65},{33,97},{2,66},{34,98},{3,67},{35,99},{4,68}... | collective-permute-start | bytes 393224 | tf_op jit(solution)/shard_map/ppermute | solution.py:192
  23.9 7.7 %collective-permute-start.4 = (bf16[256,256]{1,0:T(8,128)(2,1)S(1)}, bf16[256,256]{1,0:T(8,128)(2,1)S(1)}, u32[]{:S(2)}, u32[]{:S(2)}) collective-permute-start(bf16[256,256]{1,0:T(8,128)(2,1)S(1)} %pad_maximum_fusion.kv0), channel_id=1, source_target_pairs={{0,96},{1,97},{2,98},{3,99},{4,100},{5,101},{6,102},{7,103},{8,104... | collective-permute-start | bytes 393224 | tf_op jit(solution)/shard_map/ppermute | solution.py:192
  32.7 1.3 collective-permute-start.5
  35.5 8.5 %copy-start.3 = (bf16[256,2048]{1,0:T(8,128)(2,1)S(1)}, bf16[256,2048]{1,0:T(8,128)(2,1)}, u32[]{:S(2)}) copy-start(bf16[256,2048]{1,0:T(8,128)(2,1)} %all-gather.3.cloned.1.call-done) | copy-start | bytes 3145732
  35.5 8.7 %collective-permute-start.6 = (bf16[4,64,2048]{2,1,0:T(8,128)(2,1)}, bf16[4,64,2048]{2,1,0:T(8,128)(2,1)S(1)}, u32[]{:S(2)}, u32[]{:S(2)}) collective-permute-start(bf16[4,64,2048]{2,1,0:T(8,128)(2,1)} %bitcast.124), channel_id=1, source_target_pairs={{0,1},{1,0},{2,3},{3,2},{4,5},{5,4},{6,7},{7,6},{8,9},{9,8},{10,11... | collective-permute-start | bytes 3145736 | tf_op jit(solution)/shard_map/ppermute | solution.py:25
  35.7 9.4 %collective-permute-start.7 = (bf16[64,128]{1,0:T(8,128)(2,1)S(1)}, bf16[64,128]{1,0:T(8,128)(2,1)S(1)}, u32[]{:S(2)}, u32[]{:S(2)}) collective-permute-start(bf16[64,128]{1,0:T(8,128)(2,1)S(1)} %get-tuple-element.19), channel_id=1, source_target_pairs={{0,2},{2,4},{4,6},{6,0},{1,3},{3,5},{5,7},{7,1},{8,10},{10,12},{12... | collective-permute-start | bytes 49160 | tf_op jit(solution)/shard_map/ppermute | solution.py:29
  36.3 7.7 %collective-permute-start.8 = (bf16[64,128]{1,0:T(8,128)(2,1)S(1)}, bf16[64,128]{1,0:T(8,128)(2,1)S(1)}, u32[]{:S(2)}, u32[]{:S(2)}) collective-permute-start(bf16[64,128]{1,0:T(8,128)(2,1)S(1)} %get-tuple-element.18), channel_id=1, source_target_pairs={{0,4},{2,6},{4,0},{6,2},{1,5},{3,7},{5,1},{7,3},{8,12},{10,14},{12... | collective-permute-start | bytes 49160 | tf_op jit(solution)/shard_map/ppermute | solution.py:29
  39.1 3.7 %collective-permute-start.9 = (bf16[64,128]{1,0:T(8,128)(2,1)S(1)}, bf16[64,128]{1,0:T(8,128)(2,1)S(1)}, u32[]{:S(2)}, u32[]{:S(2)}) collective-permute-start(bf16[64,128]{1,0:T(8,128)(2,1)S(1)} %get-tuple-element.17), channel_id=1, source_target_pairs={{0,6},{2,0},{4,2},{6,4},{1,7},{3,1},{5,3},{7,5},{8,14},{10,8},{12,... | collective-permute-start | bytes 49160 | tf_op jit(solution)/shard_map/ppermute | solution.py:29
  45.4 11.2 %copy-start.4 = (f32[2048]{0:T(1024)S(1)}, f32[2048]{0:T(1024)}, u32[]{:S(2)}) copy-start(f32[2048]{0:T(1024)} %param.15) | copy-start | bytes 24580
  45.7 7.0 %collective-permute-start.10 = (bf16[16,2048]{1,0:T(8,128)(2,1)S(1)}, bf16[16,2048]{1,0:T(8,128)(2,1)S(1)}, u32[]{:S(2)}, u32[]{:S(2)}) collective-permute-start(bf16[16,2048]{1,0:T(8,128)(2,1)S(1)} %get-tuple-element.11), channel_id=1, source_target_pairs={{0,8},{8,16},{16,24},{24,0},{1,9},{9,17},{17,25},{25,1},{2,10},{10... | collective-permute-start | bytes 196616 | tf_op jit(solution)/shard_map/ppermute | solution.py:29
  47.7 6.5 %collective-permute-start.11 = (bf16[16,2048]{1,0:T(8,128)(2,1)S(1)}, bf16[16,2048]{1,0:T(8,128)(2,1)S(1)}, u32[]{:S(2)}, u32[]{:S(2)}) collective-permute-start(bf16[16,2048]{1,0:T(8,128)(2,1)S(1)} %get-tuple-element.13), channel_id=1, source_target_pairs={{0,16},{8,24},{16,0},{24,8},{1,17},{9,25},{17,1},{25,9},{2,18},{10... | collective-permute-start | bytes 196616 | tf_op jit(solution)/shard_map/ppermute | solution.py:29
  51.3 4.3 %collective-permute-start.12 = (bf16[16,2048]{1,0:T(8,128)(2,1)S(1)}, bf16[16,2048]{1,0:T(8,128)(2,1)S(1)}, u32[]{:S(2)}, u32[]{:S(2)}) collective-permute-start(bf16[16,2048]{1,0:T(8,128)(2,1)S(1)} %get-tuple-element.12), channel_id=1, source_target_pairs={{0,24},{8,0},{16,8},{24,16},{1,25},{9,1},{17,9},{25,17},{2,26},{10... | collective-permute-start | bytes 196616 | tf_op jit(solution)/shard_map/ppermute | solution.py:29
  87.5 2.5 %collective-permute-start.13 = (bf16[192,2048]{1,0:T(8,128)(2,1)S(1)}, bf16[192,2048]{1,0:T(8,128)(2,1)S(1)}, u32[]{:S(2)}, u32[]{:S(2)}) collective-permute-start(bf16[192,2048]{1,0:T(8,128)(2,1)S(1)} %reshape.90), channel_id=1, source_target_pairs={{0,1},{1,0},{2,3},{3,2},{4,5},{5,4},{6,7},{7,6},{8,9},{9,8},{10,11... | collective-permute-start | bytes 2359304 | tf_op jit(solution)/shard_map/ppermute | solution.py:25
  90.0 0.9 copy-start.8
  97.8 3.0 %collective-permute-start.14 = (bf16[192,2048]{1,0:T(8,128)(2,1)}, bf16[192,2048]{1,0:T(8,128)(2,1)}, u32[]{:S(2)}, u32[]{:S(2)}) collective-permute-start(bf16[192,2048]{1,0:T(8,128)(2,1)} %convolution_convert_fusion), channel_id=1, source_target_pairs={{0,1},{1,0},{2,3},{3,2},{4,5},{5,4},{6,7},{7,6},{8,9},{9,8},{10,11... | collective-permute-start | bytes 2359304 | tf_op jit(solution)/shard_map/ppermute | solution.py:25
  107.9 24.0 %all-to-all-start.1 = ((bf16[64,3,2048]{2,1,0:T(4,128)(2,1)}), bf16[64,3,2048]{2,1,0:T(4,128)(2,1)S(1)}, u32[]{:S(2)}, u32[]{:S(2)}) async-start(bf16[64,3,2048]{2,1,0:T(4,128)(2,1)} %reshape.91), calls=%async_computation.1 | async-start | bytes 2097152 | tf_op jit(solution)/shard_map/all_to_all | solution.py:249
Sparse Core Ops, SparseCore 0:
  9.0 26.4 all-gather.2

commit v2 on v1

--- a/solution.py
+++ b/solution.py
@@ -27,6 +27,18 @@
 
 def shift(array, axis, step):
     return lax.ppermute(array, axis, [(i, (i + step) % 4) for i in range(4)])
+
+
+def scalars(*values):
+    return jnp.stack([jnp.asarray(value, jnp.int32) for value in values])
+
+
+VMEM = pl.BlockSpec(memory_space=pltpu.VMEM)
+SMEM = pl.BlockSpec(memory_space=pltpu.SMEM)
+LIMIT = pltpu.CompilerParams(vmem_limit_bytes=32 * 1024 * 1024)
+ROWS = EXPERTS * CAP
+PIECES = D // 128
+TILE_ROWS = ROWS * PIECES
 
 
 def norm_scaled(values, gain):
@@ -130,6 +142,8 @@
         weights = scores * scores
         if number == 0:
             weights = jnp.where(allowed, weights, 0.0)
+        else:
+            weights = jnp.where(core_ref[1] >= number, weights, 0.0)
         total = total + jnp.dot(
             kv[HD:, :], weights.astype(jnp.bfloat16), preferred_element_type=jnp.float32
         )
@@ -152,6 +166,326 @@
         compiler_params=pltpu.CompilerParams(vmem_limit_bytes=32 * 1024 * 1024),
         name="window",
     )(core, q_own, q_other, *kvs, carried)
+
+
+def norm_kernel(core_ref, tokens_ref, gain_ref, out_ref):
+    floats = tokens_ref[:, 0].astype(jnp.float32).reshape(128, D)
+    out_ref[...] = norm_scaled(floats, gain_ref[...]).astype(jnp.bfloat16)
+
+
+def norm_part(core, tokens, gain):
+    return pl.pallas_call(
+        norm_kernel,
+        grid_spec=pltpu.PrefetchScalarGridSpec(
+            num_scalar_prefetch=1,
+            grid=(2,),
+            in_specs=[
+                pl.BlockSpec((8, 1, 16, D), lambda i, core: (i, core[0], 0, 0)),
+                pl.BlockSpec((1, D), lambda i, core: (0, 0)),
+            ],
+            out_specs=pl.BlockSpec((128, D), lambda i, core: (i, 0)),
+        ),
+        out_shape=jax.ShapeDtypeStruct((HALF, D), jnp.bfloat16),
+        compiler_params=LIMIT,
+        name="norm",
+    )(core, tokens.reshape(16, 2, 16, D), gain.reshape(1, D))
+
+
+def project_kernel(core_ref, normed_ref, own_ref, other_ref, q_ref, kv_ref):
+    core = core_ref[0]
+    normed = normed_ref[...]
+
+    def times(ref):
+        return lax.dot_general(
+            ref[...].reshape(192, D),
+            normed,
+            (((1,), (1,)), ((), ())),
+            preferred_element_type=jnp.float32,
+        ).astype(jnp.bfloat16)
+
+    own, other = times(own_ref), times(other_ref)
+    own_at = pl.multiple_of(core * 64, 64)
+    other_at = pl.multiple_of((1 - core) * 64, 64)
+    q_ref[pl.ds(own_at, 64), :] = own[:64]
+    q_ref[pl.ds(other_at, 64), :] = other[:64]
+    kv_ref[pl.ds(own_at, 64), :] = own[64:128]
+    kv_ref[pl.ds(other_at, 64), :] = other[64:128]
+    kv_ref[128:192, :] = own[128:]
+    kv_ref[192:256, :] = other[128:]
+
+
+def project_part(core, normed, own, other):
+    return pl.pallas_call(
+        project_kernel,
+        out_shape=(
+            jax.ShapeDtypeStruct((HD, HALF), jnp.bfloat16),
+            jax.ShapeDtypeStruct((2 * HD, HALF), jnp.bfloat16),
+        ),
+        in_specs=[SMEM, VMEM, VMEM, VMEM],
+        out_specs=(VMEM, VMEM),
+        compiler_params=LIMIT,
+        name="project",
+    )(core, normed, own, other)
+
+
+def attend_kernel(place_ref, mine_ref, received_ref, *rest):
+    outs, scratch = rest[:4], rest[4]
+    raw = (mine_ref[...] + received_ref[...].astype(jnp.float32)) / HD
+    scratch[...] = norm_scaled(raw, 1.0).reshape(4, 64, HD)
+    for step, out in enumerate(outs):
+        at = pl.multiple_of(lax.rem(place_ref[1] + step, 4) * SLAB, SLAB)
+        out[...] = scratch[:, pl.ds(at, SLAB), :].reshape(64, HD).astype(jnp.bfloat16)
+
+
+def attend_part(place, mine, received):
+    return pl.pallas_call(
+        attend_kernel,
+        out_shape=(jax.ShapeDtypeStruct((64, HD), jnp.bfloat16),) * 4,
+        in_specs=[SMEM, VMEM, VMEM],
+        out_specs=(VMEM,) * 4,
+        scratch_shapes=[pltpu.VMEM((4, 64, HD), jnp.float32)],
+        compiler_params=LIMIT,
+        name="attend",
+    )(place, mine, received)
+
+
+def output_kernel(place_ref, *rest):
+    pieces, own, other, outs, scratch = rest[:4], rest[4:8], rest[8:12], rest[12:16], rest[16]
+    loaded = [piece[...] for piece in pieces]
+    for at in range(0, D, 512):
+        total = jnp.zeros((64, 512), jnp.float32)
+        for step in range(4):
+            total = total + jnp.dot(
+                loaded[step][:, :64],
+                own[step][:, at : at + 512],
+                preferred_element_type=jnp.float32,
+            )
+            total = total + jnp.dot(
+                loaded[step][:, 64:],
+                other[step][:, at : at + 512],
+                preferred_element_type=jnp.float32,
+            )
+        scratch[:, at : at + 512] = total
+    for step, out in enumerate(outs):
+        at = pl.multiple_of(lax.rem(place_ref[0] + step, 4) * SLAB, SLAB)
+        out[...] = scratch[pl.ds(at, SLAB), :].astype(out.dtype)
+
+
+def output_part(place, pieces, own, other):
+    return pl.pallas_call(
+        output_kernel,
+        out_shape=(jax.ShapeDtypeStruct((SLAB, D), jnp.float32),)
+        + (jax.ShapeDtypeStruct((SLAB, D), jnp.bfloat16),) * 3,
+        in_specs=[SMEM] + [VMEM] * 12,
+        out_specs=(VMEM,) * 4,
+        scratch_shapes=[pltpu.VMEM((64, D), jnp.float32)],
+        compiler_params=LIMIT,
+        name="output",
+    )(place, *pieces, *own, *other)
+
+
+def map_kernel(index_ref, rows_ref, lanes_ref):
+    index = index_ref[...]
+    expert = lax.broadcasted_iota(jnp.int32, (SLAB, EXPERTS), 1)
+    chosen = jnp.zeros((SLAB, EXPERTS), jnp.float32)
+    for k in range(TOP):
+        chosen = chosen + jnp.where(index[:, k : k + 1] == expert, 1.0, 0.0)
+    before = lax.broadcasted_iota(jnp.int32, (SLAB, SLAB), 0) > lax.broadcasted_iota(
+        jnp.int32, (SLAB, SLAB), 1
+    )
+    slot = jnp.dot(
+        jnp.where(before, 1.0, 0.0).astype(jnp.bfloat16),
+        chosen.astype(jnp.bfloat16),
+        preferred_element_type=jnp.float32,
+    )
+    code = jnp.where(chosen > 0.5, slot, -1.0).astype(jnp.bfloat16)
+    lane = lax.broadcasted_iota(jnp.int32, (SLAB, TILE_ROWS), 1)
+    wide = jnp.dot(code, spread_map(), preferred_element_type=jnp.float32)
+    lanes_ref[...] = jnp.where(
+        wide == ((lane // PIECES) % CAP).astype(jnp.float32), 1.0, 0.0
+    )
+    token = lax.broadcasted_iota(jnp.int32, (SLAB, 256), 0)
+    column = lax.broadcasted_iota(jnp.int32, (SLAB, 256), 1)
+    by_column = lax.dot_general(
+        code,
+        jnp.where(column % SLAB == token, 1.0, 0.0).astype(jnp.bfloat16),
+        (((0,), (0,)), ((), ())),
+        preferred_element_type=jnp.float32,
+    ).astype(jnp.bfloat16)
+    row_expert = lax.broadcasted_iota(jnp.int32, (TILE_ROWS, EXPERTS), 0) // (CAP * PIECES)
+    pick = jnp.where(
+        row_expert == lax.broadcasted_iota(jnp.int32, (TILE_ROWS, EXPERTS), 1), 1.0, 0.0
+    ).astype(jnp.bfloat16)
+    tall = jnp.dot(pick, by_column, preferred_element_type=jnp.float32)
+    row = lax.broadcasted_iota(jnp.int32, (TILE_ROWS, 256), 0)
+    piece = lax.broadcasted_iota(jnp.int32, (TILE_ROWS, 256), 1) // SLAB
+    rows_ref[...] = jnp.where(
+        (tall == ((row // PIECES) % CAP).astype(jnp.float32)) & (row % PIECES == piece), 1.0, 0.0
+    ).astype(jnp.bfloat16)
+
+
+def spread_map():
+    lane_expert = lax.broadcasted_iota(jnp.int32, (EXPERTS, TILE_ROWS), 1) // (CAP * PIECES)
+    return jnp.where(
+        lane_expert == lax.broadcasted_iota(jnp.int32, (EXPERTS, TILE_ROWS), 0), 1.0, 0.0
+    ).astype(jnp.bfloat16)
+
+
+def map_part(index):
+    return pl.pallas_call(
+        map_kernel,
+        out_shape=(
+            jax.ShapeDtypeStruct((TILE_ROWS, 256), jnp.bfloat16),
+            jax.ShapeDtypeStruct((SLAB, TILE_ROWS), jnp.float32),
+        ),
+        in_specs=[VMEM],
+        out_specs=(VMEM, VMEM),
+        compiler_params=LIMIT,
+        name="maps",
+    )(index)
+
+
+def dispatch_kernel(slab_ref, own_ref, r1, r2, r3, gain_ref, router_ref, rows_ref, residual_ref, out_ref, gates_ref):
+    residual = slab_ref[...].astype(jnp.float32) + own_ref[...]
+    for received in (r1, r2, r3):
+        residual = residual + received[...].astype(jnp.float32)
+    residual_ref[...] = residual
+    inputs = norm_scaled(residual, gain_ref[...]).astype(jnp.bfloat16)
+    logits = lax.dot_general(
+        inputs, router_ref[...], (((1,), (1,)), ((), ())), preferred_element_type=jnp.float32
+    )
+    gates_ref[...] = jax.nn.sigmoid(logits)
+    tall = jnp.concatenate([inputs[:, at : at + 128] for at in range(0, D, 128)], axis=0)
+    out_ref[...] = jnp.dot(rows_ref[...], tall, preferred_element_type=jnp.float32).astype(
+        jnp.bfloat16
+    )
+
+
+def dispatch_part(slab, own, received, gain, router, rows):
+    return pl.pallas_call(
+        dispatch_kernel,
+        out_shape=(
+            jax.ShapeDtypeStruct((SLAB, D), jnp.float32),
+            jax.ShapeDtypeStruct((TILE_ROWS, 128), jnp.bfloat16),
+            jax.ShapeDtypeStruct((SLAB, EXPERTS), jnp.float32),
+        ),
+        in_specs=[VMEM] * 8,
+        out_specs=(VMEM,) * 3,
+        compiler_params=LIMIT,
+        name="dispatch",
+    )(slab, own, *received, gain.reshape(1, D), router, rows)
+
+
+def gate_kernel(gates_ref, lanes_ref, out_ref):
+    wide = jnp.dot(
+        gates_ref[...].astype(jnp.bfloat16), spread_map(), preferred_element_type=jnp.float32
+    )
+    wide = wide * lanes_ref[...]
+    piece = lax.broadcasted_iota(jnp.int32, (SLAB, TILE_ROWS), 1) % PIECES
+    for at in range(PIECES):
+        out_ref[at * SLAB : (at + 1) * SLAB, :] = jnp.where(piece == at, wide, 0.0).astype(
+            jnp.bfloat16
+        )
+
+
+def gate_part(gates, lanes):
+    return pl.pallas_call(
+        gate_kernel,
+        out_shape=jax.ShapeDtypeStruct((256, TILE_ROWS), jnp.bfloat16),
+        in_specs=[VMEM, VMEM],
+        out_specs=VMEM,
+        compiler_params=LIMIT,
+        name="gates",
+    )(gates, lanes)
+
+
+def expert_kernel(
+    rows_ref, first_own, second_own, first_other, second_other, out_ref,
+    first_ref, second_ref, flat_ref, input_ref, total_ref, first_sem, second_sem,
+):
+    sources = ((first_own, second_own), (first_other, second_other))
+    copies = []
+    for piece, (first, second) in enumerate(sources):
+        for part in range(2):
+            copies.append(
+                pltpu.make_async_copy(
+                    first.at[part], first_ref.at[piece, part], first_sem.at[piece, part]
+                )
+            )
+        copies.append(
+            pltpu.make_async_copy(second, second_ref.at[piece], second_sem.at[piece])
+        )
+    for copy in copies:
+        copy.start()
+    flat_ref[...] = rows_ref[...].astype(jnp.float32)
+    for at in range(PIECES):
+        input_ref[:, at * 128 : (at + 1) * 128] = flat_ref[
+            pl.ds(at, ROWS, stride=PIECES), :
+        ].astype(jnp.bfloat16)
+    for piece in range(2):
+        copies[3 * piece].wait()
+        gate = jnp.dot(input_ref[...], first_ref[piece, 0], preferred_element_type=jnp.float32)
+        copies[3 * piece + 1].wait()
+        up = jnp.dot(input_ref[...], first_ref[piece, 1], preferred_element_type=jnp.float32)
+        hidden = (gate / (1.0 + jnp.exp(-gate)) * up).astype(jnp.bfloat16)
+        copies[3 * piece + 2].wait()
+        product = jnp.dot(hidden, second_ref[piece], preferred_element_type=jnp.float32)
+        if piece == 0:
+            total_ref[...] = product
+        else:
+            total_ref[...] += product
+    for at in range(PIECES):
+        flat_ref[pl.ds(at, ROWS, stride=PIECES), :] = total_ref[:, at * 128 : (at + 1) * 128]
+    out_ref[...] = flat_ref[...].astype(jnp.bfloat16)
+
+
+def expert_part(rows, first, second, first_other, second_other):
+    anywhere = pl.BlockSpec(memory_space=pl.ANY)
+    width = second.shape[0]
+    return pl.pallas_call(
+        expert_kernel,
+        out_shape=jax.ShapeDtypeStruct((TILE_ROWS, 128), jnp.bfloat16),
+        in_specs=[VMEM] + [anywhere] * 4,
+        out_specs=VMEM,
+        scratch_shapes=[
+            pltpu.VMEM((2, 2, D, width), jnp.bfloat16),
+            pltpu.VMEM((2, width, D), jnp.bfloat16),
+            pltpu.VMEM((TILE_ROWS, 128), jnp.float32),
+            pltpu.VMEM((ROWS, D), jnp.bfloat16),
+            pltpu.VMEM((ROWS, D), jnp.float32),
+            pltpu.SemaphoreType.DMA((2, 2)),
+            pltpu.SemaphoreType.DMA((2,)),
+        ],
+        compiler_params=LIMIT,
+        name="experts",
+    )(rows, first, second, first_other, second_other)
+
+
+def combine_kernel(residual_ref, gates_ref, rows_ref, out_ref):
+    tall = jnp.dot(gates_ref[...], rows_ref[...], preferred_element_type=jnp.float32)
+    for at in range(PIECES):
+        columns = slice(at * 128, (at + 1) * 128)
+        out_ref[:, columns] = (
+            residual_ref[:, columns] + tall[at * SLAB : (at + 1) * SLAB, :]
+        ).astype(jnp.bfloat16)
+
+
+def combine_part(residual, gates, rows):
+    return pl.pallas_call(
+        combine_kernel,
+        out_shape=jax.ShapeDtypeStruct((SLAB, D), jnp.bfloat16),
+        in_specs=[VMEM] * 3,
+        out_specs=VMEM,
+        compiler_params=LIMIT,
+        name="combine",
+    )(residual, gates, rows)
+
+
+def chips(rows):
+    shaped = rows.reshape(EXPERTS, CAP * PIECES, 128)
+    return lax.all_to_all(shaped, CHIP_AXES, split_axis=0, concat_axis=0, tiled=True).reshape(
+        TILE_ROWS, 128
+    )
 
 
 def body(
@@ -167,92 +501,35 @@
     expert_second,
 ):
     z, y, c = (lax.axis_index(name) for name in ("z", "y", "c"))
+    place = scalars(z, y, c)
+    core = scalars(c)
     own_weights = head_weights.transpose(0, 2, 1)
     other_weights = swap_core(own_weights)
-    output_own = lax.all_gather(output_weight, "y")
-    output_other = swap_core(output_own)
-
-    half_tokens = lax.dynamic_index_in_dim(
-        tokens.reshape(16, 2, 16, D), c, axis=1, keepdims=False
-    ).reshape(HALF, D)
-    normed = norm_scaled(half_tokens.astype(jnp.float32), attention_gain).astype(jnp.bfloat16)
-
-    def project(weights):
-        return jnp.einsum("afd,td->aft", weights, normed, preferred_element_type=jnp.float32).astype(
-            jnp.bfloat16
-        )
-
-    own, other = project(own_weights), project(other_weights)
-    lower = jnp.where(c == 0, own[:2], other[:2])
-    upper = jnp.where(c == 0, other[:2], own[:2])
-    q_own = jnp.concatenate([lower[0], upper[0]])
-    kv = jnp.concatenate([lower[1], upper[1], own[2], other[2]])
+    normed = norm_part(core, tokens, attention_gain)
+    q_own, kv = project_part(core, normed, own_weights, other_weights)
+    kvs = [kv] + [shift(kv, "x", step) for step in (1, 2, 3)]
     q_other = swap_core(q_own)
-    kvs = [kv] + [
-        lax.ppermute(kv, "x", [(i, i + step) for i in range(4 - step)]) for step in (1, 2, 3)
-    ]
+    later = lax.optimization_barrier((kv, output_weight, expert_first, expert_second))[1:]
+    output_own = [later[0]] + [shift(later[0], "y", step) for step in (1, 2, 3)]
+    output_other = [swap_core(rows) for rows in output_own]
+    first_other, second_other = swap_core(later[1]), swap_core(later[2])
+    rows_map, lanes_map = map_part(expert_index)
+
     carried = carried_part(carried_state.T, q_own, q_other)
-    mine, send = window_part(c.reshape(1), q_own, q_other, kvs, carried)
-    raw = (mine + swap_core(send).astype(jnp.float32)) / HD
-    attended = norm_scaled(raw, 1.0).astype(jnp.bfloat16)
-
-    by_y = attended.reshape(4, 4, SLAB, HD).transpose(1, 0, 2, 3).reshape(4, 64, HD)
-
-    def block(array, at):
-        return lax.dynamic_index_in_dim(array, at % 4, axis=0, keepdims=False)
-
-    pieces = [block(by_y, y)] + [shift(block(by_y, y + step), "y", step) for step in (1, 2, 3)]
-    partial = jnp.zeros((64, D), jnp.float32)
-    for step in range(4):
-        for columns, weights in ((slice(0, 64), output_own), (slice(64, 128), output_other)):
-            partial = partial + jnp.dot(
-                pieces[step][:, columns],
-                block(weights, y - step + 4),
-                preferred_element_type=jnp.float32,
-            )
-    by_z = partial.reshape(4, SLAB, D)
-    attention_sum = block(by_z, z)
-    by_z = by_z.astype(jnp.bfloat16)
-    for step in (1, 2, 3):
-        attention_sum = attention_sum + shift(block(by_z, z + step), "z", step).astype(jnp.float32)
+    x = lax.axis_index("x")
+    mine, send = window_part(scalars(c, x), q_own, q_other, kvs, carried)
+    pieces = attend_part(place, mine, swap_core(send))
+    pieces = [pieces[0]] + [shift(pieces[step], "y", step) for step in (1, 2, 3)]
+    sums = output_part(place, pieces, output_own, output_other)
+    received = [shift(sums[step], "z", step) for step in (1, 2, 3)]
     slab = lax.dynamic_slice_in_dim(tokens, ((z * 4 + y) * 2 + c) * SLAB, SLAB, 0)
-    residual = slab.astype(jnp.float32) + attention_sum
-    expert_input = norm_scaled(residual, expert_gain).astype(jnp.bfloat16)
-    logits = jnp.dot(expert_input, router_weight, preferred_element_type=jnp.float32)
-    matches = expert_index[:, :, None] == jnp.arange(EXPERTS, dtype=jnp.int32)
-    gate_values = jax.nn.sigmoid(jnp.sum(jnp.where(matches, logits[:, None, :], 0.0), axis=2))
-    flat_matches = matches.reshape(SLAB * TOP, EXPERTS).astype(jnp.int32)
-    earlier = jnp.cumsum(flat_matches, axis=0) - flat_matches
-    slots = jnp.sum(earlier * flat_matches, axis=1).reshape(SLAB, TOP)
-    cells = EXPERTS * CAP
-    hits = (expert_index * CAP + slots)[:, :, None] == jnp.arange(cells, dtype=jnp.int32)
-    send_map = jnp.sum(hits.astype(jnp.bfloat16), axis=1)
-    combine_map = jnp.sum(jnp.where(hits, gate_values[:, :, None], 0.0), axis=1)
-    outgoing = (
-        lax.dot_general(
-            send_map, expert_input, (((0,), (0,)), ((), ())), preferred_element_type=jnp.float32
-        )
-        .astype(jnp.bfloat16)
-        .reshape(EXPERTS, CAP, D)
-    )
-    arrived = lax.all_to_all(outgoing, CHIP_AXES, split_axis=0, concat_axis=0, tiled=True).reshape(cells, D)
-    arrived_other = swap_core(arrived)
-
-    def expert(rows):
-        gate = jnp.dot(rows, expert_first[0], preferred_element_type=jnp.float32)
-        up = jnp.dot(rows, expert_first[1], preferred_element_type=jnp.float32)
-        hidden = (jax.nn.silu(gate) * up).astype(jnp.bfloat16)
-        return jnp.dot(hidden, expert_second, preferred_element_type=jnp.float32)
-
-    back = swap_core(expert(arrived_other).astype(jnp.bfloat16))
-    produced = (expert(arrived) + back.astype(jnp.float32)).astype(jnp.bfloat16)
-    returned = lax.all_to_all(
-        produced.reshape(EXPERTS, CAP, D), CHIP_AXES, split_axis=0, concat_axis=0, tiled=True
-    ).reshape(cells, D)
-    expert_sum = jnp.dot(
-        combine_map.astype(jnp.bfloat16), returned, preferred_element_type=jnp.float32
-    )
-    return (residual + expert_sum).astype(jnp.bfloat16)
+    residual, outgoing, gates = dispatch_part(
+        slab, sums[0], received, expert_gain, router_weight.T, rows_map
+    )
+    arrived = chips(outgoing)
+    gate_map = gate_part(gates, lanes_map)
+    produced = expert_part(arrived, expert_first, expert_second, first_other, second_other)
+    return combine_part(residual, gate_map, chips(produced))
 
 
 def solution(mesh):

time: 143 us -> 119 us (0.83)
  matrix products: 24.2 us -> 0 us
  Pallas kernels: 7.44 us -> 23.2 us
  between operations: 14 us -> 0.21 us
  other arithmetic: 7.25 us -> 0.15 us
  waiting for transfers between devices: 27.4 us -> 31.2 us
  blocking collectives: 24.7 us -> 21.7 us
  starting transfers between devices: 26.3 us -> 28.8 us
  local copies, waits for them, and re-layouts: 10.9 us -> 13 us
    dot_general x17 -> x0, matrix products: 24.2 us -> none  [the longest x2 7.76 us: expert(): return jnp.dot(hidden, expert_second, preferred_element_type=jnp.float32)]
    pallas_call x0 -> x9, Pallas kernels: none -> 15.2 us  [the longest x1 6.35 us: expert_part(): pl.pallas_call(expert_kernel, out_shape=jax.ShapeDtypeStruct((TILE_ROWS,...]
    ppermute x6 -> x12, starting transfers between devices: 11.4 us -> 22.6 us  [shift(): return lax.ppermute(array, axis, [(i, (i + step) % 4) for i in range(4)])]
    unnamed x19 -> x37, local copies, waits for them, and re-layouts: 1.02 us -> 12.1 us
    reshape x6 -> x0, local copies, waits for them, and re-layouts: 9.62 us -> none  [the longest x1 3.27 us: body(): produced.reshape(EXPERTS, CAP, D)]
    ppermute x3 -> x0, starting transfers between devices: 9.42 us -> none  [body(): lax.ppermute(kv, 'x', [(i, i + step) for i in range(4 - step)])]
    ppermute x6 -> x12, waiting for transfers between devices: 4.36 us -> 11.5 us  [shift(): return lax.ppermute(array, axis, [(i, (i + step) % 4) for i in range(4)])]
    convert_element_type x5 -> x0, other arithmetic: 5 us -> none  [the longest x1 2.95 us: body(): half_tokens.astype(jnp.float32)]
  transfers between devices with their start and end apart: 17 -> 22, of which waited for: 8 -> 10; matrix products, arithmetic and copies ran while one was open for 11% -> 1% of each run, Pallas kernels for 5% -> 13%
where the time goes in v2:
time: 119 us; the launch traced here: 118 us
  waiting for transfers between devices  31.2 us (26%)
  starting transfers between devices  28.8 us (24%)
  Pallas kernels  23.2 us (19%)
  blocking collectives  21.7 us (18%)
  local copies, waits for them, and re-layouts  13 us (11%)
    ppermute x12, starting transfers between devices, shift(): return lax.ppermute(array, axis, [(i, (i + step) % 4) for i in range(4)])  22.6 us
    all_to_all x1, blocking collectives, chips(): lax.all_to_all(shaped, CHIP_AXES, split_axis=0, concat_axis=0, tiled=True)  21.7 us
    all_to_all x1, waiting for transfers between devices, chips(): lax.all_to_all(shaped, CHIP_AXES, split_axis=0, concat_axis=0, tiled=True)  13.2 us
    unnamed x37, local copies, waits for them, and re-layouts  12.1 us
    ppermute x12, waiting for transfers between devices, shift(): return lax.ppermute(array, axis, [(i, (i + step) % 4) for i in range(4)])  11.5 us
    ppermute x9, waiting for transfers between devices, swap_core(): return lax.ppermute(array, 'c', [(0, 1), (1, 0)])  6.54 us
    pallas_call x1, Pallas kernels, expert_part(): pl.pallas_call(expert_kernel, out_shape=jax.ShapeDtypeStruct((TILE_ROWS,...  6.35 us
    pallas_call x1, Pallas kernels, carried_part(): pl.pallas_call(carried_kernel, out_shape=jax.ShapeDtypeStruct((64, SHARD)...  6.35 us
  transfers between devices with their start and end apart: 22, of which 10 were waited for; matrix products, arithmetic and copies ran while one was open for 1% of the time, Pallas kernels for 13%

profile of v2, /device:TPU:0, one launch (start us, length us, event | category | flops | bytes accessed | tf_op | source)
XLA Modules:
  0.0 118.2 jit_solution(7425034867365994548)
XLA Ops:
  0.0 0.0 collective-permute-start
  0.0 1.6 %copy-done = bf16[512,2048]{1,0:T(8,128)(2,1)S(1)} copy-done((bf16[512,2048]{1,0:T(8,128)(2,1)S(1)}, bf16[512,2048]{1,0:T(8,128)(2,1)}, u32[]{:S(2)}) %copy-start) | copy-done | bytes 2097176
  1.6 0.7 copy-done.13
  2.3 0.6 norm.1.normed_ref
  2.9 0.0 copy-start.1
  2.9 0.0 copy-start.3
  2.9 0.0 collective-permute-done.other_ref
  2.9 0.5 copy-done.2
  3.4 0.8 project.1
  4.3 0.6 collective-permute-start.19
  4.9 0.2 collective-permute-start.20
  5.0 1.6 %collective-permute-start.2 = (bf16[256,256]{1,0:T(8,128)(2,1)S(1)}, bf16[256,256]{1,0:T(8,128)(2,1)S(1)}, u32[]{:S(2)}, u32[]{:S(2)}) collective-permute-start(bf16[256,256]{1,0:T(8,128)(2,1)S(1)} %get-tuple-element.26.kv0), channel_id=1, source_target_pairs={{0,32},{32,64},{64,96},{96,0},{1,33},{33,65},{65,97},{97,1},{2,34}... | collective-permute-start | bytes 393224 | tf_op jit(solution)/shard_map/ppermute | solution.py:29
  6.6 0.1 collective-permute-start.1
  6.7 0.1 pad_add_fusion.1.core_ref
  6.7 2.7 %collective-permute-start.3 = (bf16[256,256]{1,0:T(8,128)(2,1)S(1)}, bf16[256,256]{1,0:T(8,128)(2,1)S(1)}, u32[]{:S(2)}, u32[]{:S(2)}) collective-permute-start(bf16[256,256]{1,0:T(8,128)(2,1)S(1)} %get-tuple-element.26.kv0), channel_id=1, source_target_pairs={{0,64},{32,96},{64,0},{96,32},{1,65},{33,97},{65,1},{97,33},{2,66}... | collective-permute-start | bytes 393224 | tf_op jit(solution)/shard_map/ppermute | solution.py:29
  9.5 4.1 %collective-permute-done.1.q_other_ref = bf16[128,256]{1,0:T(8,128)(2,1)S(1)} collective-permute-done((bf16[128,256]{1,0:T(8,128)(2,1)S(1)}, bf16[128,256]{1,0:T(8,128)(2,1)S(1)}, u32[]{:S(2)}, u32[]{:S(2)}) %collective-permute-start.1) | collective-permute-done | bytes 65568 | tf_op jit(solution)/shard_map/ppermute | solution.py:25
  13.6 2.8 %collective-permute-start.4 = (bf16[256,256]{1,0:T(8,128)(2,1)S(1)}, bf16[256,256]{1,0:T(8,128)(2,1)S(1)}, u32[]{:S(2)}, u32[]{:S(2)}) collective-permute-start(bf16[256,256]{1,0:T(8,128)(2,1)S(1)} %get-tuple-element.26.kv0), channel_id=1, source_target_pairs={{0,96},{32,0},{64,32},{96,64},{1,97},{33,1},{65,33},{97,65},{2,98}... | collective-permute-start | bytes 393224 | tf_op jit(solution)/shard_map/ppermute | solution.py:29
  16.4 1.6 %collective-permute-start.9 = (bf16[64,2048]{1,0:T(8,128)(2,1)S(1)}, bf16[64,2048]{1,0:T(8,128)(2,1)S(1)}, u32[]{:S(2)}, u32[]{:S(2)}) collective-permute-start(bf16[64,2048]{1,0:T(8,128)(2,1)S(1)} %copy-done.3), channel_id=1, source_target_pairs={{0,2},{2,4},{4,6},{6,0},{1,3},{3,5},{5,7},{7,1},{8,10},{10,12},{12... | collective-permute-start | bytes 786440 | tf_op jit(solution)/shard_map/ppermute | solution.py:29
  18.0 1.6 %copy-done.17 = f32[8256,64]{0,1:T(8,128)S(1)} copy-done((f32[8256,64]{0,1:T(8,128)S(1)}, f32[8256,64]{0,1:T(8,128)}, u32[]{:S(2)}) %copy-start.17) | copy-done | bytes 2113560
  19.6 6.4 %carried.1.carried_ref = f32[64,512]{1,0:T(8,128)S(1)} custom-call(f32[64,8256]{1,0:T(8,128)S(1)} %bitcast.23, bf16[128,256]{1,0:T(8,128)(2,1)S(1)} %get-tuple-element.25.q_own_ref, bf16[128,256]{1,0:T(8,128)(2,1)S(1)} %collective-permute-done.1.q_other_ref), custom_call_target="tpu_custom_call" | custom-call | flops 2147483648 | bytes 2113536 | tf_op jit(solution)/shard_map/carried/pallas_call | solution.py:110
  25.9 0.0 copy-start.4
  25.9 1.6 %window.1 = (f32[256,128]{1,0:T(8,128)S(1)}, bf16[256,128]{1,0:T(8,128)(2,1)S(1)}) custom-call(s32[2]{0:T(128)S(1)} %pad_add_fusion.1.core_ref, bf16[128,256]{1,0:T(8,128)(2,1)S(1)} %get-tuple-element.25.q_own_ref, bf16[128,256]{1,0:T(8,128)(2,1)S(1)} %collective-permute-done.1.q_other_ref, bf16[256,256]{1,0:T(8,128)(2,1)S(1)} %get-tuple-element.26.kv0, ...), custom_call_target="tpu_custom_call" | custom-call | tf_op jit(solution)/shard_map/window/pallas_call | solution.py:157
  27.6 0.1 collective-permute-start.5
  27.7 0.1 pad_add_fusion.place_ref
  27.8 1.2 collective-permute-done.5.received_ref
  28.9 0.7 attend.1
  29.6 1.7 %collective-permute-start.6 = (bf16[64,128]{1,0:T(8,128)(2,1)S(1)}, bf16[64,128]{1,0:T(8,128)(2,1)S(1)}, u32[]{:S(2)}, u32[]{:S(2)}) collective-permute-start(bf16[64,128]{1,0:T(8,128)(2,1)S(1)} %get-tuple-element.30), channel_id=1, source_target_pairs={{0,2},{2,4},{4,6},{6,0},{1,3},{3,5},{5,7},{7,1},{8,10},{10,12},{12... | collective-permute-start | bytes 49160 | tf_op jit(solution)/shard_map/ppermute | solution.py:29
  31.3 1.5 %collective-permute-start.7 = (bf16[64,128]{1,0:T(8,128)(2,1)S(1)}, bf16[64,128]{1,0:T(8,128)(2,1)S(1)}, u32[]{:S(2)}, u32[]{:S(2)}) collective-permute-start(bf16[64,128]{1,0:T(8,128)(2,1)S(1)} %get-tuple-element.31), channel_id=1, source_target_pairs={{0,4},{2,6},{4,0},{6,2},{1,5},{3,7},{5,1},{7,3},{8,12},{10,14},{12... | collective-permute-start | bytes 49160 | tf_op jit(solution)/shard_map/ppermute | solution.py:29
  32.8 1.8 %collective-permute-done.6.rest_1_ = bf16[64,128]{1,0:T(8,128)(2,1)S(1)} collective-permute-done((bf16[64,128]{1,0:T(8,128)(2,1)S(1)}, bf16[64,128]{1,0:T(8,128)(2,1)S(1)}, u32[]{:S(2)}, u32[]{:S(2)}) %collective-permute-start.6) | collective-permute-done | bytes 16416 | tf_op jit(solution)/shard_map/ppermute | solution.py:29
  34.6 0.6 copy-done.7
  35.2 0.6 collective-permute-start.8
  35.8 0.7 collective-permute-done.7.rest_2_
  36.5 0.6 copy-done.9
  37.1 1.5 %collective-permute-start.10 = (bf16[64,2048]{1,0:T(8,128)(2,1)S(1)}, bf16[64,2048]{1,0:T(8,128)(2,1)S(1)}, u32[]{:S(2)}, u32[]{:S(2)}) collective-permute-start(bf16[64,2048]{1,0:T(8,128)(2,1)S(1)} %copy-done.3), channel_id=1, source_target_pairs={{0,4},{2,6},{4,0},{6,2},{1,5},{3,7},{5,1},{7,3},{8,12},{10,14},{12... | collective-permute-start | bytes 786440 | tf_op jit(solution)/shard_map/ppermute | solution.py:29
  38.6 0.4 collective-permute-done.8.rest_3_
  39.0 0.6 copy-done.11
  39.6 2.0 %collective-permute-start.11 = (bf16[64,2048]{1,0:T(8,128)(2,1)S(1)}, bf16[64,2048]{1,0:T(8,128)(2,1)S(1)}, u32[]{:S(2)}, u32[]{:S(2)}) collective-permute-start(bf16[64,2048]{1,0:T(8,128)(2,1)S(1)} %copy-done.3), channel_id=1, source_target_pairs={{0,6},{2,0},{4,2},{6,4},{1,7},{3,1},{5,3},{7,5},{8,14},{10,8},{12,... | collective-permute-start | bytes 786440 | tf_op jit(solution)/shard_map/ppermute | solution.py:29
  41.7 3.9 %collective-permute-done.10.rest_6_ = bf16[64,2048]{1,0:T(8,128)(2,1)S(1)} collective-permute-done((bf16[64,2048]{1,0:T(8,128)(2,1)S(1)}, bf16[64,2048]{1,0:T(8,128)(2,1)S(1)}, u32[]{:S(2)}, u32[]{:S(2)}) %collective-permute-start.10) | collective-permute-done | bytes 262176 | tf_op jit(solution)/shard_map/ppermute | solution.py:29
  45.5 4.7 %collective-permute-done.11.rest_7_ = bf16[64,2048]{1,0:T(8,128)(2,1)S(1)} collective-permute-done((bf16[64,2048]{1,0:T(8,128)(2,1)S(1)}, bf16[64,2048]{1,0:T(8,128)(2,1)S(1)}, u32[]{:S(2)}, u32[]{:S(2)}) %collective-permute-start.11) | collective-permute-done | bytes 262176 | tf_op jit(solution)/shard_map/ppermute | solution.py:29
  50.2 0.7 copy-done.5
  50.9 0.5 collective-permute-start.15
  51.4 0.4 collective-permute-done.14.rest_10_
  51.9 0.8 collective-permute-done.15.rest_11_
  52.7 0.9 copy-done.6
  53.7 0.7 copy-done.8
  54.4 0.7 copy-done.10
  55.1 0.7 copy-done.12
  55.8 0.7 copy-done.16
  56.5 2.5 %output.1 = (f32[16,2048]{1,0:T(8,128)S(1)}, bf16[16,2048]{1,0:T(8,128)(2,1)}, bf16[16,2048]{1,0:T(8,128)(2,1)}, bf16[16,2048]{1,0:T(8,128)(2,1)}) custom-call(s32[3]{0:T(128)S(1)} %copy-done.16, bf16[64,128]{1,0:T(8,128)(2,1)S(1)} %get-tuple-element.29.rest_0_, bf16[64,128]{1,0:T(8,128)(2,1)S(1)} %copy-done.8, bf16[64,128]{1,0:T(8,128)(2,1)S(1)} %copy-done.10, ...), custom_call_target="tpu_custom_call" | custom-call | tf_op jit(solution)/shard_map/output/pallas_call | solution.py:275
  59.0 2.0 %collective-permute-start.16 = (bf16[16,2048]{1,0:T(8,128)(2,1)}, bf16[16,2048]{1,0:T(8,128)(2,1)S(1)}, u32[]{:S(2)}, u32[]{:S(2)}) collective-permute-start(bf16[16,2048]{1,0:T(8,128)(2,1)} %get-tuple-element.35), channel_id=1, source_target_pairs={{0,8},{8,16},{16,24},{24,0},{1,9},{9,17},{17,25},{25,1},{2,10},{10... | collective-permute-start | bytes 196616 | tf_op jit(solution)/shard_map/ppermute | solution.py:29
  61.0 3.5 %collective-permute-start.17 = (bf16[16,2048]{1,0:T(8,128)(2,1)}, bf16[16,2048]{1,0:T(8,128)(2,1)S(1)}, u32[]{:S(2)}, u32[]{:S(2)}) collective-permute-start(bf16[16,2048]{1,0:T(8,128)(2,1)} %get-tuple-element.36), channel_id=1, source_target_pairs={{0,16},{8,24},{16,0},{24,8},{1,17},{9,25},{17,1},{25,9},{2,18},{10... | collective-permute-start | bytes 196616 | tf_op jit(solution)/shard_map/ppermute | solution.py:29
  64.5 1.0 collective-permute-start.18
  65.5 0.8 constant_dynamic-slice_fusion.slab_ref
  66.4 0.8 copy.11.index_ref
  67.1 1.8 %maps.1 = (bf16[3072,256]{1,0:T(8,128)(2,1)S(1)}, f32[16,3072]{1,0:T(8,128)S(1)}) custom-call(s32[16,8]{1,0:T(8,128)S(1)} %copy.11.index_ref), custom_call_target="tpu_custom_call" | custom-call | tf_op jit(solution)/shard_map/maps/pallas_call | solution.py:335
  69.0 0.0 copy-start.14
  69.1 0.7 copy-done.14
  69.7 0.8 dispatch.1
  70.5 21.7 %all_to_all.10 = bf16[64,48,128]{2,1,0:T(8,128)(2,1)S(1)} all-to-all(bf16[64,48,128]{2,1,0:T(8,128)(2,1)S(1)} %bitcast.17), channel_id=1, replica_groups=mesh['x'=4,'z'=4,'y'=4,'c'=2] {'x','z','y'}, dimensions={0} | all-to-all | bytes 1572864 | tf_op jit(solution)/shard_map/all_to_all | solution.py:486
  92.2 6.4 %experts.1 = bf16[3072,128]{1,0:T(8,128)(2,1)} custom-call(bf16[3072,128]{1,0:T(8,128)(2,1)S(1)} %bitcast.14, bf16[2,2048,512]{2,1,0:T(8,128)(2,1)} %first_own.1, bf16[512,2048]{1,0:T(8,128)(2,1)S(1)} %copy-done.1, bf16[2,2048,512]{2,1,0:T(8,128)(2,1)} %collective-permute-done.19.first_other, bf16[512,2048]{1,0:T(8,128)(2,1)} %collective-permute-done.20.second_other), custom_call_target="tpu_custom_call" | custom-call | tf_op jit(solution)/shard_map/experts/pallas_call | solution.py:445
  98.6 4.8 %all-to-all-start.1 = ((bf16[64,48,128]{2,1,0:T(8,128)(2,1)}), bf16[64,48,128]{2,1,0:T(8,128)(2,1)S(1)}, u32[]{:S(2)}, u32[]{:S(2)}) async-start(bf16[64,48,128]{2,1,0:T(8,128)(2,1)} %bitcast.12), calls=%async_computation.1 | async-start | bytes 1572864 | tf_op jit(solution)/shard_map/all_to_all | solution.py:486
  103.4 0.4 gates.1.gates_ref
  103.8 13.2 %all-to-all-done.1 = bf16[64,48,128]{2,1,0:T(8,128)(2,1)S(1)} async-done(((bf16[64,48,128]{2,1,0:T(8,128)(2,1)}), bf16[64,48,128]{2,1,0:T(8,128)(2,1)S(1)}, u32[]{:S(2)}, u32[]{:S(2)}) %all-to-all-start.1) | async-done | bytes 786464 | tf_op jit(solution)/shard_map/all_to_all | solution.py:486
  117.0 1.2 %combine.1 = bf16[16,2048]{1,0:T(8,128)(2,1)} custom-call(f32[16,2048]{1,0:T(8,128)S(1)} %get-tuple-element.39.residual_ref, bf16[256,3072]{1,0:T(8,128)(2,1)S(1)} %gates.1.gates_ref, bf16[3072,128]{1,0:T(8,128)(2,1)S(1)} %bitcast.15), custom_call_target="tpu_custom_call" | custom-call | tf_op jit(solution)/shard_map/combine/pallas_call | solution.py:474
  (32 shorter events, 0.1 us)
Async XLA Ops:
  0.0 2.9 %collective-permute-start = (bf16[3,64,2048]{2,1,0:T(8,128)(2,1)}, bf16[3,64,2048]{2,1,0:T(8,128)(2,1)S(1)}, u32[]{:S(2)}, u32[]{:S(2)}) collective-permute-start(bf16[3,64,2048]{2,1,0:T(8,128)(2,1)} %bitcast.18), channel_id=1, source_target_pairs={{0,1},{1,0},{2,3},{3,2},{4,5},{5,4},{6,7},{7,6},{8,9},{9,8},{10,11... | collective-permute-start | bytes 2359304 | tf_op jit(solution)/shard_map/ppermute | solution.py:25
  0.0 1.6 %copy-start = (bf16[512,2048]{1,0:T(8,128)(2,1)S(1)}, bf16[512,2048]{1,0:T(8,128)(2,1)}, u32[]{:S(2)}) copy-start(bf16[512,2048]{1,0:T(8,128)(2,1)} %param.10) | copy-start | bytes 6291460
  1.6 0.7 copy-start.13
  2.3 1.1 copy-start.2
  2.9 2.0 %copy-start.1 = (bf16[512,2048]{1,0:T(8,128)(2,1)S(1)}, bf16[512,2048]{1,0:T(8,128)(2,1)}, u32[]{:S(2)}) copy-start(bf16[512,2048]{1,0:T(8,128)(2,1)} %second_own.1) | copy-start | bytes 6291460
  2.9 13.5 %copy-start.3 = (bf16[64,2048]{1,0:T(8,128)(2,1)S(1)}, bf16[64,2048]{1,0:T(8,128)(2,1)}, u32[]{:S(2)}) copy-start(bf16[64,2048]{1,0:T(8,128)(2,1)} %rest_4_) | copy-start | bytes 786436
  4.3 88.0 %collective-permute-start.19 = (bf16[2,2048,512]{2,1,0:T(8,128)(2,1)}, bf16[2,2048,512]{2,1,0:T(8,128)(2,1)}, u32[]{:S(2)}, u32[]{:S(2)}) collective-permute-start(bf16[2,2048,512]{2,1,0:T(8,128)(2,1)} %first_own.1), channel_id=1, source_target_pairs={{0,1},{1,0},{2,3},{3,2},{4,5},{5,4},{6,7},{7,6},{8,9},{9,8},{10,11... | collective-permute-start | bytes 12582920 | tf_op jit(solution)/shard_map/ppermute | solution.py:25
  4.9 87.4 %collective-permute-start.20 = (bf16[512,2048]{1,0:T(8,128)(2,1)S(1)}, bf16[512,2048]{1,0:T(8,128)(2,1)}, u32[]{:S(2)}, u32[]{:S(2)}) collective-permute-start(bf16[512,2048]{1,0:T(8,128)(2,1)S(1)} %copy-done.1), channel_id=1, source_target_pairs={{0,1},{1,0},{2,3},{3,2},{4,5},{5,4},{6,7},{7,6},{8,9},{9,8},{10,11... | collective-permute-start | bytes 6291464 | tf_op jit(solution)/shard_map/ppermute | solution.py:25
  5.0 11.3 %collective-permute-start.2 = (bf16[256,256]{1,0:T(8,128)(2,1)S(1)}, bf16[256,256]{1,0:T(8,128)(2,1)S(1)}, u32[]{:S(2)}, u32[]{:S(2)}) collective-permute-start(bf16[256,256]{1,0:T(8,128)(2,1)S(1)} %get-tuple-element.26.kv0), channel_id=1, source_target_pairs={{0,32},{32,64},{64,96},{96,0},{1,33},{33,65},{65,97},{97,1},{2,34}... | collective-permute-start | bytes 393224 | tf_op jit(solution)/shard_map/ppermute | solution.py:29
  6.6 7.0 %collective-permute-start.1 = (bf16[128,256]{1,0:T(8,128)(2,1)S(1)}, bf16[128,256]{1,0:T(8,128)(2,1)S(1)}, u32[]{:S(2)}, u32[]{:S(2)}) collective-permute-start(bf16[128,256]{1,0:T(8,128)(2,1)S(1)} %get-tuple-element.25.q_own_ref), channel_id=1, source_target_pairs={{0,1},{1,0},{2,3},{3,2},{4,5},{5,4},{6,7},{7,6},{8,9},{9,8},{10,11... | collective-permute-start | bytes 196616 | tf_op jit(solution)/shard_map/ppermute | solution.py:25
  6.7 19.2 %collective-permute-start.3 = (bf16[256,256]{1,0:T(8,128)(2,1)S(1)}, bf16[256,256]{1,0:T(8,128)(2,1)S(1)}, u32[]{:S(2)}, u32[]{:S(2)}) collective-permute-start(bf16[256,256]{1,0:T(8,128)(2,1)S(1)} %get-tuple-element.26.kv0), channel_id=1, source_target_pairs={{0,64},{32,96},{64,0},{96,32},{1,65},{33,97},{65,1},{97,33},{2,66}... | collective-permute-start | bytes 393224 | tf_op jit(solution)/shard_map/ppermute | solution.py:29
  13.6 12.4 %collective-permute-start.4 = (bf16[256,256]{1,0:T(8,128)(2,1)S(1)}, bf16[256,256]{1,0:T(8,128)(2,1)S(1)}, u32[]{:S(2)}, u32[]{:S(2)}) collective-permute-start(bf16[256,256]{1,0:T(8,128)(2,1)S(1)} %get-tuple-element.26.kv0), channel_id=1, source_target_pairs={{0,96},{32,0},{64,32},{96,64},{1,97},{33,1},{65,33},{97,65},{2,98}... | collective-permute-start | bytes 393224 | tf_op jit(solution)/shard_map/ppermute | solution.py:29
  16.4 25.3 %collective-permute-start.9 = (bf16[64,2048]{1,0:T(8,128)(2,1)S(1)}, bf16[64,2048]{1,0:T(8,128)(2,1)S(1)}, u32[]{:S(2)}, u32[]{:S(2)}) collective-permute-start(bf16[64,2048]{1,0:T(8,128)(2,1)S(1)} %copy-done.3), channel_id=1, source_target_pairs={{0,2},{2,4},{4,6},{6,0},{1,3},{3,5},{5,7},{7,1},{8,10},{10,12},{12... | collective-permute-start | bytes 786440 | tf_op jit(solution)/shard_map/ppermute | solution.py:29
  18.0 1.6 %copy-start.17 = (f32[8256,64]{0,1:T(8,128)S(1)}, f32[8256,64]{0,1:T(8,128)}, u32[]{:S(2)}) copy-start(f32[8256,64]{0,1:T(8,128)} %param.13) | copy-start | bytes 6340612
  25.9 43.1 %copy-start.4 = (bf16[2048,64]{0,1:T(8,128)(2,1)S(1)}, bf16[2048,64]{0,1:T(8,128)(2,1)}, u32[]{:S(2)}) copy-start(bf16[2048,64]{0,1:T(8,128)(2,1)} %param.16) | copy-start | bytes 786436
  27.6 1.3 %collective-permute-start.5 = (bf16[256,128]{1,0:T(8,128)(2,1)S(1)}, bf16[256,128]{1,0:T(8,128)(2,1)S(1)}, u32[]{:S(2)}, u32[]{:S(2)}) collective-permute-start(bf16[256,128]{1,0:T(8,128)(2,1)S(1)} %get-tuple-element.28), channel_id=1, source_target_pairs={{0,1},{1,0},{2,3},{3,2},{4,5},{5,4},{6,7},{7,6},{8,9},{9,8},{10,11... | collective-permute-start | bytes 196616 | tf_op jit(solution)/shard_map/ppermute | solution.py:25
  27.8 22.5 %copy-start.15 = (s32[3]{0:T(128)}, s32[3]{0:T(128)S(1)}, u32[]{:S(2)}) copy-start(s32[3]{0:T(128)S(1)} %pad_add_fusion.place_ref) | copy-start | bytes 40
  29.6 5.0 %collective-permute-start.6 = (bf16[64,128]{1,0:T(8,128)(2,1)S(1)}, bf16[64,128]{1,0:T(8,128)(2,1)S(1)}, u32[]{:S(2)}, u32[]{:S(2)}) collective-permute-start(bf16[64,128]{1,0:T(8,128)(2,1)S(1)} %get-tuple-element.30), channel_id=1, source_target_pairs={{0,2},{2,4},{4,6},{6,0},{1,3},{3,5},{5,7},{7,1},{8,10},{10,12},{12... | collective-permute-start | bytes 49160 | tf_op jit(solution)/shard_map/ppermute | solution.py:29
  31.3 5.2 %collective-permute-start.7 = (bf16[64,128]{1,0:T(8,128)(2,1)S(1)}, bf16[64,128]{1,0:T(8,128)(2,1)S(1)}, u32[]{:S(2)}, u32[]{:S(2)}) collective-permute-start(bf16[64,128]{1,0:T(8,128)(2,1)S(1)} %get-tuple-element.31), channel_id=1, source_target_pairs={{0,4},{2,6},{4,0},{6,2},{1,5},{3,7},{5,1},{7,3},{8,12},{10,14},{12... | collective-permute-start | bytes 49160 | tf_op jit(solution)/shard_map/ppermute | solution.py:29
  34.6 0.6 copy-start.7
  35.2 3.8 %collective-permute-start.8 = (bf16[64,128]{1,0:T(8,128)(2,1)S(1)}, bf16[64,128]{1,0:T(8,128)(2,1)S(1)}, u32[]{:S(2)}, u32[]{:S(2)}) collective-permute-start(bf16[64,128]{1,0:T(8,128)(2,1)S(1)} %get-tuple-element.32), channel_id=1, source_target_pairs={{0,6},{2,0},{4,2},{6,4},{1,7},{3,1},{5,3},{7,5},{8,14},{10,8},{12,... | collective-permute-start | bytes 49160 | tf_op jit(solution)/shard_map/ppermute | solution.py:29
  36.5 0.6 copy-start.9
  37.1 8.4 %collective-permute-start.10 = (bf16[64,2048]{1,0:T(8,128)(2,1)S(1)}, bf16[64,2048]{1,0:T(8,128)(2,1)S(1)}, u32[]{:S(2)}, u32[]{:S(2)}) collective-permute-start(bf16[64,2048]{1,0:T(8,128)(2,1)S(1)} %copy-done.3), channel_id=1, source_target_pairs={{0,4},{2,6},{4,0},{6,2},{1,5},{3,7},{5,1},{7,3},{8,12},{10,14},{12... | collective-permute-start | bytes 786440 | tf_op jit(solution)/shard_map/ppermute | solution.py:29
  39.0 0.6 copy-start.11
  39.6 10.6 %collective-permute-start.11 = (bf16[64,2048]{1,0:T(8,128)(2,1)S(1)}, bf16[64,2048]{1,0:T(8,128)(2,1)S(1)}, u32[]{:S(2)}, u32[]{:S(2)}) collective-permute-start(bf16[64,2048]{1,0:T(8,128)(2,1)S(1)} %copy-done.3), channel_id=1, source_target_pairs={{0,6},{2,0},{4,2},{6,4},{1,7},{3,1},{5,3},{7,5},{8,14},{10,8},{12,... | collective-permute-start | bytes 786440 | tf_op jit(solution)/shard_map/ppermute | solution.py:29
  41.7 8.5 %collective-permute-start.12 = (bf16[64,2048]{1,0:T(8,128)(2,1)S(1)}, bf16[64,2048]{1,0:T(8,128)(2,1)S(1)}, u32[]{:S(2)}, u32[]{:S(2)}) collective-permute-start(bf16[64,2048]{1,0:T(8,128)(2,1)S(1)} %copy-done.3), channel_id=1, source_target_pairs={{0,1},{1,0},{2,3},{3,2},{4,5},{5,4},{6,7},{7,6},{8,9},{9,8},{10,11... | collective-permute-start | bytes 786440 | tf_op jit(solution)/shard_map/ppermute | solution.py:25
  45.5 5.9 %collective-permute-start.13 = (bf16[64,2048]{1,0:T(8,128)(2,1)S(1)}, bf16[64,2048]{1,0:T(8,128)(2,1)}, u32[]{:S(2)}, u32[]{:S(2)}) collective-permute-start(bf16[64,2048]{1,0:T(8,128)(2,1)S(1)} %collective-permute-done.9.rest_5_), channel_id=1, source_target_pairs={{0,1},{1,0},{2,3},{3,2},{4,5},{5,4},{6,7},{7,6},{8,9},{9,8},{10,11... | collective-permute-start | bytes 786440 | tf_op jit(solution)/shard_map/ppermute | solution.py:25
  50.2 1.7 %collective-permute-start.14 = (bf16[64,2048]{1,0:T(8,128)(2,1)S(1)}, bf16[64,2048]{1,0:T(8,128)(2,1)}, u32[]{:S(2)}, u32[]{:S(2)}) collective-permute-start(bf16[64,2048]{1,0:T(8,128)(2,1)S(1)} %collective-permute-done.10.rest_6_), channel_id=1, source_target_pairs={{0,1},{1,0},{2,3},{3,2},{4,5},{5,4},{6,7},{7,6},{8,9},{9,8},{10,11... | collective-permute-start | bytes 786440 | tf_op jit(solution)/shard_map/ppermute | solution.py:25
  50.2 0.7 copy-start.5
  50.9 1.8 %collective-permute-start.15 = (bf16[64,2048]{1,0:T(8,128)(2,1)S(1)}, bf16[64,2048]{1,0:T(8,128)(2,1)}, u32[]{:S(2)}, u32[]{:S(2)}) collective-permute-start(bf16[64,2048]{1,0:T(8,128)(2,1)S(1)} %collective-permute-done.11.rest_7_), channel_id=1, source_target_pairs={{0,1},{1,0},{2,3},{3,2},{4,5},{5,4},{6,7},{7,6},{8,9},{9,8},{10,11... | collective-permute-start | bytes 786440 | tf_op jit(solution)/shard_map/ppermute | solution.py:25
  52.7 0.9 copy-start.6
  53.7 0.7 copy-start.8
  54.4 0.7 copy-start.10
  55.1 0.7 copy-start.12
  55.8 0.7 copy-start.16
  59.0 10.0 %collective-permute-start.16 = (bf16[16,2048]{1,0:T(8,128)(2,1)}, bf16[16,2048]{1,0:T(8,128)(2,1)S(1)}, u32[]{:S(2)}, u32[]{:S(2)}) collective-permute-start(bf16[16,2048]{1,0:T(8,128)(2,1)} %get-tuple-element.35), channel_id=1, source_target_pairs={{0,8},{8,16},{16,24},{24,0},{1,9},{9,17},{17,25},{25,1},{2,10},{10... | collective-permute-start | bytes 196616 | tf_op jit(solution)/shard_map/ppermute | solution.py:29
  61.0 8.0 %collective-permute-start.17 = (bf16[16,2048]{1,0:T(8,128)(2,1)}, bf16[16,2048]{1,0:T(8,128)(2,1)S(1)}, u32[]{:S(2)}, u32[]{:S(2)}) collective-permute-start(bf16[16,2048]{1,0:T(8,128)(2,1)} %get-tuple-element.36), channel_id=1, source_target_pairs={{0,16},{8,24},{16,0},{24,8},{1,17},{9,25},{17,1},{25,9},{2,18},{10... | collective-permute-start | bytes 196616 | tf_op jit(solution)/shard_map/ppermute | solution.py:29
  64.5 4.5 %collective-permute-start.18 = (bf16[16,2048]{1,0:T(8,128)(2,1)}, bf16[16,2048]{1,0:T(8,128)(2,1)S(1)}, u32[]{:S(2)}, u32[]{:S(2)}) collective-permute-start(bf16[16,2048]{1,0:T(8,128)(2,1)} %get-tuple-element.37), channel_id=1, source_target_pairs={{0,24},{8,0},{16,8},{24,16},{1,25},{9,1},{17,9},{25,17},{2,26},{10... | collective-permute-start | bytes 196616 | tf_op jit(solution)/shard_map/ppermute | solution.py:29
  69.0 0.7 copy-start.14
  98.6 18.4 %all-to-all-start.1 = ((bf16[64,48,128]{2,1,0:T(8,128)(2,1)}), bf16[64,48,128]{2,1,0:T(8,128)(2,1)S(1)}, u32[]{:S(2)}, u32[]{:S(2)}) async-start(bf16[64,48,128]{2,1,0:T(8,128)(2,1)} %bitcast.12), calls=%async_computation.1 | async-start | bytes 1572864 | tf_op jit(solution)/shard_map/all_to_all | solution.py:486

commit v3 on v2

--- a/solution.py
+++ b/solution.py
@@ -1,4 +1,3 @@
-import functools
 import math
 
 import jax
@@ -29,13 +28,19 @@
     return lax.ppermute(array, axis, [(i, (i + step) % 4) for i in range(4)])
 
 
-def scalars(*values):
-    return jnp.stack([jnp.asarray(value, jnp.int32) for value in values])
-
-
 VMEM = pl.BlockSpec(memory_space=pltpu.VMEM)
-SMEM = pl.BlockSpec(memory_space=pltpu.SMEM)
-LIMIT = pltpu.CompilerParams(vmem_limit_bytes=32 * 1024 * 1024)
+
+
+def room(mebibytes):
+    return pltpu.CompilerParams(vmem_limit_bytes=int(mebibytes * 1024 * 1024))
+
+
+def cost(microseconds):
+    return pl.CostEstimate(
+        flops=int(microseconds * 1e9), bytes_accessed=int(microseconds * 3e6), transcendentals=0
+    )
+
+
 ROWS = EXPERTS * CAP
 PIECES = D // 128
 TILE_ROWS = ROWS * PIECES
@@ -46,87 +51,75 @@
 
 
 GROUP = 8
-LOOPED = 112
 TAIL_AT = 8064
 
 
-def carried_kernel(m_ref, q_own_ref, q_other_ref, out_ref, q_ref, w_ref, tail_ref):
+def carried_kernel(m_ref, q_own_ref, q_other_ref, out_ref, q_ref, w_a, w_b, tail_ref):
+    tail_ref[:, : STATE - TAIL_AT] = m_ref[:, TAIL_AT:]
     q_ref[:, :HALF] = q_own_ref[...].astype(jnp.float32)
     q_ref[:, HALF:] = q_other_ref[...].astype(jnp.float32)
-    tail_ref[:, : STATE - TAIL_AT] = m_ref[:, TAIL_AT:]
     q_cols = jnp.concatenate([q_own_ref[...], q_other_ref[...]], axis=1)
     lane = lax.broadcasted_iota(jnp.int32, (64, 128), 1)
     root = math.sqrt(2.0)
-
-    def piece(first, second, turn, i):
-        joined = jnp.where(
-            lane < 128 - turn,
-            pltpu.roll(first, (128 - turn) % 128, 1),
-            pltpu.roll(second, (128 - turn) % 128, 1),
-        )
-        return jnp.where(lane > i, joined * root, jnp.where(lane == i, joined, 0.0)).astype(
-            jnp.bfloat16
-        )
-
-    def finish(rows):
-        spread = jnp.dot(w_ref[...], q_cols, preferred_element_type=jnp.float32)
-        total = spread[0:64] * rows[0]
-        for k in range(1, GROUP):
-            total = total + spread[64 * k : 64 * k + 64] * rows[k]
-        return total
-
-    out_ref[...] = jnp.zeros_like(out_ref)
-
-    def group(g, carry):
-        base = g * GROUP
+    weights = (w_a, w_b)
+
+    def prepare(number):
+        base = number * GROUP
         for k in range(GROUP):
             i = base + k
             offset = 127 * i - (i * (i - 1)) // 2
-            tile = pl.multiple_of((offset // 128) * 128, 128)
-            w_ref[64 * k : 64 * k + 64, :] = piece(
-                m_ref[:, pl.ds(tile, 128)],
-                m_ref[:, pl.ds(pl.multiple_of(tile + 128, 128), 128)],
-                offset - tile,
-                i,
-            )
-        out_ref[...] += finish([q_ref[pl.ds(base + k, 1), :] for k in range(GROUP)])
-        return carry
-
-    lax.fori_loop(0, LOOPED // GROUP, group, 0)
-    for base in range(LOOPED, HD, GROUP):
-        for k in range(GROUP):
-            i = base + k
-            offset = 127 * i - (i * (i - 1)) // 2
-            tile = (offset // 128) * 128
+            tile, turn = (offset // 128) * 128, offset % 128
             if tile < TAIL_AT:
                 first, second = m_ref[:, tile : tile + 128], m_ref[:, tile + 128 : tile + 256]
             else:
                 first, second = tail_ref[:, :128], tail_ref[:, 128:]
-            w_ref[64 * k : 64 * k + 64, :] = piece(first, second, offset - tile, i)
-        out_ref[...] += finish([q_ref[base + k : base + k + 1, :] for k in range(GROUP)])
+            if turn == 0:
+                joined = first
+            else:
+                joined = jnp.where(
+                    lane < 128 - turn,
+                    pltpu.roll(first, 128 - turn, 1),
+                    pltpu.roll(second, 128 - turn, 1),
+                )
+            weights[number % 2][64 * k : 64 * k + 64, :] = jnp.where(
+                lane > i, joined * root, jnp.where(lane == i, joined, 0.0)
+            ).astype(jnp.bfloat16)
+
+    prepare(0)
+    for number in range(HD // GROUP):
+        spread = jnp.dot(weights[number % 2][...], q_cols, preferred_element_type=jnp.float32)
+        if number + 1 < HD // GROUP:
+            prepare(number + 1)
+        base = number * GROUP
+        total = spread[0:64] * q_ref[base : base + 1, :]
+        for k in range(1, GROUP):
+            total = total + spread[64 * k : 64 * k + 64] * q_ref[base + k : base + k + 1, :]
+        if number == 0:
+            out_ref[...] = total
+        else:
+            out_ref[...] += total
 
 
 def carried_part(state_cols, q_own, q_other):
     return pl.pallas_call(
         carried_kernel,
         out_shape=jax.ShapeDtypeStruct((64, SHARD), jnp.float32),
-        in_specs=[pl.BlockSpec(memory_space=pltpu.VMEM)] * 3,
-        out_specs=pl.BlockSpec(memory_space=pltpu.VMEM),
+        in_specs=[VMEM] * 3,
+        out_specs=VMEM,
         scratch_shapes=[
             pltpu.VMEM((HD, SHARD), jnp.float32),
             pltpu.VMEM((64 * GROUP, HD), jnp.bfloat16),
+            pltpu.VMEM((64 * GROUP, HD), jnp.bfloat16),
             pltpu.VMEM((64, 256), jnp.float32),
         ],
-        compiler_params=pltpu.CompilerParams(vmem_limit_bytes=32 * 1024 * 1024),
-        cost_estimate=pl.CostEstimate(
-            flops=8192 * 512 * 128 * 4, bytes_accessed=64 * STATE * 4, transcendentals=0
-        ),
+        compiler_params=room(2),
+        cost_estimate=cost(5),
         name="carried",
     )(state_cols, q_own, q_other)
 
 
-def window_kernel(core_ref, q_own_ref, q_other_ref, kv0, kv1, kv2, kv3, carried_ref, mine_ref, send_ref):
-    core = core_ref[0]
+def window_kernel(q_own_ref, q_other_ref, kv0, kv1, kv2, kv3, carried_ref, mine_ref, send_ref):
+    core, shard = lax.axis_index("c"), lax.axis_index("x")
     q_cols = jnp.concatenate([q_own_ref[...], q_other_ref[...]], axis=1)
     key = lax.broadcasted_iota(jnp.int32, (HALF, SHARD), 0)
     query = lax.broadcasted_iota(jnp.int32, (HALF, SHARD), 1)
@@ -143,7 +136,7 @@
         if number == 0:
             weights = jnp.where(allowed, weights, 0.0)
         else:
-            weights = jnp.where(core_ref[1] >= number, weights, 0.0)
+            weights = jnp.where(shard >= number, weights, 0.0)
         total = total + jnp.dot(
             kv[HD:, :], weights.astype(jnp.bfloat16), preferred_element_type=jnp.float32
         )
@@ -153,46 +146,46 @@
     send_ref[...] = jnp.concatenate([lower[:, HALF:], upper[:, HALF:]], axis=0).T.astype(jnp.bfloat16)
 
 
-def window_part(core, q_own, q_other, kvs, carried):
+def window_part(q_own, q_other, kvs, carried):
     return pl.pallas_call(
         window_kernel,
         out_shape=(
             jax.ShapeDtypeStruct((HALF, HD), jnp.float32),
             jax.ShapeDtypeStruct((HALF, HD), jnp.bfloat16),
         ),
-        in_specs=[pl.BlockSpec(memory_space=pltpu.SMEM)]
-        + [pl.BlockSpec(memory_space=pltpu.VMEM)] * 7,
-        out_specs=(pl.BlockSpec(memory_space=pltpu.VMEM),) * 2,
-        compiler_params=pltpu.CompilerParams(vmem_limit_bytes=32 * 1024 * 1024),
+        in_specs=[VMEM] * 7,
+        out_specs=(VMEM,) * 2,
+        compiler_params=room(2),
+        cost_estimate=cost(2),
         name="window",
-    )(core, q_own, q_other, *kvs, carried)
-
-
-def norm_kernel(core_ref, tokens_ref, gain_ref, out_ref):
-    floats = tokens_ref[:, 0].astype(jnp.float32).reshape(128, D)
-    out_ref[...] = norm_scaled(floats, gain_ref[...]).astype(jnp.bfloat16)
-
-
-def norm_part(core, tokens, gain):
+    )(q_own, q_other, *kvs, carried)
+
+
+def norm_kernel(tokens_ref, gain_ref, out_ref, slab_ref):
+    core = lax.axis_index("c")
+    slab_ref[...] = tokens_ref[lax.axis_index("z") * 4 + lax.axis_index("y"), core]
+    for k in range(4):
+        floats = tokens_ref[4 * k : 4 * k + 4, core].astype(jnp.float32).reshape(64, D)
+        out_ref[64 * k : 64 * k + 64, :] = norm_scaled(floats, gain_ref[...]).astype(jnp.bfloat16)
+
+
+def norm_part(tokens, gain):
     return pl.pallas_call(
         norm_kernel,
-        grid_spec=pltpu.PrefetchScalarGridSpec(
-            num_scalar_prefetch=1,
-            grid=(2,),
-            in_specs=[
-                pl.BlockSpec((8, 1, 16, D), lambda i, core: (i, core[0], 0, 0)),
-                pl.BlockSpec((1, D), lambda i, core: (0, 0)),
-            ],
-            out_specs=pl.BlockSpec((128, D), lambda i, core: (i, 0)),
+        out_shape=(
+            jax.ShapeDtypeStruct((HALF, D), jnp.bfloat16),
+            jax.ShapeDtypeStruct((SLAB, D), jnp.bfloat16),
         ),
-        out_shape=jax.ShapeDtypeStruct((HALF, D), jnp.bfloat16),
-        compiler_params=LIMIT,
+        in_specs=[VMEM, VMEM],
+        out_specs=(VMEM, VMEM),
+        compiler_params=room(2),
+        cost_estimate=cost(1),
         name="norm",
-    )(core, tokens.reshape(16, 2, 16, D), gain.reshape(1, D))
-
-
-def project_kernel(core_ref, normed_ref, own_ref, other_ref, q_ref, kv_ref):
-    core = core_ref[0]
+    )(tokens.reshape(16, 2, 16, D), gain.reshape(1, D))
+
+
+def project_kernel(normed_ref, own_ref, other_ref, q_ref, kv_ref):
+    core = lax.axis_index("c")
     normed = normed_ref[...]
 
     def times(ref):
@@ -214,102 +207,124 @@
     kv_ref[192:256, :] = other[128:]
 
 
-def project_part(core, normed, own, other):
+def project_part(normed, own, other):
     return pl.pallas_call(
         project_kernel,
         out_shape=(
             jax.ShapeDtypeStruct((HD, HALF), jnp.bfloat16),
             jax.ShapeDtypeStruct((2 * HD, HALF), jnp.bfloat16),
         ),
-        in_specs=[SMEM, VMEM, VMEM, VMEM],
+        in_specs=[VMEM, VMEM, VMEM],
         out_specs=(VMEM, VMEM),
-        compiler_params=LIMIT,
+        compiler_params=room(2),
+        cost_estimate=cost(1),
         name="project",
-    )(core, normed, own, other)
-
-
-def attend_kernel(place_ref, mine_ref, received_ref, *rest):
+    )(normed, own, other)
+
+
+def attend_kernel(mine_ref, received_ref, *rest):
     outs, scratch = rest[:4], rest[4]
     raw = (mine_ref[...] + received_ref[...].astype(jnp.float32)) / HD
     scratch[...] = norm_scaled(raw, 1.0).reshape(4, 64, HD)
     for step, out in enumerate(outs):
-        at = pl.multiple_of(lax.rem(place_ref[1] + step, 4) * SLAB, SLAB)
+        at = pl.multiple_of(lax.rem(lax.axis_index("y") + step, 4) * SLAB, SLAB)
         out[...] = scratch[:, pl.ds(at, SLAB), :].reshape(64, HD).astype(jnp.bfloat16)
 
 
-def attend_part(place, mine, received):
+def attend_part(mine, received):
     return pl.pallas_call(
         attend_kernel,
         out_shape=(jax.ShapeDtypeStruct((64, HD), jnp.bfloat16),) * 4,
-        in_specs=[SMEM, VMEM, VMEM],
+        in_specs=[VMEM, VMEM],
         out_specs=(VMEM,) * 4,
         scratch_shapes=[pltpu.VMEM((4, 64, HD), jnp.float32)],
-        compiler_params=LIMIT,
+        compiler_params=room(2),
+        cost_estimate=cost(0.7),
         name="attend",
-    )(place, mine, received)
-
-
-def output_kernel(place_ref, *rest):
-    pieces, own, other, outs, scratch = rest[:4], rest[4:8], rest[8:12], rest[12:16], rest[16]
+    )(mine, received)
+
+
+def pack_kernel(*refs):
+    for step in range(4):
+        refs[4][64 * step : 64 * step + 64, :] = refs[step][...]
+
+
+def pack_part(rows):
+    return pl.pallas_call(
+        pack_kernel,
+        out_shape=jax.ShapeDtypeStruct((HALF, D), jnp.bfloat16),
+        in_specs=[VMEM] * 4,
+        out_specs=VMEM,
+        compiler_params=room(2),
+        cost_estimate=cost(0.5),
+        name="pack",
+    )(*rows)
+
+
+def output_kernel(*rest):
+    pieces, own, other, outs, scratch = rest[:4], rest[4], rest[5], rest[6:10], rest[10]
     loaded = [piece[...] for piece in pieces]
     for at in range(0, D, 512):
         total = jnp.zeros((64, 512), jnp.float32)
         for step in range(4):
             total = total + jnp.dot(
                 loaded[step][:, :64],
-                own[step][:, at : at + 512],
+                own[64 * step : 64 * step + 64, at : at + 512],
                 preferred_element_type=jnp.float32,
             )
             total = total + jnp.dot(
                 loaded[step][:, 64:],
-                other[step][:, at : at + 512],
+                other[64 * step : 64 * step + 64, at : at + 512],
                 preferred_element_type=jnp.float32,
             )
         scratch[:, at : at + 512] = total
     for step, out in enumerate(outs):
-        at = pl.multiple_of(lax.rem(place_ref[0] + step, 4) * SLAB, SLAB)
+        at = pl.multiple_of(lax.rem(lax.axis_index("z") + step, 4) * SLAB, SLAB)
         out[...] = scratch[pl.ds(at, SLAB), :].astype(out.dtype)
 
 
-def output_part(place, pieces, own, other):
+def output_part(pieces, own, other):
     return pl.pallas_call(
         output_kernel,
         out_shape=(jax.ShapeDtypeStruct((SLAB, D), jnp.float32),)
         + (jax.ShapeDtypeStruct((SLAB, D), jnp.bfloat16),) * 3,
-        in_specs=[SMEM] + [VMEM] * 12,
+        in_specs=[VMEM] * 6,
         out_specs=(VMEM,) * 4,
         scratch_shapes=[pltpu.VMEM((64, D), jnp.float32)],
-        compiler_params=LIMIT,
+        compiler_params=room(2),
+        cost_estimate=cost(2),
         name="output",
-    )(place, *pieces, *own, *other)
-
-
-def map_kernel(index_ref, rows_ref, lanes_ref):
+    )(*pieces, own, other)
+
+
+def map_kernel(index_ref, gain_ref, rows_ref, lanes_ref, gain_out):
+    gain_out[...] = gain_ref[...]
     index = index_ref[...]
-    expert = lax.broadcasted_iota(jnp.int32, (SLAB, EXPERTS), 1)
-    chosen = jnp.zeros((SLAB, EXPERTS), jnp.float32)
+    expert = lax.broadcasted_iota(jnp.int32, (EXPERTS, SLAB), 0)
+    chosen = jnp.zeros((EXPERTS, SLAB), jnp.float32)
     for k in range(TOP):
-        chosen = chosen + jnp.where(index[:, k : k + 1] == expert, 1.0, 0.0)
-    before = lax.broadcasted_iota(jnp.int32, (SLAB, SLAB), 0) > lax.broadcasted_iota(
+        chosen = chosen + jnp.where(index[k : k + 1, :] == expert, 1.0, 0.0)
+    before = lax.broadcasted_iota(jnp.int32, (SLAB, SLAB), 0) < lax.broadcasted_iota(
         jnp.int32, (SLAB, SLAB), 1
     )
     slot = jnp.dot(
+        chosen.astype(jnp.bfloat16),
         jnp.where(before, 1.0, 0.0).astype(jnp.bfloat16),
-        chosen.astype(jnp.bfloat16),
         preferred_element_type=jnp.float32,
     )
     code = jnp.where(chosen > 0.5, slot, -1.0).astype(jnp.bfloat16)
     lane = lax.broadcasted_iota(jnp.int32, (SLAB, TILE_ROWS), 1)
-    wide = jnp.dot(code, spread_map(), preferred_element_type=jnp.float32)
+    wide = lax.dot_general(
+        code, spread_map(), (((0,), (0,)), ((), ())), preferred_element_type=jnp.float32
+    )
     lanes_ref[...] = jnp.where(
         wide == ((lane // PIECES) % CAP).astype(jnp.float32), 1.0, 0.0
     )
     token = lax.broadcasted_iota(jnp.int32, (SLAB, 256), 0)
     column = lax.broadcasted_iota(jnp.int32, (SLAB, 256), 1)
-    by_column = lax.dot_general(
+    by_column = jnp.dot(
         code,
         jnp.where(column % SLAB == token, 1.0, 0.0).astype(jnp.bfloat16),
-        (((0,), (0,)), ((), ())),
         preferred_element_type=jnp.float32,
     ).astype(jnp.bfloat16)
     row_expert = lax.broadcasted_iota(jnp.int32, (TILE_ROWS, EXPERTS), 0) // (CAP * PIECES)
@@ -331,18 +346,20 @@
     ).astype(jnp.bfloat16)
 
 
-def map_part(index):
+def map_part(index, gain):
     return pl.pallas_call(
         map_kernel,
         out_shape=(
             jax.ShapeDtypeStruct((TILE_ROWS, 256), jnp.bfloat16),
             jax.ShapeDtypeStruct((SLAB, TILE_ROWS), jnp.float32),
+            jax.ShapeDtypeStruct((1, D), jnp.float32),
         ),
-        in_specs=[VMEM],
-        out_specs=(VMEM, VMEM),
-        compiler_params=LIMIT,
+        in_specs=[VMEM, VMEM],
+        out_specs=(VMEM,) * 3,
+        compiler_params=room(14),
+        cost_estimate=cost(2),
         name="maps",
-    )(index)
+    )(index, gain.reshape(1, D))
 
 
 def dispatch_kernel(slab_ref, own_ref, r1, r2, r3, gain_ref, router_ref, rows_ref, residual_ref, out_ref, gates_ref):
@@ -371,9 +388,10 @@
         ),
         in_specs=[VMEM] * 8,
         out_specs=(VMEM,) * 3,
-        compiler_params=LIMIT,
+        compiler_params=room(6),
+        cost_estimate=cost(1),
         name="dispatch",
-    )(slab, own, *received, gain.reshape(1, D), router, rows)
+    )(slab, own, *received, gain, router, rows)
 
 
 def gate_kernel(gates_ref, lanes_ref, out_ref):
@@ -394,7 +412,8 @@
         out_shape=jax.ShapeDtypeStruct((256, TILE_ROWS), jnp.bfloat16),
         in_specs=[VMEM, VMEM],
         out_specs=VMEM,
-        compiler_params=LIMIT,
+        compiler_params=room(8),
+        cost_estimate=cost(0.5),
         name="gates",
     )(gates, lanes)
 
@@ -456,7 +475,8 @@
             pltpu.SemaphoreType.DMA((2, 2)),
             pltpu.SemaphoreType.DMA((2,)),
         ],
-        compiler_params=LIMIT,
+        compiler_params=room(24),
+        cost_estimate=cost(6),
         name="experts",
     )(rows, first, second, first_other, second_other)
 
@@ -476,7 +496,8 @@
         out_shape=jax.ShapeDtypeStruct((SLAB, D), jnp.bfloat16),
         in_specs=[VMEM] * 3,
         out_specs=VMEM,
-        compiler_params=LIMIT,
+        compiler_params=room(4),
+        cost_estimate=cost(1),
         name="combine",
     )(residual, gates, rows)
 
@@ -500,31 +521,29 @@
     expert_first,
     expert_second,
 ):
-    z, y, c = (lax.axis_index(name) for name in ("z", "y", "c"))
-    place = scalars(z, y, c)
-    core = scalars(c)
     own_weights = head_weights.transpose(0, 2, 1)
     other_weights = swap_core(own_weights)
-    normed = norm_part(core, tokens, attention_gain)
-    q_own, kv = project_part(core, normed, own_weights, other_weights)
+    output_own = [output_weight] + [shift(output_weight, "y", step) for step in (1, 2, 3)]
+    normed, slab = norm_part(tokens, attention_gain)
+    q_own, kv = project_part(normed, own_weights, other_weights)
     kvs = [kv] + [shift(kv, "x", step) for step in (1, 2, 3)]
     q_other = swap_core(q_own)
-    later = lax.optimization_barrier((kv, output_weight, expert_first, expert_second))[1:]
-    output_own = [later[0]] + [shift(later[0], "y", step) for step in (1, 2, 3)]
-    output_other = [swap_core(rows) for rows in output_own]
-    first_other, second_other = swap_core(later[1]), swap_core(later[2])
-    rows_map, lanes_map = map_part(expert_index)
+    rows_map, lanes_map, gain = map_part(expert_index.T, expert_gain)
 
     carried = carried_part(carried_state.T, q_own, q_other)
-    x = lax.axis_index("x")
-    mine, send = window_part(scalars(c, x), q_own, q_other, kvs, carried)
-    pieces = attend_part(place, mine, swap_core(send))
+    mine, send = window_part(q_own, q_other, kvs, carried)
+    tied = lax.optimization_barrier((swap_core(send), *output_own))
+    received, output_own = tied[0], pack_part(tied[1:])
+    output_other = swap_core(output_own)
+    pieces = attend_part(mine, received)
     pieces = [pieces[0]] + [shift(pieces[step], "y", step) for step in (1, 2, 3)]
-    sums = output_part(place, pieces, output_own, output_other)
-    received = [shift(sums[step], "z", step) for step in (1, 2, 3)]
-    slab = lax.dynamic_slice_in_dim(tokens, ((z * 4 + y) * 2 + c) * SLAB, SLAB, 0)
+    sums = output_part(pieces, output_own, output_other)
+    tied = lax.optimization_barrier((*sums, expert_first, expert_second))
+    sums, first_given, second_given = tied[:4], tied[4], tied[5]
+    first_other, second_other = swap_core(first_given), swap_core(second_given)
+    summed = [shift(sums[step], "z", step) for step in (1, 2, 3)]
     residual, outgoing, gates = dispatch_part(
-        slab, sums[0], received, expert_gain, router_weight.T, rows_map
+        slab, sums[0], summed, gain, router_weight.T, rows_map
     )
     arrived = chips(outgoing)
     gate_map = gate_part(gates, lanes_map)

time: 119 us -> 93.3 us (0.78)
  waiting for transfers between devices: 31.2 us -> 21.3 us
  local copies, waits for them, and re-layouts: 13 us -> 5.09 us
  Pallas kernels: 23.2 us -> 16.9 us
    unnamed x37 -> x20, local copies, waits for them, and re-layouts: 12.1 us -> 5.09 us
    ppermute x9 -> x6, waiting for transfers between devices: 6.54 us -> 0.07 us  [swap_core(): return lax.ppermute(array, 'c', [(0, 1), (1, 0)])]
    ppermute x12, waiting for transfers between devices: 11.5 us -> 7.76 us  [shift(): return lax.ppermute(array, axis, [(i, (i + step) % 4) for i in range(4)])]
    pallas_call x1, Pallas kernels: 6.35 us -> 3.15 us  [carried_part(): pl.pallas_call(carried_kernel, out_shape=jax.ShapeDtypeStruct((64, SHARD)...]
    pallas_call x1, Pallas kernels: 2.55 us -> 0.75 us  [output_part(): pl.pallas_call(output_kernel, out_shape=(jax.ShapeDtypeStruct((SLAB, D),...]
  transfers between devices with their start and end apart: 22 -> 19, of which waited for: 10 -> 9; matrix products, arithmetic and copies ran while one was open for 1% -> 0% of each run, Pallas kernels for 13% -> 8%
where the time goes in v3:
time: 93.3 us; the launch traced here: 93 us
  starting transfers between devices  28 us (30%)
  blocking collectives  21.5 us (23%)
  waiting for transfers between devices  21.3 us (23%)
  Pallas kernels  16.9 us (18%)
  local copies, waits for them, and re-layouts  5.09 us (5%)
    ppermute x12, starting transfers between devices, shift(): return lax.ppermute(array, axis, [(i, (i + step) % 4) for i in range(4)])  22.6 us
    all_to_all x1, blocking collectives, chips(): lax.all_to_all(shaped, CHIP_AXES, split_axis=0, concat_axis=0, tiled=True)  21.5 us
    all_to_all x1, waiting for transfers between devices, chips(): lax.all_to_all(shaped, CHIP_AXES, split_axis=0, concat_axis=0, tiled=True)  13.5 us
    ppermute x12, waiting for transfers between devices, shift(): return lax.ppermute(array, axis, [(i, (i + step) % 4) for i in range(4)])  7.76 us
    pallas_call x1, Pallas kernels, expert_part(): pl.pallas_call(expert_kernel, out_shape=jax.ShapeDtypeStruct((TILE_ROWS,...  6.28 us
    unnamed x20, local copies, waits for them, and re-layouts  5.09 us
    all_to_all x1, starting transfers between devices, chips(): lax.all_to_all(shaped, CHIP_AXES, split_axis=0, concat_axis=0, tiled=True)  4.79 us
    pallas_call x1, Pallas kernels, carried_part(): pl.pallas_call(carried_kernel, out_shape=jax.ShapeDtypeStruct((64, SHARD)...  3.15 us
  transfers between devices with their start and end apart: 19, of which 9 were waited for; matrix products, arithmetic and copies ran while one was open for 0% of the time, Pallas kernels for 8%

profile of v3, /device:TPU:0, one launch (start us, length us, event | category | flops | bytes accessed | tf_op | source)
XLA Modules:
  0.0 93.0 jit_solution(9564095564984615899)
XLA Ops:
  0.0 0.0 collective-permute-start
  0.0 1.6 %copy-done.3 = bf16[512,2048]{1,0:T(8,128)(2,1)S(1)} copy-done((bf16[512,2048]{1,0:T(8,128)(2,1)S(1)}, bf16[512,2048]{1,0:T(8,128)(2,1)}, u32[]{:S(2)}) %copy-start.3) | copy-done | bytes 2097176
  1.6 0.7 copy-done.7
  2.3 0.4 norm.1
  2.7 0.0 copy-start
  2.7 0.0 copy-start.2
  2.7 0.0 collective-permute-done.other_ref
  2.7 0.7 copy-done.5
  3.4 0.8 project.1
  4.3 1.6 %collective-permute-start.2 = (bf16[256,256]{1,0:T(8,128)(2,1)S(1)}, bf16[256,256]{1,0:T(8,128)(2,1)S(1)}, u32[]{:S(2)}, u32[]{:S(2)}) collective-permute-start(bf16[256,256]{1,0:T(8,128)(2,1)S(1)} %get-tuple-element.39.kv0), channel_id=1, source_target_pairs={{0,32},{32,64},{64,96},{96,0},{1,33},{33,65},{65,97},{97,1},{2,34}... | collective-permute-start | bytes 393224 | tf_op jit(solution)/shard_map/ppermute | solution.py:28
  5.9 0.2 collective-permute-start.1
  6.1 0.0 copy-done
  6.1 1.6 %collective-permute-start.6 = (bf16[64,2048]{1,0:T(8,128)(2,1)S(1)}, bf16[64,2048]{1,0:T(8,128)(2,1)S(1)}, u32[]{:S(2)}, u32[]{:S(2)}) collective-permute-start(bf16[64,2048]{1,0:T(8,128)(2,1)S(1)} %copy-done), channel_id=1, source_target_pairs={{0,2},{2,4},{4,6},{6,0},{1,3},{3,5},{5,7},{7,1},{8,10},{10,12},{12... | collective-permute-start | bytes 786440 | tf_op jit(solution)/shard_map/ppermute | solution.py:28
  7.7 2.9 %collective-permute-start.7 = (bf16[64,2048]{1,0:T(8,128)(2,1)S(1)}, bf16[64,2048]{1,0:T(8,128)(2,1)S(1)}, u32[]{:S(2)}, u32[]{:S(2)}) collective-permute-start(bf16[64,2048]{1,0:T(8,128)(2,1)S(1)} %copy-done), channel_id=1, source_target_pairs={{0,4},{2,6},{4,0},{6,2},{1,5},{3,7},{5,1},{7,3},{8,12},{10,14},{12... | collective-permute-start | bytes 786440 | tf_op jit(solution)/shard_map/ppermute | solution.py:28
  10.6 1.3 %collective-permute-start.8 = (bf16[64,2048]{1,0:T(8,128)(2,1)S(1)}, bf16[64,2048]{1,0:T(8,128)(2,1)S(1)}, u32[]{:S(2)}, u32[]{:S(2)}) collective-permute-start(bf16[64,2048]{1,0:T(8,128)(2,1)S(1)} %copy-done), channel_id=1, source_target_pairs={{0,6},{2,0},{4,2},{6,4},{1,7},{3,1},{5,3},{7,5},{8,14},{10,8},{12,... | collective-permute-start | bytes 786440 | tf_op jit(solution)/shard_map/ppermute | solution.py:28
  12.0 0.0 collective-permute-done.1.q_other_ref
  12.0 2.7 %collective-permute-start.3 = (bf16[256,256]{1,0:T(8,128)(2,1)S(1)}, bf16[256,256]{1,0:T(8,128)(2,1)S(1)}, u32[]{:S(2)}, u32[]{:S(2)}) collective-permute-start(bf16[256,256]{1,0:T(8,128)(2,1)S(1)} %get-tuple-element.39.kv0), channel_id=1, source_target_pairs={{0,64},{32,96},{64,0},{96,32},{1,65},{33,97},{65,1},{97,33},{2,66}... | collective-permute-start | bytes 393224 | tf_op jit(solution)/shard_map/ppermute | solution.py:28
  14.7 0.0 collective-permute-done.2.kv1
  14.7 1.4 %collective-permute-start.4 = (bf16[256,256]{1,0:T(8,128)(2,1)S(1)}, bf16[256,256]{1,0:T(8,128)(2,1)S(1)}, u32[]{:S(2)}, u32[]{:S(2)}) collective-permute-start(bf16[256,256]{1,0:T(8,128)(2,1)S(1)} %get-tuple-element.39.kv0), channel_id=1, source_target_pairs={{0,96},{32,0},{64,32},{96,64},{1,97},{33,1},{65,33},{97,65},{2,98}... | collective-permute-start | bytes 393224 | tf_op jit(solution)/shard_map/ppermute | solution.py:28
  16.1 0.0 copy-done.2
  16.1 3.2 %carried.1.carried_ref = f32[64,512]{1,0:T(8,128)S(1)} custom-call(f32[64,8256]{1,0:T(8,128)S(1)} %bitcast.14, bf16[128,256]{1,0:T(8,128)(2,1)S(1)} %get-tuple-element.38.q_own_ref, bf16[128,256]{1,0:T(8,128)(2,1)S(1)} %collective-permute-done.1.q_other_ref), custom_call_target="tpu_custom_call" | custom-call | flops 5000000000 | bytes 15000000 | tf_op jit(solution)/shard_map/carried/pallas_call | solution.py:104
  19.3 0.0 collective-permute-done.3.kv2
  19.3 1.0 %collective-permute-done.4.kv3 = bf16[256,256]{1,0:T(8,128)(2,1)S(1)} collective-permute-done((bf16[256,256]{1,0:T(8,128)(2,1)S(1)}, bf16[256,256]{1,0:T(8,128)(2,1)S(1)}, u32[]{:S(2)}, u32[]{:S(2)}) %collective-permute-start.4) | collective-permute-done | bytes 131104 | tf_op jit(solution)/shard_map/ppermute | solution.py:28
  20.3 1.1 %window.1 = (f32[256,128]{1,0:T(8,128)S(1)}, bf16[256,128]{1,0:T(8,128)(2,1)S(1)}) custom-call(bf16[128,256]{1,0:T(8,128)(2,1)S(1)} %get-tuple-element.38.q_own_ref, bf16[128,256]{1,0:T(8,128)(2,1)S(1)} %collective-permute-done.1.q_other_ref, bf16[256,256]{1,0:T(8,128)(2,1)S(1)} %get-tuple-element.39.kv0, bf16[256,256]{1,0:T(8,128)(2,1)S(1)} %collective-permute-done.2.kv1, ...), custom_call_target="tpu_custom_call" | custom-call | flops 2000000000 | bytes 6000000 | tf_op jit(solution)/shard_map/window/pallas_call | solution.py:150
  21.4 0.1 collective-permute-start.5
  21.5 0.0 collective-permute-done.6.refs_1_
  21.5 1.2 %collective-permute-done.7.refs_2_ = bf16[64,2048]{1,0:T(8,128)(2,1)S(1)} collective-permute-done((bf16[64,2048]{1,0:T(8,128)(2,1)S(1)}, bf16[64,2048]{1,0:T(8,128)(2,1)S(1)}, u32[]{:S(2)}, u32[]{:S(2)}) %collective-permute-start.7) | collective-permute-done | bytes 262176 | tf_op jit(solution)/shard_map/ppermute | solution.py:28
  22.7 0.0 collective-permute-done.8.refs_3_
  22.7 0.1 collective-permute-done.5.received_ref
  22.8 0.1 pack.1.rest_4_
  22.8 0.2 collective-permute-start.12
  23.1 0.1 attend.1
  23.2 2.5 %collective-permute-start.10 = (bf16[64,128]{1,0:T(8,128)(2,1)S(1)}, bf16[64,128]{1,0:T(8,128)(2,1)S(1)}, u32[]{:S(2)}, u32[]{:S(2)}) collective-permute-start(bf16[64,128]{1,0:T(8,128)(2,1)S(1)} %get-tuple-element.45), channel_id=1, source_target_pairs={{0,4},{2,6},{4,0},{6,2},{1,5},{3,7},{5,1},{7,3},{8,12},{10,14},{12... | collective-permute-start | bytes 49160 | tf_op jit(solution)/shard_map/ppermute | solution.py:28
  25.7 1.2 %collective-permute-start.11 = (bf16[64,128]{1,0:T(8,128)(2,1)S(1)}, bf16[64,128]{1,0:T(8,128)(2,1)S(1)}, u32[]{:S(2)}, u32[]{:S(2)}) collective-permute-start(bf16[64,128]{1,0:T(8,128)(2,1)S(1)} %get-tuple-element.46), channel_id=1, source_target_pairs={{0,6},{2,0},{4,2},{6,4},{1,7},{3,1},{5,3},{7,5},{8,14},{10,8},{12,... | collective-permute-start | bytes 49160 | tf_op jit(solution)/shard_map/ppermute | solution.py:28
  26.9 0.8 collective-permute-start.9
  27.7 0.8 collective-permute-done.10.rest_2_
  28.5 0.9 collective-permute-done.11.rest_3_
  29.4 2.4 %collective-permute-done.9.rest_1_ = bf16[64,128]{1,0:T(8,128)(2,1)S(1)} collective-permute-done((bf16[64,128]{1,0:T(8,128)(2,1)S(1)}, bf16[64,128]{1,0:T(8,128)(2,1)S(1)}, u32[]{:S(2)}, u32[]{:S(2)}) %collective-permute-start.9) | collective-permute-done | bytes 16416 | tf_op jit(solution)/shard_map/ppermute | solution.py:28
  31.9 0.0 collective-permute-done.12.rest_5_
  31.9 0.0 copy-start.9
  31.9 0.7 output.1
  32.6 1.4 %copy-done.1 = bf16[2,2048,512]{2,1,0:T(8,128)(2,1)S(1)} copy-done((bf16[2,2048,512]{2,1,0:T(8,128)(2,1)S(1)}, bf16[2,2048,512]{2,1,0:T(8,128)(2,1)}, u32[]{:S(2)}) %copy-start.1) | copy-done | bytes 4194328
  34.1 0.0 collective-permute-start.16
  34.1 0.7 copy-done.4
  34.7 0.0 collective-permute-start.17
  34.7 1.9 %collective-permute-start.13 = (bf16[16,2048]{1,0:T(8,128)(2,1)S(1)}, bf16[16,2048]{1,0:T(8,128)(2,1)S(1)}, u32[]{:S(2)}, u32[]{:S(2)}) collective-permute-start(bf16[16,2048]{1,0:T(8,128)(2,1)S(1)} %get-tuple-element.56), channel_id=1, source_target_pairs={{0,8},{8,16},{16,24},{24,0},{1,9},{9,17},{17,25},{25,1},{2,10},{10... | collective-permute-start | bytes 196616 | tf_op jit(solution)/shard_map/ppermute | solution.py:28
  36.7 3.6 %collective-permute-start.14 = (bf16[16,2048]{1,0:T(8,128)(2,1)S(1)}, bf16[16,2048]{1,0:T(8,128)(2,1)S(1)}, u32[]{:S(2)}, u32[]{:S(2)}) collective-permute-start(bf16[16,2048]{1,0:T(8,128)(2,1)S(1)} %get-tuple-element.57), channel_id=1, source_target_pairs={{0,16},{8,24},{16,0},{24,8},{1,17},{9,25},{17,1},{25,9},{2,18},{10... | collective-permute-start | bytes 196616 | tf_op jit(solution)/shard_map/ppermute | solution.py:28
  40.2 1.0 %collective-permute-start.15 = (bf16[16,2048]{1,0:T(8,128)(2,1)S(1)}, bf16[16,2048]{1,0:T(8,128)(2,1)S(1)}, u32[]{:S(2)}, u32[]{:S(2)}) collective-permute-start(bf16[16,2048]{1,0:T(8,128)(2,1)S(1)} %get-tuple-element.58), channel_id=1, source_target_pairs={{0,24},{8,0},{16,8},{24,16},{1,25},{9,1},{17,9},{25,17},{2,26},{10... | collective-permute-start | bytes 196616 | tf_op jit(solution)/shard_map/ppermute | solution.py:28
  41.2 0.0 copy-done.8
  41.3 0.0 copy-done.9
  41.3 1.8 %maps.1 = (bf16[3072,256]{1,0:T(8,128)(2,1)S(1)}, f32[16,3072]{1,0:T(8,128)S(1)}, f32[1,2048]{1,0:T(1,128)S(1)}) custom-call(s32[8,16]{1,0:T(8,128)S(1)} %bitcast.21, f32[1,2048]{1,0:T(1,128)S(1)} %bitcast.20), custom_call_target="tpu_custom_call" | custom-call | flops 2000000000 | bytes 6000000 | tf_op jit(solution)/shard_map/maps/pallas_call | solution.py:350
  43.1 0.0 collective-permute-done.13.r1
  43.1 1.0 %collective-permute-done.14.r2 = bf16[16,2048]{1,0:T(8,128)(2,1)S(1)} collective-permute-done((bf16[16,2048]{1,0:T(8,128)(2,1)S(1)}, bf16[16,2048]{1,0:T(8,128)(2,1)S(1)}, u32[]{:S(2)}, u32[]{:S(2)}) %collective-permute-start.14) | collective-permute-done | bytes 65568 | tf_op jit(solution)/shard_map/ppermute | solution.py:28
  44.1 0.4 collective-permute-done.15.r3
  44.5 0.0 copy-done.6
  44.5 0.8 dispatch.1
  45.3 21.5 %all_to_all.10 = bf16[64,48,128]{2,1,0:T(8,128)(2,1)S(1)} all-to-all(bf16[64,48,128]{2,1,0:T(8,128)(2,1)S(1)} %bitcast.12), channel_id=1, replica_groups=mesh['x'=4,'z'=4,'y'=4,'c'=2] {'x','z','y'}, dimensions={0} | all-to-all | bytes 1572864 | tf_op jit(solution)/shard_map/all_to_all | solution.py:507
  66.8 0.0 collective-permute-done.17.second_other
  66.8 0.0 collective-permute-done.16.first_other
  66.8 6.3 %experts.1 = bf16[3072,128]{1,0:T(8,128)(2,1)} custom-call(bf16[3072,128]{1,0:T(8,128)(2,1)S(1)} %bitcast.13, bf16[2,2048,512]{2,1,0:T(8,128)(2,1)S(1)} %copy-done.1, bf16[512,2048]{1,0:T(8,128)(2,1)S(1)} %copy-done.4, bf16[2,2048,512]{2,1,0:T(8,128)(2,1)S(1)} %collective-permute-done.16.first_other, bf16[512,2048]{1,0:T(8,128)(2,1)S(1)} %collective-permute-done.17.second_other), custom_call_target="tpu_custom_call" | custom-call | flops 6000000000 | bytes 18000000 | tf_op jit(solution)/shard_map/experts/pallas_call | solution.py:464
  73.1 4.8 %all-to-all-start.1 = ((bf16[64,48,128]{2,1,0:T(8,128)(2,1)}), bf16[64,48,128]{2,1,0:T(8,128)(2,1)S(1)}, u32[]{:S(2)}, u32[]{:S(2)}) async-start(bf16[64,48,128]{2,1,0:T(8,128)(2,1)} %bitcast.9), calls=%async_computation.1 | async-start | bytes 1572864 | tf_op jit(solution)/shard_map/all_to_all | solution.py:507
  77.9 0.4 gates.1.gates_ref
  78.3 13.5 %all-to-all-done.1 = bf16[64,48,128]{2,1,0:T(8,128)(2,1)S(1)} async-done(((bf16[64,48,128]{2,1,0:T(8,128)(2,1)}), bf16[64,48,128]{2,1,0:T(8,128)(2,1)S(1)}, u32[]{:S(2)}, u32[]{:S(2)}) %all-to-all-start.1) | async-done | bytes 786464 | tf_op jit(solution)/shard_map/all_to_all | solution.py:507
  91.8 1.2 %combine.1 = bf16[16,2048]{1,0:T(8,128)(2,1)} custom-call(f32[16,2048]{1,0:T(8,128)S(1)} %get-tuple-element.61.residual_ref, bf16[256,3072]{1,0:T(8,128)(2,1)S(1)} %gates.1.gates_ref, bf16[3072,128]{1,0:T(8,128)(2,1)S(1)} %bitcast.11), custom_call_target="tpu_custom_call" | custom-call | flops 1000000000 | bytes 3000000 | tf_op jit(solution)/shard_map/combine/pallas_call | solution.py:494
  (7 shorter events, 0.0 us)
Async XLA Ops:
  0.0 2.7 %collective-permute-start = (bf16[3,64,2048]{2,1,0:T(8,128)(2,1)}, bf16[3,64,2048]{2,1,0:T(8,128)(2,1)S(1)}, u32[]{:S(2)}, u32[]{:S(2)}) collective-permute-start(bf16[3,64,2048]{2,1,0:T(8,128)(2,1)} %bitcast.16), channel_id=1, source_target_pairs={{0,1},{1,0},{2,3},{3,2},{4,5},{5,4},{6,7},{7,6},{8,9},{9,8},{10,11... | collective-permute-start | bytes 2359304 | tf_op jit(solution)/shard_map/ppermute | solution.py:24
  0.0 1.6 %copy-start.3 = (bf16[512,2048]{1,0:T(8,128)(2,1)S(1)}, bf16[512,2048]{1,0:T(8,128)(2,1)}, u32[]{:S(2)}) copy-start(bf16[512,2048]{1,0:T(8,128)(2,1)} %param.10) | copy-start | bytes 6291460
  1.6 0.7 copy-start.7
  2.3 1.1 %copy-start.5 = (bf16[3,2048,64]{1,2,0:T(8,128)(2,1)S(1)}, bf16[3,2048,64]{1,2,0:T(8,128)(2,1)}, u32[]{:S(2)}) copy-start(bf16[3,2048,64]{1,2,0:T(8,128)(2,1)} %param.12) | copy-start | bytes 2359300
  2.7 3.4 %copy-start = (bf16[64,2048]{1,0:T(8,128)(2,1)S(1)}, bf16[64,2048]{1,0:T(8,128)(2,1)}, u32[]{:S(2)}) copy-start(bf16[64,2048]{1,0:T(8,128)(2,1)} %refs_0_) | copy-start | bytes 786436
  2.7 13.4 %copy-start.2 = (f32[8256,64]{0,1:T(8,128)S(1)}, f32[8256,64]{0,1:T(8,128)}, u32[]{:S(2)}) copy-start(f32[8256,64]{0,1:T(8,128)} %param.13) | copy-start | bytes 6340612
  4.3 10.4 %collective-permute-start.2 = (bf16[256,256]{1,0:T(8,128)(2,1)S(1)}, bf16[256,256]{1,0:T(8,128)(2,1)S(1)}, u32[]{:S(2)}, u32[]{:S(2)}) collective-permute-start(bf16[256,256]{1,0:T(8,128)(2,1)S(1)} %get-tuple-element.39.kv0), channel_id=1, source_target_pairs={{0,32},{32,64},{64,96},{96,0},{1,33},{33,65},{65,97},{97,1},{2,34}... | collective-permute-start | bytes 393224 | tf_op jit(solution)/shard_map/ppermute | solution.py:28
  5.9 6.1 %collective-permute-start.1 = (bf16[128,256]{1,0:T(8,128)(2,1)S(1)}, bf16[128,256]{1,0:T(8,128)(2,1)S(1)}, u32[]{:S(2)}, u32[]{:S(2)}) collective-permute-start(bf16[128,256]{1,0:T(8,128)(2,1)S(1)} %get-tuple-element.38.q_own_ref), channel_id=1, source_target_pairs={{0,1},{1,0},{2,3},{3,2},{4,5},{5,4},{6,7},{7,6},{8,9},{9,8},{10,11... | collective-permute-start | bytes 196616 | tf_op jit(solution)/shard_map/ppermute | solution.py:24
  6.1 15.4 %collective-permute-start.6 = (bf16[64,2048]{1,0:T(8,128)(2,1)S(1)}, bf16[64,2048]{1,0:T(8,128)(2,1)S(1)}, u32[]{:S(2)}, u32[]{:S(2)}) collective-permute-start(bf16[64,2048]{1,0:T(8,128)(2,1)S(1)} %copy-done), channel_id=1, source_target_pairs={{0,2},{2,4},{4,6},{6,0},{1,3},{3,5},{5,7},{7,1},{8,10},{10,12},{12... | collective-permute-start | bytes 786440 | tf_op jit(solution)/shard_map/ppermute | solution.py:28
  7.7 15.0 %collective-permute-start.7 = (bf16[64,2048]{1,0:T(8,128)(2,1)S(1)}, bf16[64,2048]{1,0:T(8,128)(2,1)S(1)}, u32[]{:S(2)}, u32[]{:S(2)}) collective-permute-start(bf16[64,2048]{1,0:T(8,128)(2,1)S(1)} %copy-done), channel_id=1, source_target_pairs={{0,4},{2,6},{4,0},{6,2},{1,5},{3,7},{5,1},{7,3},{8,12},{10,14},{12... | collective-permute-start | bytes 786440 | tf_op jit(solution)/shard_map/ppermute | solution.py:28
  10.6 12.1 %collective-permute-start.8 = (bf16[64,2048]{1,0:T(8,128)(2,1)S(1)}, bf16[64,2048]{1,0:T(8,128)(2,1)S(1)}, u32[]{:S(2)}, u32[]{:S(2)}) collective-permute-start(bf16[64,2048]{1,0:T(8,128)(2,1)S(1)} %copy-done), channel_id=1, source_target_pairs={{0,6},{2,0},{4,2},{6,4},{1,7},{3,1},{5,3},{7,5},{8,14},{10,8},{12,... | collective-permute-start | bytes 786440 | tf_op jit(solution)/shard_map/ppermute | solution.py:28
  12.0 7.3 %collective-permute-start.3 = (bf16[256,256]{1,0:T(8,128)(2,1)S(1)}, bf16[256,256]{1,0:T(8,128)(2,1)S(1)}, u32[]{:S(2)}, u32[]{:S(2)}) collective-permute-start(bf16[256,256]{1,0:T(8,128)(2,1)S(1)} %get-tuple-element.39.kv0), channel_id=1, source_target_pairs={{0,64},{32,96},{64,0},{96,32},{1,65},{33,97},{65,1},{97,33},{2,66}... | collective-permute-start | bytes 393224 | tf_op jit(solution)/shard_map/ppermute | solution.py:28
  14.7 5.6 %collective-permute-start.4 = (bf16[256,256]{1,0:T(8,128)(2,1)S(1)}, bf16[256,256]{1,0:T(8,128)(2,1)S(1)}, u32[]{:S(2)}, u32[]{:S(2)}) collective-permute-start(bf16[256,256]{1,0:T(8,128)(2,1)S(1)} %get-tuple-element.39.kv0), channel_id=1, source_target_pairs={{0,96},{32,0},{64,32},{96,64},{1,97},{33,1},{65,33},{97,65},{2,98}... | collective-permute-start | bytes 393224 | tf_op jit(solution)/shard_map/ppermute | solution.py:28
  21.4 1.3 %collective-permute-start.5 = (bf16[256,128]{1,0:T(8,128)(2,1)S(1)}, bf16[256,128]{1,0:T(8,128)(2,1)S(1)}, u32[]{:S(2)}, u32[]{:S(2)}) collective-permute-start(bf16[256,128]{1,0:T(8,128)(2,1)S(1)} %get-tuple-element.41), channel_id=1, source_target_pairs={{0,1},{1,0},{2,3},{3,2},{4,5},{5,4},{6,7},{7,6},{8,9},{9,8},{10,11... | collective-permute-start | bytes 196616 | tf_op jit(solution)/shard_map/ppermute | solution.py:24
  22.8 9.0 %collective-permute-start.12 = (bf16[256,2048]{1,0:T(8,128)(2,1)S(1)}, bf16[256,2048]{1,0:T(8,128)(2,1)S(1)}, u32[]{:S(2)}, u32[]{:S(2)}) collective-permute-start(bf16[256,2048]{1,0:T(8,128)(2,1)S(1)} %pack.1.rest_4_), channel_id=1, source_target_pairs={{0,1},{1,0},{2,3},{3,2},{4,5},{5,4},{6,7},{7,6},{8,9},{9,8},{10,11... | collective-permute-start | bytes 3145736 | tf_op jit(solution)/shard_map/ppermute | solution.py:24
  23.2 5.3 %collective-permute-start.10 = (bf16[64,128]{1,0:T(8,128)(2,1)S(1)}, bf16[64,128]{1,0:T(8,128)(2,1)S(1)}, u32[]{:S(2)}, u32[]{:S(2)}) collective-permute-start(bf16[64,128]{1,0:T(8,128)(2,1)S(1)} %get-tuple-element.45), channel_id=1, source_target_pairs={{0,4},{2,6},{4,0},{6,2},{1,5},{3,7},{5,1},{7,3},{8,12},{10,14},{12... | collective-permute-start | bytes 49160 | tf_op jit(solution)/shard_map/ppermute | solution.py:28
  25.7 3.7 %collective-permute-start.11 = (bf16[64,128]{1,0:T(8,128)(2,1)S(1)}, bf16[64,128]{1,0:T(8,128)(2,1)S(1)}, u32[]{:S(2)}, u32[]{:S(2)}) collective-permute-start(bf16[64,128]{1,0:T(8,128)(2,1)S(1)} %get-tuple-element.46), channel_id=1, source_target_pairs={{0,6},{2,0},{4,2},{6,4},{1,7},{3,1},{5,3},{7,5},{8,14},{10,8},{12,... | collective-permute-start | bytes 49160 | tf_op jit(solution)/shard_map/ppermute | solution.py:28
  26.9 4.9 %collective-permute-start.9 = (bf16[64,128]{1,0:T(8,128)(2,1)S(1)}, bf16[64,128]{1,0:T(8,128)(2,1)S(1)}, u32[]{:S(2)}, u32[]{:S(2)}) collective-permute-start(bf16[64,128]{1,0:T(8,128)(2,1)S(1)} %get-tuple-element.44), channel_id=1, source_target_pairs={{0,2},{2,4},{4,6},{6,0},{1,3},{3,5},{5,7},{7,1},{8,10},{10,12},{12... | collective-permute-start | bytes 49160 | tf_op jit(solution)/shard_map/ppermute | solution.py:28
  31.9 2.2 %copy-start.1 = (bf16[2,2048,512]{2,1,0:T(8,128)(2,1)S(1)}, bf16[2,2048,512]{2,1,0:T(8,128)(2,1)}, u32[]{:S(2)}) copy-start(bf16[2,2048,512]{2,1,0:T(8,128)(2,1)} %first_own.1) | copy-start | bytes 12582916
  31.9 2.9 %copy-start.4 = (bf16[512,2048]{1,0:T(8,128)(2,1)S(1)}, bf16[512,2048]{1,0:T(8,128)(2,1)}, u32[]{:S(2)}) copy-start(bf16[512,2048]{1,0:T(8,128)(2,1)} %second_own.1) | copy-start | bytes 6291460
  31.9 9.4 %copy-start.8 = (f32[2048]{0:T(1024)S(1)}, f32[2048]{0:T(1024)}, u32[]{:S(2)}) copy-start(f32[2048]{0:T(1024)} %param.15) | copy-start | bytes 24580
  31.9 9.4 %copy-start.9 = (s32[16,8]{0,1:T(8,128)S(1)}, s32[16,8]{0,1:T(8,128)}, u32[]{:S(2)}) copy-start(s32[16,8]{0,1:T(8,128)} %param.17) | copy-start | bytes 1540
  34.1 32.7 %collective-permute-start.16 = (bf16[2,2048,512]{2,1,0:T(8,128)(2,1)S(1)}, bf16[2,2048,512]{2,1,0:T(8,128)(2,1)S(1)}, u32[]{:S(2)}, u32[]{:S(2)}) collective-permute-start(bf16[2,2048,512]{2,1,0:T(8,128)(2,1)S(1)} %copy-done.1), channel_id=1, source_target_pairs={{0,1},{1,0},{2,3},{3,2},{4,5},{5,4},{6,7},{7,6},{8,9},{9,8},{10,11... | collective-permute-start | bytes 12582920 | tf_op jit(solution)/shard_map/ppermute | solution.py:24
  34.7 32.0 %collective-permute-start.17 = (bf16[512,2048]{1,0:T(8,128)(2,1)S(1)}, bf16[512,2048]{1,0:T(8,128)(2,1)S(1)}, u32[]{:S(2)}, u32[]{:S(2)}) collective-permute-start(bf16[512,2048]{1,0:T(8,128)(2,1)S(1)} %copy-done.4), channel_id=1, source_target_pairs={{0,1},{1,0},{2,3},{3,2},{4,5},{5,4},{6,7},{7,6},{8,9},{9,8},{10,11... | collective-permute-start | bytes 6291464 | tf_op jit(solution)/shard_map/ppermute | solution.py:24
  34.7 8.4 %collective-permute-start.13 = (bf16[16,2048]{1,0:T(8,128)(2,1)S(1)}, bf16[16,2048]{1,0:T(8,128)(2,1)S(1)}, u32[]{:S(2)}, u32[]{:S(2)}) collective-permute-start(bf16[16,2048]{1,0:T(8,128)(2,1)S(1)} %get-tuple-element.56), channel_id=1, source_target_pairs={{0,8},{8,16},{16,24},{24,0},{1,9},{9,17},{17,25},{25,1},{2,10},{10... | collective-permute-start | bytes 196616 | tf_op jit(solution)/shard_map/ppermute | solution.py:28
  36.7 7.5 %collective-permute-start.14 = (bf16[16,2048]{1,0:T(8,128)(2,1)S(1)}, bf16[16,2048]{1,0:T(8,128)(2,1)S(1)}, u32[]{:S(2)}, u32[]{:S(2)}) collective-permute-start(bf16[16,2048]{1,0:T(8,128)(2,1)S(1)} %get-tuple-element.57), channel_id=1, source_target_pairs={{0,16},{8,24},{16,0},{24,8},{1,17},{9,25},{17,1},{25,9},{2,18},{10... | collective-permute-start | bytes 196616 | tf_op jit(solution)/shard_map/ppermute | solution.py:28
  40.2 4.3 %collective-permute-start.15 = (bf16[16,2048]{1,0:T(8,128)(2,1)S(1)}, bf16[16,2048]{1,0:T(8,128)(2,1)S(1)}, u32[]{:S(2)}, u32[]{:S(2)}) collective-permute-start(bf16[16,2048]{1,0:T(8,128)(2,1)S(1)} %get-tuple-element.58), channel_id=1, source_target_pairs={{0,24},{8,0},{16,8},{24,16},{1,25},{9,1},{17,9},{25,17},{2,26},{10... | collective-permute-start | bytes 196616 | tf_op jit(solution)/shard_map/ppermute | solution.py:28
  41.3 3.3 %copy-start.6 = (bf16[2048,64]{0,1:T(8,128)(2,1)S(1)}, bf16[2048,64]{0,1:T(8,128)(2,1)}, u32[]{:S(2)}) copy-start(bf16[2048,64]{0,1:T(8,128)(2,1)} %param.16) | copy-start | bytes 786436
  73.1 18.7 %all-to-all-start.1 = ((bf16[64,48,128]{2,1,0:T(8,128)(2,1)}), bf16[64,48,128]{2,1,0:T(8,128)(2,1)S(1)}, u32[]{:S(2)}, u32[]{:S(2)}) async-start(bf16[64,48,128]{2,1,0:T(8,128)(2,1)} %bitcast.9), calls=%async_computation.1 | async-start | bytes 1572864 | tf_op jit(solution)/shard_map/all_to_all | solution.py:507

commit v4 on v3

--- a/solution.py
+++ b/solution.py
@@ -419,64 +419,42 @@
 
 
 def expert_kernel(
-    rows_ref, first_own, second_own, first_other, second_other, out_ref,
-    first_ref, second_ref, flat_ref, input_ref, total_ref, first_sem, second_sem,
+    rows_ref, first_own, second_own, first_other, second_other, out_ref, flat_ref, input_ref, total_ref
 ):
-    sources = ((first_own, second_own), (first_other, second_other))
-    copies = []
-    for piece, (first, second) in enumerate(sources):
-        for part in range(2):
-            copies.append(
-                pltpu.make_async_copy(
-                    first.at[part], first_ref.at[piece, part], first_sem.at[piece, part]
-                )
-            )
-        copies.append(
-            pltpu.make_async_copy(second, second_ref.at[piece], second_sem.at[piece])
-        )
-    for copy in copies:
-        copy.start()
     flat_ref[...] = rows_ref[...].astype(jnp.float32)
     for at in range(PIECES):
         input_ref[:, at * 128 : (at + 1) * 128] = flat_ref[
             pl.ds(at, ROWS, stride=PIECES), :
         ].astype(jnp.bfloat16)
-    for piece in range(2):
-        copies[3 * piece].wait()
-        gate = jnp.dot(input_ref[...], first_ref[piece, 0], preferred_element_type=jnp.float32)
-        copies[3 * piece + 1].wait()
-        up = jnp.dot(input_ref[...], first_ref[piece, 1], preferred_element_type=jnp.float32)
+    for piece, (first, second) in enumerate(
+        ((first_own, second_own), (first_other, second_other))
+    ):
+        gate = jnp.dot(input_ref[...], first[0], preferred_element_type=jnp.float32)
+        up = jnp.dot(input_ref[...], first[1], preferred_element_type=jnp.float32)
         hidden = (gate / (1.0 + jnp.exp(-gate)) * up).astype(jnp.bfloat16)
-        copies[3 * piece + 2].wait()
-        product = jnp.dot(hidden, second_ref[piece], preferred_element_type=jnp.float32)
+        product = jnp.dot(hidden, second[...], preferred_element_type=jnp.float32)
         if piece == 0:
             total_ref[...] = product
         else:
-            total_ref[...] += product
-    for at in range(PIECES):
-        flat_ref[pl.ds(at, ROWS, stride=PIECES), :] = total_ref[:, at * 128 : (at + 1) * 128]
+            product = product + total_ref[...]
+            for at in range(PIECES):
+                flat_ref[pl.ds(at, ROWS, stride=PIECES), :] = product[:, at * 128 : (at + 1) * 128]
     out_ref[...] = flat_ref[...].astype(jnp.bfloat16)
 
 
 def expert_part(rows, first, second, first_other, second_other):
-    anywhere = pl.BlockSpec(memory_space=pl.ANY)
-    width = second.shape[0]
     return pl.pallas_call(
         expert_kernel,
         out_shape=jax.ShapeDtypeStruct((TILE_ROWS, 128), jnp.bfloat16),
-        in_specs=[VMEM] + [anywhere] * 4,
+        in_specs=[VMEM] * 5,
         out_specs=VMEM,
         scratch_shapes=[
-            pltpu.VMEM((2, 2, D, width), jnp.bfloat16),
-            pltpu.VMEM((2, width, D), jnp.bfloat16),
             pltpu.VMEM((TILE_ROWS, 128), jnp.float32),
             pltpu.VMEM((ROWS, D), jnp.bfloat16),
             pltpu.VMEM((ROWS, D), jnp.float32),
-            pltpu.SemaphoreType.DMA((2, 2)),
-            pltpu.SemaphoreType.DMA((2,)),
         ],
-        compiler_params=room(24),
-        cost_estimate=cost(6),
+        compiler_params=room(28),
+        cost_estimate=cost(5),
         name="experts",
     )(rows, first, second, first_other, second_other)
 
@@ -532,15 +510,13 @@
 
     carried = carried_part(carried_state.T, q_own, q_other)
     mine, send = window_part(q_own, q_other, kvs, carried)
-    tied = lax.optimization_barrier((swap_core(send), *output_own))
-    received, output_own = tied[0], pack_part(tied[1:])
+    tied = lax.optimization_barrier((swap_core(send), expert_first, expert_second, *output_own))
+    received, output_own = tied[0], pack_part(tied[3:])
+    first_other, second_other = swap_core(tied[1]), swap_core(tied[2])
     output_other = swap_core(output_own)
     pieces = attend_part(mine, received)
     pieces = [pieces[0]] + [shift(pieces[step], "y", step) for step in (1, 2, 3)]
     sums = output_part(pieces, output_own, output_other)
-    tied = lax.optimization_barrier((*sums, expert_first, expert_second))
-    sums, first_given, second_given = tied[:4], tied[4], tied[5]
-    first_other, second_other = swap_core(first_given), swap_core(second_given)
     summed = [shift(sums[step], "z", step) for step in (1, 2, 3)]
     residual, outgoing, gates = dispatch_part(
         slab, sums[0], summed, gain, router_weight.T, rows_map

time: 93.3 us -> 89.9 us (0.964)
  local copies, waits for them, and re-layouts: 5.09 us -> 3.01 us
  Pallas kernels: 16.9 us -> 15.2 us
    unnamed x20, local copies, waits for them, and re-layouts: 5.09 us -> 3.01 us
    pallas_call x1, Pallas kernels: 6.28 us -> 4.52 us  [expert_part(): pl.pallas_call(expert_kernel, out_shape=jax.ShapeDtypeStruct((TILE_ROWS,...]
    ppermute x12, waiting for transfers between devices: 7.76 us -> 9.08 us  [shift(): return lax.ppermute(array, axis, [(i, (i + step) % 4) for i in range(4)])]
  transfers between devices with their start and end apart: 19 -> 19, of which waited for: 9 -> 8; matrix products, arithmetic and copies ran while one was open for 0% -> 0% of each run, Pallas kernels for 8% -> 10%
where the time goes in v4:
time: 89.9 us; the launch traced here: 89.6 us
  starting transfers between devices  28.8 us (32%)
  waiting for transfers between devices  21.8 us (24%)
  blocking collectives  20.6 us (23%)
  Pallas kernels  15.2 us (17%)
  local copies, waits for them, and re-layouts  3.01 us (3%)
    ppermute x12, starting transfers between devices, shift(): return lax.ppermute(array, axis, [(i, (i + step) % 4) for i in range(4)])  23 us
    all_to_all x1, blocking collectives, chips(): lax.all_to_all(shaped, CHIP_AXES, split_axis=0, concat_axis=0, tiled=True)  20.6 us
    all_to_all x1, waiting for transfers between devices, chips(): lax.all_to_all(shaped, CHIP_AXES, split_axis=0, concat_axis=0, tiled=True)  12.6 us
    ppermute x12, waiting for transfers between devices, shift(): return lax.ppermute(array, axis, [(i, (i + step) % 4) for i in range(4)])  9.08 us
    all_to_all x1, starting transfers between devices, chips(): lax.all_to_all(shaped, CHIP_AXES, split_axis=0, concat_axis=0, tiled=True)  4.77 us
    pallas_call x1, Pallas kernels, expert_part(): pl.pallas_call(expert_kernel, out_shape=jax.ShapeDtypeStruct((TILE_ROWS,...  4.52 us
    pallas_call x1, Pallas kernels, carried_part(): pl.pallas_call(carried_kernel, out_shape=jax.ShapeDtypeStruct((64, SHARD)...  3.15 us
    unnamed x20, local copies, waits for them, and re-layouts  3.01 us
  transfers between devices with their start and end apart: 19, of which 8 were waited for; matrix products, arithmetic and copies ran while one was open for 0% of the time, Pallas kernels for 10%

profile of v4, /device:TPU:0, one launch (start us, length us, event | category | flops | bytes accessed | tf_op | source)
XLA Modules:
  0.0 89.6 jit_solution(616658143775796581)
XLA Ops:
  0.0 0.0 collective-permute-start
  0.0 1.6 %copy-done.3 = bf16[512,2048]{1,0:T(8,128)(2,1)S(1)} copy-done((bf16[512,2048]{1,0:T(8,128)(2,1)S(1)}, bf16[512,2048]{1,0:T(8,128)(2,1)}, u32[]{:S(2)}) %copy-start.3) | copy-done | bytes 2097176
  1.6 0.7 copy-done.7
  2.3 0.4 norm.1
  2.7 0.0 copy-start
  2.7 0.0 copy-start.2
  2.7 0.0 collective-permute-done.other_ref
  2.7 0.7 copy-done.5
  3.4 0.8 project.1
  4.3 1.6 %collective-permute-start.2 = (bf16[256,256]{1,0:T(8,128)(2,1)S(1)}, bf16[256,256]{1,0:T(8,128)(2,1)S(1)}, u32[]{:S(2)}, u32[]{:S(2)}) collective-permute-start(bf16[256,256]{1,0:T(8,128)(2,1)S(1)} %get-tuple-element.35.kv0), channel_id=1, source_target_pairs={{0,32},{32,64},{64,96},{96,0},{1,33},{33,65},{65,97},{97,1},{2,34}... | collective-permute-start | bytes 393224 | tf_op jit(solution)/shard_map/ppermute | solution.py:28
  5.9 0.2 collective-permute-start.1
  6.1 0.0 copy-done
  6.1 1.6 %collective-permute-start.6 = (bf16[64,2048]{1,0:T(8,128)(2,1)S(1)}, bf16[64,2048]{1,0:T(8,128)(2,1)S(1)}, u32[]{:S(2)}, u32[]{:S(2)}) collective-permute-start(bf16[64,2048]{1,0:T(8,128)(2,1)S(1)} %copy-done), channel_id=1, source_target_pairs={{0,2},{2,4},{4,6},{6,0},{1,3},{3,5},{5,7},{7,1},{8,10},{10,12},{12... | collective-permute-start | bytes 786440 | tf_op jit(solution)/shard_map/ppermute | solution.py:28
  7.7 2.9 %collective-permute-start.7 = (bf16[64,2048]{1,0:T(8,128)(2,1)S(1)}, bf16[64,2048]{1,0:T(8,128)(2,1)S(1)}, u32[]{:S(2)}, u32[]{:S(2)}) collective-permute-start(bf16[64,2048]{1,0:T(8,128)(2,1)S(1)} %copy-done), channel_id=1, source_target_pairs={{0,4},{2,6},{4,0},{6,2},{1,5},{3,7},{5,1},{7,3},{8,12},{10,14},{12... | collective-permute-start | bytes 786440 | tf_op jit(solution)/shard_map/ppermute | solution.py:28
  10.6 1.3 %collective-permute-start.8 = (bf16[64,2048]{1,0:T(8,128)(2,1)S(1)}, bf16[64,2048]{1,0:T(8,128)(2,1)S(1)}, u32[]{:S(2)}, u32[]{:S(2)}) collective-permute-start(bf16[64,2048]{1,0:T(8,128)(2,1)S(1)} %copy-done), channel_id=1, source_target_pairs={{0,6},{2,0},{4,2},{6,4},{1,7},{3,1},{5,3},{7,5},{8,14},{10,8},{12,... | collective-permute-start | bytes 786440 | tf_op jit(solution)/shard_map/ppermute | solution.py:28
  12.0 0.0 collective-permute-done.1.q_other_ref
  12.0 2.7 %collective-permute-start.3 = (bf16[256,256]{1,0:T(8,128)(2,1)S(1)}, bf16[256,256]{1,0:T(8,128)(2,1)S(1)}, u32[]{:S(2)}, u32[]{:S(2)}) collective-permute-start(bf16[256,256]{1,0:T(8,128)(2,1)S(1)} %get-tuple-element.35.kv0), channel_id=1, source_target_pairs={{0,64},{32,96},{64,0},{96,32},{1,65},{33,97},{65,1},{97,33},{2,66}... | collective-permute-start | bytes 393224 | tf_op jit(solution)/shard_map/ppermute | solution.py:28
  14.7 0.0 collective-permute-done.2.kv1
  14.7 1.4 %collective-permute-start.4 = (bf16[256,256]{1,0:T(8,128)(2,1)S(1)}, bf16[256,256]{1,0:T(8,128)(2,1)S(1)}, u32[]{:S(2)}, u32[]{:S(2)}) collective-permute-start(bf16[256,256]{1,0:T(8,128)(2,1)S(1)} %get-tuple-element.35.kv0), channel_id=1, source_target_pairs={{0,96},{32,0},{64,32},{96,64},{1,97},{33,1},{65,33},{97,65},{2,98}... | collective-permute-start | bytes 393224 | tf_op jit(solution)/shard_map/ppermute | solution.py:28
  16.1 0.0 copy-done.2
  16.1 3.2 %carried.1.carried_ref = f32[64,512]{1,0:T(8,128)S(1)} custom-call(f32[64,8256]{1,0:T(8,128)S(1)} %bitcast.14, bf16[128,256]{1,0:T(8,128)(2,1)S(1)} %get-tuple-element.34.q_own_ref, bf16[128,256]{1,0:T(8,128)(2,1)S(1)} %collective-permute-done.1.q_other_ref), custom_call_target="tpu_custom_call" | custom-call | flops 5000000000 | bytes 15000000 | tf_op jit(solution)/shard_map/carried/pallas_call | solution.py:104
  19.3 0.0 copy-start.1
  19.3 0.0 collective-permute-done.3.kv2
  19.3 1.0 %collective-permute-done.4.kv3 = bf16[256,256]{1,0:T(8,128)(2,1)S(1)} collective-permute-done((bf16[256,256]{1,0:T(8,128)(2,1)S(1)}, bf16[256,256]{1,0:T(8,128)(2,1)S(1)}, u32[]{:S(2)}, u32[]{:S(2)}) %collective-permute-start.4) | collective-permute-done | bytes 131104 | tf_op jit(solution)/shard_map/ppermute | solution.py:28
  20.3 1.1 %window.1 = (f32[256,128]{1,0:T(8,128)S(1)}, bf16[256,128]{1,0:T(8,128)(2,1)S(1)}) custom-call(bf16[128,256]{1,0:T(8,128)(2,1)S(1)} %get-tuple-element.34.q_own_ref, bf16[128,256]{1,0:T(8,128)(2,1)S(1)} %collective-permute-done.1.q_other_ref, bf16[256,256]{1,0:T(8,128)(2,1)S(1)} %get-tuple-element.35.kv0, bf16[256,256]{1,0:T(8,128)(2,1)S(1)} %collective-permute-done.2.kv1, ...), custom_call_target="tpu_custom_call" | custom-call | flops 2000000000 | bytes 6000000 | tf_op jit(solution)/shard_map/window/pallas_call | solution.py:150
  21.4 0.0 copy-start.4
  21.4 0.1 collective-permute-start.5
  21.5 0.0 collective-permute-done.6.refs_1_
  21.5 1.2 %collective-permute-done.7.refs_2_ = bf16[64,2048]{1,0:T(8,128)(2,1)S(1)} collective-permute-done((bf16[64,2048]{1,0:T(8,128)(2,1)S(1)}, bf16[64,2048]{1,0:T(8,128)(2,1)S(1)}, u32[]{:S(2)}, u32[]{:S(2)}) %collective-permute-start.7) | collective-permute-done | bytes 262176 | tf_op jit(solution)/shard_map/ppermute | solution.py:28
  22.7 0.0 collective-permute-done.8.refs_3_
  22.7 0.1 collective-permute-done.5.received_ref
  22.8 0.0 copy-done.1
  22.8 0.2 collective-permute-start.16
  22.9 0.1 pack.1.rest_4_
  23.0 0.4 collective-permute-start.12
  23.5 0.0 copy-done.4
  23.5 0.1 collective-permute-start.17
  23.6 0.1 attend.1
  23.7 2.5 %collective-permute-start.10 = (bf16[64,128]{1,0:T(8,128)(2,1)S(1)}, bf16[64,128]{1,0:T(8,128)(2,1)S(1)}, u32[]{:S(2)}, u32[]{:S(2)}) collective-permute-start(bf16[64,128]{1,0:T(8,128)(2,1)S(1)} %get-tuple-element.41), channel_id=1, source_target_pairs={{0,4},{2,6},{4,0},{6,2},{1,5},{3,7},{5,1},{7,3},{8,12},{10,14},{12... | collective-permute-start | bytes 49160 | tf_op jit(solution)/shard_map/ppermute | solution.py:28
  26.3 1.2 %collective-permute-start.11 = (bf16[64,128]{1,0:T(8,128)(2,1)S(1)}, bf16[64,128]{1,0:T(8,128)(2,1)S(1)}, u32[]{:S(2)}, u32[]{:S(2)}) collective-permute-start(bf16[64,128]{1,0:T(8,128)(2,1)S(1)} %get-tuple-element.42), channel_id=1, source_target_pairs={{0,6},{2,0},{4,2},{6,4},{1,7},{3,1},{5,3},{7,5},{8,14},{10,8},{12,... | collective-permute-start | bytes 49160 | tf_op jit(solution)/shard_map/ppermute | solution.py:28
  27.5 1.6 %collective-permute-done.10.rest_2_ = bf16[64,128]{1,0:T(8,128)(2,1)S(1)} collective-permute-done((bf16[64,128]{1,0:T(8,128)(2,1)S(1)}, bf16[64,128]{1,0:T(8,128)(2,1)S(1)}, u32[]{:S(2)}, u32[]{:S(2)}) %collective-permute-start.10) | collective-permute-done | bytes 16416 | tf_op jit(solution)/shard_map/ppermute | solution.py:28
  29.1 1.0 %collective-permute-start.9 = (bf16[64,128]{1,0:T(8,128)(2,1)S(1)}, bf16[64,128]{1,0:T(8,128)(2,1)S(1)}, u32[]{:S(2)}, u32[]{:S(2)}) collective-permute-start(bf16[64,128]{1,0:T(8,128)(2,1)S(1)} %get-tuple-element.40), channel_id=1, source_target_pairs={{0,2},{2,4},{4,6},{6,0},{1,3},{3,5},{5,7},{7,1},{8,10},{10,12},{12... | collective-permute-start | bytes 49160 | tf_op jit(solution)/shard_map/ppermute | solution.py:28
  30.1 0.0 collective-permute-done.11.rest_3_
  30.1 3.9 %collective-permute-done.9.rest_1_ = bf16[64,128]{1,0:T(8,128)(2,1)S(1)} collective-permute-done((bf16[64,128]{1,0:T(8,128)(2,1)S(1)}, bf16[64,128]{1,0:T(8,128)(2,1)S(1)}, u32[]{:S(2)}, u32[]{:S(2)}) %collective-permute-start.9) | collective-permute-done | bytes 16416 | tf_op jit(solution)/shard_map/ppermute | solution.py:28
  34.0 0.0 collective-permute-done.12.rest_5_
  34.0 0.7 output.1
  34.8 2.0 %collective-permute-start.13 = (bf16[16,2048]{1,0:T(8,128)(2,1)S(1)}, bf16[16,2048]{1,0:T(8,128)(2,1)S(1)}, u32[]{:S(2)}, u32[]{:S(2)}) collective-permute-start(bf16[16,2048]{1,0:T(8,128)(2,1)S(1)} %get-tuple-element.48), channel_id=1, source_target_pairs={{0,8},{8,16},{16,24},{24,0},{1,9},{9,17},{17,25},{25,1},{2,10},{10... | collective-permute-start | bytes 196616 | tf_op jit(solution)/shard_map/ppermute | solution.py:28
  36.8 3.6 %collective-permute-start.14 = (bf16[16,2048]{1,0:T(8,128)(2,1)S(1)}, bf16[16,2048]{1,0:T(8,128)(2,1)S(1)}, u32[]{:S(2)}, u32[]{:S(2)}) collective-permute-start(bf16[16,2048]{1,0:T(8,128)(2,1)S(1)} %get-tuple-element.49), channel_id=1, source_target_pairs={{0,16},{8,24},{16,0},{24,8},{1,17},{9,25},{17,1},{25,9},{2,18},{10... | collective-permute-start | bytes 196616 | tf_op jit(solution)/shard_map/ppermute | solution.py:28
  40.4 1.0 %collective-permute-start.15 = (bf16[16,2048]{1,0:T(8,128)(2,1)S(1)}, bf16[16,2048]{1,0:T(8,128)(2,1)S(1)}, u32[]{:S(2)}, u32[]{:S(2)}) collective-permute-start(bf16[16,2048]{1,0:T(8,128)(2,1)S(1)} %get-tuple-element.50), channel_id=1, source_target_pairs={{0,24},{8,0},{16,8},{24,16},{1,25},{9,1},{17,9},{25,17},{2,26},{10... | collective-permute-start | bytes 196616 | tf_op jit(solution)/shard_map/ppermute | solution.py:28
  41.4 0.0 copy-done.8
  41.4 0.0 copy-done.9
  41.4 1.8 %maps.1 = (bf16[3072,256]{1,0:T(8,128)(2,1)S(1)}, f32[16,3072]{1,0:T(8,128)S(1)}, f32[1,2048]{1,0:T(1,128)S(1)}) custom-call(s32[8,16]{1,0:T(8,128)S(1)} %bitcast.21, f32[1,2048]{1,0:T(1,128)S(1)} %bitcast.20), custom_call_target="tpu_custom_call" | custom-call | flops 2000000000 | bytes 6000000 | tf_op jit(solution)/shard_map/maps/pallas_call | solution.py:350
  43.2 0.0 collective-permute-done.13.r1
  43.2 0.1 collective-permute-done.14.r2
  43.3 1.3 %collective-permute-done.15.r3 = bf16[16,2048]{1,0:T(8,128)(2,1)S(1)} collective-permute-done((bf16[16,2048]{1,0:T(8,128)(2,1)S(1)}, bf16[16,2048]{1,0:T(8,128)(2,1)S(1)}, u32[]{:S(2)}, u32[]{:S(2)}) %collective-permute-start.15) | collective-permute-done | bytes 65568 | tf_op jit(solution)/shard_map/ppermute | solution.py:28
  44.6 0.8 dispatch.1
  45.4 20.6 %all_to_all.10 = bf16[64,48,128]{2,1,0:T(8,128)(2,1)S(1)} all-to-all(bf16[64,48,128]{2,1,0:T(8,128)(2,1)S(1)} %bitcast.12), channel_id=1, replica_groups=mesh['x'=4,'z'=4,'y'=4,'c'=2] {'x','z','y'}, dimensions={0} | all-to-all | bytes 1572864 | tf_op jit(solution)/shard_map/all_to_all | solution.py:485
  66.0 0.0 collective-permute-done.17.second_other
  66.0 0.0 collective-permute-done.16.first_other
  66.0 4.5 %experts.1 = bf16[3072,128]{1,0:T(8,128)(2,1)} custom-call(bf16[3072,128]{1,0:T(8,128)(2,1)S(1)} %bitcast.13, bf16[2,2048,512]{2,1,0:T(8,128)(2,1)S(1)} %copy-done.1, bf16[512,2048]{1,0:T(8,128)(2,1)S(1)} %copy-done.4, bf16[2,2048,512]{2,1,0:T(8,128)(2,1)S(1)} %collective-permute-done.16.first_other, bf16[512,2048]{1,0:T(8,128)(2,1)S(1)} %collective-permute-done.17.second_other), custom_call_target="tpu_custom_call" | custom-call | flops 5000000000 | bytes 15000000 | tf_op jit(solution)/shard_map/experts/pallas_call | solution.py:446
  70.6 4.8 %all-to-all-start.1 = ((bf16[64,48,128]{2,1,0:T(8,128)(2,1)}), bf16[64,48,128]{2,1,0:T(8,128)(2,1)S(1)}, u32[]{:S(2)}, u32[]{:S(2)}) async-start(bf16[64,48,128]{2,1,0:T(8,128)(2,1)} %bitcast.9), calls=%async_computation.1 | async-start | bytes 1572864 | tf_op jit(solution)/shard_map/all_to_all | solution.py:485
  75.3 0.4 gates.1.gates_ref
  75.8 12.6 %all-to-all-done.1 = bf16[64,48,128]{2,1,0:T(8,128)(2,1)S(1)} async-done(((bf16[64,48,128]{2,1,0:T(8,128)(2,1)}), bf16[64,48,128]{2,1,0:T(8,128)(2,1)S(1)}, u32[]{:S(2)}, u32[]{:S(2)}) %all-to-all-start.1) | async-done | bytes 786464 | tf_op jit(solution)/shard_map/all_to_all | solution.py:485
  88.4 1.2 %combine.1 = bf16[16,2048]{1,0:T(8,128)(2,1)} custom-call(f32[16,2048]{1,0:T(8,128)S(1)} %get-tuple-element.53.residual_ref, bf16[256,3072]{1,0:T(8,128)(2,1)S(1)} %gates.1.gates_ref, bf16[3072,128]{1,0:T(8,128)(2,1)S(1)} %bitcast.11), custom_call_target="tpu_custom_call" | custom-call | flops 1000000000 | bytes 3000000 | tf_op jit(solution)/shard_map/combine/pallas_call | solution.py:472
  (7 shorter events, 0.0 us)
Async XLA Ops:
  0.0 2.7 %collective-permute-start = (bf16[3,64,2048]{2,1,0:T(8,128)(2,1)}, bf16[3,64,2048]{2,1,0:T(8,128)(2,1)S(1)}, u32[]{:S(2)}, u32[]{:S(2)}) collective-permute-start(bf16[3,64,2048]{2,1,0:T(8,128)(2,1)} %bitcast.16), channel_id=1, source_target_pairs={{0,1},{1,0},{2,3},{3,2},{4,5},{5,4},{6,7},{7,6},{8,9},{9,8},{10,11... | collective-permute-start | bytes 2359304 | tf_op jit(solution)/shard_map/ppermute | solution.py:24
  0.0 1.6 %copy-start.3 = (bf16[512,2048]{1,0:T(8,128)(2,1)S(1)}, bf16[512,2048]{1,0:T(8,128)(2,1)}, u32[]{:S(2)}) copy-start(bf16[512,2048]{1,0:T(8,128)(2,1)} %param.10) | copy-start | bytes 6291460
  1.6 0.7 copy-start.7
  2.3 1.1 %copy-start.5 = (bf16[3,2048,64]{1,2,0:T(8,128)(2,1)S(1)}, bf16[3,2048,64]{1,2,0:T(8,128)(2,1)}, u32[]{:S(2)}) copy-start(bf16[3,2048,64]{1,2,0:T(8,128)(2,1)} %param.12) | copy-start | bytes 2359300
  2.7 3.4 %copy-start = (bf16[64,2048]{1,0:T(8,128)(2,1)S(1)}, bf16[64,2048]{1,0:T(8,128)(2,1)}, u32[]{:S(2)}) copy-start(bf16[64,2048]{1,0:T(8,128)(2,1)} %refs_0_) | copy-start | bytes 786436
  2.7 13.4 %copy-start.2 = (f32[8256,64]{0,1:T(8,128)S(1)}, f32[8256,64]{0,1:T(8,128)}, u32[]{:S(2)}) copy-start(f32[8256,64]{0,1:T(8,128)} %param.13) | copy-start | bytes 6340612
  4.3 10.4 %collective-permute-start.2 = (bf16[256,256]{1,0:T(8,128)(2,1)S(1)}, bf16[256,256]{1,0:T(8,128)(2,1)S(1)}, u32[]{:S(2)}, u32[]{:S(2)}) collective-permute-start(bf16[256,256]{1,0:T(8,128)(2,1)S(1)} %get-tuple-element.35.kv0), channel_id=1, source_target_pairs={{0,32},{32,64},{64,96},{96,0},{1,33},{33,65},{65,97},{97,1},{2,34}... | collective-permute-start | bytes 393224 | tf_op jit(solution)/shard_map/ppermute | solution.py:28
  5.9 6.1 %collective-permute-start.1 = (bf16[128,256]{1,0:T(8,128)(2,1)S(1)}, bf16[128,256]{1,0:T(8,128)(2,1)S(1)}, u32[]{:S(2)}, u32[]{:S(2)}) collective-permute-start(bf16[128,256]{1,0:T(8,128)(2,1)S(1)} %get-tuple-element.34.q_own_ref), channel_id=1, source_target_pairs={{0,1},{1,0},{2,3},{3,2},{4,5},{5,4},{6,7},{7,6},{8,9},{9,8},{10,11... | collective-permute-start | bytes 196616 | tf_op jit(solution)/shard_map/ppermute | solution.py:24
  6.1 15.4 %collective-permute-start.6 = (bf16[64,2048]{1,0:T(8,128)(2,1)S(1)}, bf16[64,2048]{1,0:T(8,128)(2,1)S(1)}, u32[]{:S(2)}, u32[]{:S(2)}) collective-permute-start(bf16[64,2048]{1,0:T(8,128)(2,1)S(1)} %copy-done), channel_id=1, source_target_pairs={{0,2},{2,4},{4,6},{6,0},{1,3},{3,5},{5,7},{7,1},{8,10},{10,12},{12... | collective-permute-start | bytes 786440 | tf_op jit(solution)/shard_map/ppermute | solution.py:28
  7.7 15.0 %collective-permute-start.7 = (bf16[64,2048]{1,0:T(8,128)(2,1)S(1)}, bf16[64,2048]{1,0:T(8,128)(2,1)S(1)}, u32[]{:S(2)}, u32[]{:S(2)}) collective-permute-start(bf16[64,2048]{1,0:T(8,128)(2,1)S(1)} %copy-done), channel_id=1, source_target_pairs={{0,4},{2,6},{4,0},{6,2},{1,5},{3,7},{5,1},{7,3},{8,12},{10,14},{12... | collective-permute-start | bytes 786440 | tf_op jit(solution)/shard_map/ppermute | solution.py:28
  10.6 12.1 %collective-permute-start.8 = (bf16[64,2048]{1,0:T(8,128)(2,1)S(1)}, bf16[64,2048]{1,0:T(8,128)(2,1)S(1)}, u32[]{:S(2)}, u32[]{:S(2)}) collective-permute-start(bf16[64,2048]{1,0:T(8,128)(2,1)S(1)} %copy-done), channel_id=1, source_target_pairs={{0,6},{2,0},{4,2},{6,4},{1,7},{3,1},{5,3},{7,5},{8,14},{10,8},{12,... | collective-permute-start | bytes 786440 | tf_op jit(solution)/shard_map/ppermute | solution.py:28
  12.0 7.3 %collective-permute-start.3 = (bf16[256,256]{1,0:T(8,128)(2,1)S(1)}, bf16[256,256]{1,0:T(8,128)(2,1)S(1)}, u32[]{:S(2)}, u32[]{:S(2)}) collective-permute-start(bf16[256,256]{1,0:T(8,128)(2,1)S(1)} %get-tuple-element.35.kv0), channel_id=1, source_target_pairs={{0,64},{32,96},{64,0},{96,32},{1,65},{33,97},{65,1},{97,33},{2,66}... | collective-permute-start | bytes 393224 | tf_op jit(solution)/shard_map/ppermute | solution.py:28
  14.7 5.6 %collective-permute-start.4 = (bf16[256,256]{1,0:T(8,128)(2,1)S(1)}, bf16[256,256]{1,0:T(8,128)(2,1)S(1)}, u32[]{:S(2)}, u32[]{:S(2)}) collective-permute-start(bf16[256,256]{1,0:T(8,128)(2,1)S(1)} %get-tuple-element.35.kv0), channel_id=1, source_target_pairs={{0,96},{32,0},{64,32},{96,64},{1,97},{33,1},{65,33},{97,65},{2,98}... | collective-permute-start | bytes 393224 | tf_op jit(solution)/shard_map/ppermute | solution.py:28
  19.3 3.5 %copy-start.1 = (bf16[2,2048,512]{2,1,0:T(8,128)(2,1)S(1)}, bf16[2,2048,512]{2,1,0:T(8,128)(2,1)}, u32[]{:S(2)}) copy-start(bf16[2,2048,512]{2,1,0:T(8,128)(2,1)} %first_own.1) | copy-start | bytes 12582916
  21.4 2.0 %copy-start.4 = (bf16[512,2048]{1,0:T(8,128)(2,1)S(1)}, bf16[512,2048]{1,0:T(8,128)(2,1)}, u32[]{:S(2)}) copy-start(bf16[512,2048]{1,0:T(8,128)(2,1)} %second_own.1) | copy-start | bytes 6291460
  21.4 1.3 %collective-permute-start.5 = (bf16[256,128]{1,0:T(8,128)(2,1)S(1)}, bf16[256,128]{1,0:T(8,128)(2,1)S(1)}, u32[]{:S(2)}, u32[]{:S(2)}) collective-permute-start(bf16[256,128]{1,0:T(8,128)(2,1)S(1)} %get-tuple-element.37), channel_id=1, source_target_pairs={{0,1},{1,0},{2,3},{3,2},{4,5},{5,4},{6,7},{7,6},{8,9},{9,8},{10,11... | collective-permute-start | bytes 196616 | tf_op jit(solution)/shard_map/ppermute | solution.py:24
  22.8 43.3 %collective-permute-start.16 = (bf16[2,2048,512]{2,1,0:T(8,128)(2,1)S(1)}, bf16[2,2048,512]{2,1,0:T(8,128)(2,1)S(1)}, u32[]{:S(2)}, u32[]{:S(2)}) collective-permute-start(bf16[2,2048,512]{2,1,0:T(8,128)(2,1)S(1)} %copy-done.1), channel_id=1, source_target_pairs={{0,1},{1,0},{2,3},{3,2},{4,5},{5,4},{6,7},{7,6},{8,9},{9,8},{10,11... | collective-permute-start | bytes 12582920 | tf_op jit(solution)/shard_map/ppermute | solution.py:24
  23.0 11.0 %collective-permute-start.12 = (bf16[256,2048]{1,0:T(8,128)(2,1)S(1)}, bf16[256,2048]{1,0:T(8,128)(2,1)S(1)}, u32[]{:S(2)}, u32[]{:S(2)}) collective-permute-start(bf16[256,2048]{1,0:T(8,128)(2,1)S(1)} %pack.1.rest_4_), channel_id=1, source_target_pairs={{0,1},{1,0},{2,3},{3,2},{4,5},{5,4},{6,7},{7,6},{8,9},{9,8},{10,11... | collective-permute-start | bytes 3145736 | tf_op jit(solution)/shard_map/ppermute | solution.py:24
  23.5 42.6 %collective-permute-start.17 = (bf16[512,2048]{1,0:T(8,128)(2,1)S(1)}, bf16[512,2048]{1,0:T(8,128)(2,1)S(1)}, u32[]{:S(2)}, u32[]{:S(2)}) collective-permute-start(bf16[512,2048]{1,0:T(8,128)(2,1)S(1)} %copy-done.4), channel_id=1, source_target_pairs={{0,1},{1,0},{2,3},{3,2},{4,5},{5,4},{6,7},{7,6},{8,9},{9,8},{10,11... | collective-permute-start | bytes 6291464 | tf_op jit(solution)/shard_map/ppermute | solution.py:24
  23.7 5.3 %collective-permute-start.10 = (bf16[64,128]{1,0:T(8,128)(2,1)S(1)}, bf16[64,128]{1,0:T(8,128)(2,1)S(1)}, u32[]{:S(2)}, u32[]{:S(2)}) collective-permute-start(bf16[64,128]{1,0:T(8,128)(2,1)S(1)} %get-tuple-element.41), channel_id=1, source_target_pairs={{0,4},{2,6},{4,0},{6,2},{1,5},{3,7},{5,1},{7,3},{8,12},{10,14},{12... | collective-permute-start | bytes 49160 | tf_op jit(solution)/shard_map/ppermute | solution.py:28
  26.3 3.8 %collective-permute-start.11 = (bf16[64,128]{1,0:T(8,128)(2,1)S(1)}, bf16[64,128]{1,0:T(8,128)(2,1)S(1)}, u32[]{:S(2)}, u32[]{:S(2)}) collective-permute-start(bf16[64,128]{1,0:T(8,128)(2,1)S(1)} %get-tuple-element.42), channel_id=1, source_target_pairs={{0,6},{2,0},{4,2},{6,4},{1,7},{3,1},{5,3},{7,5},{8,14},{10,8},{12,... | collective-permute-start | bytes 49160 | tf_op jit(solution)/shard_map/ppermute | solution.py:28
  29.1 4.9 %collective-permute-start.9 = (bf16[64,128]{1,0:T(8,128)(2,1)S(1)}, bf16[64,128]{1,0:T(8,128)(2,1)S(1)}, u32[]{:S(2)}, u32[]{:S(2)}) collective-permute-start(bf16[64,128]{1,0:T(8,128)(2,1)S(1)} %get-tuple-element.40), channel_id=1, source_target_pairs={{0,2},{2,4},{4,6},{6,0},{1,3},{3,5},{5,7},{7,1},{8,10},{10,12},{12... | collective-permute-start | bytes 49160 | tf_op jit(solution)/shard_map/ppermute | solution.py:28
  34.0 7.3 %copy-start.8 = (f32[2048]{0:T(1024)S(1)}, f32[2048]{0:T(1024)}, u32[]{:S(2)}) copy-start(f32[2048]{0:T(1024)} %param.15) | copy-start | bytes 24580
  34.0 7.3 %copy-start.9 = (s32[16,8]{0,1:T(8,128)S(1)}, s32[16,8]{0,1:T(8,128)}, u32[]{:S(2)}) copy-start(s32[16,8]{0,1:T(8,128)} %param.17) | copy-start | bytes 1540
  34.8 8.4 %collective-permute-start.13 = (bf16[16,2048]{1,0:T(8,128)(2,1)S(1)}, bf16[16,2048]{1,0:T(8,128)(2,1)S(1)}, u32[]{:S(2)}, u32[]{:S(2)}) collective-permute-start(bf16[16,2048]{1,0:T(8,128)(2,1)S(1)} %get-tuple-element.48), channel_id=1, source_target_pairs={{0,8},{8,16},{16,24},{24,0},{1,9},{9,17},{17,25},{25,1},{2,10},{10... | collective-permute-start | bytes 196616 | tf_op jit(solution)/shard_map/ppermute | solution.py:28
  36.8 6.5 %collective-permute-start.14 = (bf16[16,2048]{1,0:T(8,128)(2,1)S(1)}, bf16[16,2048]{1,0:T(8,128)(2,1)S(1)}, u32[]{:S(2)}, u32[]{:S(2)}) collective-permute-start(bf16[16,2048]{1,0:T(8,128)(2,1)S(1)} %get-tuple-element.49), channel_id=1, source_target_pairs={{0,16},{8,24},{16,0},{24,8},{1,17},{9,25},{17,1},{25,9},{2,18},{10... | collective-permute-start | bytes 196616 | tf_op jit(solution)/shard_map/ppermute | solution.py:28
  40.4 4.3 %collective-permute-start.15 = (bf16[16,2048]{1,0:T(8,128)(2,1)S(1)}, bf16[16,2048]{1,0:T(8,128)(2,1)S(1)}, u32[]{:S(2)}, u32[]{:S(2)}) collective-permute-start(bf16[16,2048]{1,0:T(8,128)(2,1)S(1)} %get-tuple-element.50), channel_id=1, source_target_pairs={{0,24},{8,0},{16,8},{24,16},{1,25},{9,1},{17,9},{25,17},{2,26},{10... | collective-permute-start | bytes 196616 | tf_op jit(solution)/shard_map/ppermute | solution.py:28
  41.4 3.3 %copy-start.6 = (bf16[2048,64]{0,1:T(8,128)(2,1)S(1)}, bf16[2048,64]{0,1:T(8,128)(2,1)}, u32[]{:S(2)}) copy-start(bf16[2048,64]{0,1:T(8,128)(2,1)} %param.16) | copy-start | bytes 786436
  70.6 17.8 %all-to-all-start.1 = ((bf16[64,48,128]{2,1,0:T(8,128)(2,1)}), bf16[64,48,128]{2,1,0:T(8,128)(2,1)S(1)}, u32[]{:S(2)}, u32[]{:S(2)}) async-start(bf16[64,48,128]{2,1,0:T(8,128)(2,1)} %bitcast.9), calls=%async_computation.1 | async-start | bytes 1572864 | tf_op jit(solution)/shard_map/all_to_all | solution.py:485

commit v5 on v4

--- a/solution.py
+++ b/solution.py
@@ -362,7 +362,9 @@
     )(index, gain.reshape(1, D))
 
 
-def dispatch_kernel(slab_ref, own_ref, r1, r2, r3, gain_ref, router_ref, rows_ref, residual_ref, out_ref, gates_ref):
+def dispatch_kernel(
+    slab_ref, own_ref, r1, r2, r3, gain_ref, router_ref, rows_ref, lanes_ref, residual_ref, out_ref, wide_ref
+):
     residual = slab_ref[...].astype(jnp.float32) + own_ref[...]
     for received in (r1, r2, r3):
         residual = residual + received[...].astype(jnp.float32)
@@ -371,51 +373,31 @@
     logits = lax.dot_general(
         inputs, router_ref[...], (((1,), (1,)), ((), ())), preferred_element_type=jnp.float32
     )
-    gates_ref[...] = jax.nn.sigmoid(logits)
+    wide_ref[...] = lanes_ref[...] * jnp.dot(
+        jax.nn.sigmoid(logits).astype(jnp.bfloat16),
+        spread_map(),
+        preferred_element_type=jnp.float32,
+    )
     tall = jnp.concatenate([inputs[:, at : at + 128] for at in range(0, D, 128)], axis=0)
     out_ref[...] = jnp.dot(rows_ref[...], tall, preferred_element_type=jnp.float32).astype(
         jnp.bfloat16
     )
 
 
-def dispatch_part(slab, own, received, gain, router, rows):
+def dispatch_part(slab, own, received, gain, router, rows, lanes):
     return pl.pallas_call(
         dispatch_kernel,
         out_shape=(
             jax.ShapeDtypeStruct((SLAB, D), jnp.float32),
             jax.ShapeDtypeStruct((TILE_ROWS, 128), jnp.bfloat16),
-            jax.ShapeDtypeStruct((SLAB, EXPERTS), jnp.float32),
+            jax.ShapeDtypeStruct((SLAB, TILE_ROWS), jnp.float32),
         ),
-        in_specs=[VMEM] * 8,
+        in_specs=[VMEM] * 9,
         out_specs=(VMEM,) * 3,
         compiler_params=room(6),
         cost_estimate=cost(1),
         name="dispatch",
-    )(slab, own, *received, gain, router, rows)
-
-
-def gate_kernel(gates_ref, lanes_ref, out_ref):
-    wide = jnp.dot(
-        gates_ref[...].astype(jnp.bfloat16), spread_map(), preferred_element_type=jnp.float32
-    )
-    wide = wide * lanes_ref[...]
-    piece = lax.broadcasted_iota(jnp.int32, (SLAB, TILE_ROWS), 1) % PIECES
-    for at in range(PIECES):
-        out_ref[at * SLAB : (at + 1) * SLAB, :] = jnp.where(piece == at, wide, 0.0).astype(
-            jnp.bfloat16
-        )
-
-
-def gate_part(gates, lanes):
-    return pl.pallas_call(
-        gate_kernel,
-        out_shape=jax.ShapeDtypeStruct((256, TILE_ROWS), jnp.bfloat16),
-        in_specs=[VMEM, VMEM],
-        out_specs=VMEM,
-        compiler_params=room(8),
-        cost_estimate=cost(0.5),
-        name="gates",
-    )(gates, lanes)
+    )(slab, own, *received, gain, router, rows, lanes)
 
 
 def expert_kernel(
@@ -459,8 +441,14 @@
     )(rows, first, second, first_other, second_other)
 
 
-def combine_kernel(residual_ref, gates_ref, rows_ref, out_ref):
-    tall = jnp.dot(gates_ref[...], rows_ref[...], preferred_element_type=jnp.float32)
+def combine_kernel(residual_ref, wide_ref, rows_ref, out_ref, map_ref):
+    wide = wide_ref[...]
+    piece = lax.broadcasted_iota(jnp.int32, (SLAB, TILE_ROWS), 1) % PIECES
+    for at in range(PIECES):
+        map_ref[at * SLAB : (at + 1) * SLAB, :] = jnp.where(piece == at, wide, 0.0).astype(
+            jnp.bfloat16
+        )
+    tall = jnp.dot(map_ref[...], rows_ref[...], preferred_element_type=jnp.float32)
     for at in range(PIECES):
         columns = slice(at * 128, (at + 1) * 128)
         out_ref[:, columns] = (
@@ -468,16 +456,17 @@
         ).astype(jnp.bfloat16)
 
 
-def combine_part(residual, gates, rows):
+def combine_part(residual, wide, rows):
     return pl.pallas_call(
         combine_kernel,
         out_shape=jax.ShapeDtypeStruct((SLAB, D), jnp.bfloat16),
         in_specs=[VMEM] * 3,
         out_specs=VMEM,
-        compiler_params=room(4),
+        scratch_shapes=[pltpu.VMEM((256, TILE_ROWS), jnp.bfloat16)],
+        compiler_params=room(6),
         cost_estimate=cost(1),
         name="combine",
-    )(residual, gates, rows)
+    )(residual, wide, rows)
 
 
 def chips(rows):
@@ -518,13 +507,12 @@
     pieces = [pieces[0]] + [shift(pieces[step], "y", step) for step in (1, 2, 3)]
     sums = output_part(pieces, output_own, output_other)
     summed = [shift(sums[step], "z", step) for step in (1, 2, 3)]
-    residual, outgoing, gates = dispatch_part(
-        slab, sums[0], summed, gain, router_weight.T, rows_map
+    residual, outgoing, wide = dispatch_part(
+        slab, sums[0], summed, gain, router_weight.T, rows_map, lanes_map
     )
     arrived = chips(outgoing)
-    gate_map = gate_part(gates, lanes_map)
     produced = expert_part(arrived, expert_first, expert_second, first_other, second_other)
-    return combine_part(residual, gate_map, chips(produced))
+    return combine_part(residual, wide, chips(produced))
 
 
 def solution(mesh):

time: 89.9 us -> 88.3 us (0.982)
  blocking collectives: 20.6 us -> 36.3 us
  waiting for transfers between devices: 21.8 us -> 13.6 us
  starting transfers between devices: 28.8 us -> 20.7 us
  Pallas kernels: 15.2 us -> 14.2 us
    all_to_all x1 -> x2, blocking collectives: 20.6 us -> 36.3 us  [chips(): lax.all_to_all(shaped, CHIP_AXES, split_axis=0, concat_axis=0, tiled=True)]
    all_to_all x1 -> x0, waiting for transfers between devices: 12.6 us -> none  [chips(): lax.all_to_all(shaped, CHIP_AXES, split_axis=0, concat_axis=0, tiled=True)]
    all_to_all x1 -> x0, starting transfers between devices: 4.77 us -> none  [chips(): lax.all_to_all(shaped, CHIP_AXES, split_axis=0, concat_axis=0, tiled=True)]
    ppermute x12, starting transfers between devices: 23 us -> 19.7 us  [shift(): return lax.ppermute(array, axis, [(i, (i + step) % 4) for i in range(4)])]
    ppermute x12, waiting for transfers between devices: 9.08 us -> 12.4 us  [shift(): return lax.ppermute(array, axis, [(i, (i + step) % 4) for i in range(4)])]
    ppermute x6, waiting for transfers between devices: 0.08 us -> 1.22 us  [swap_core(): return lax.ppermute(array, 'c', [(0, 1), (1, 0)])]
  transfers between devices with their start and end apart: 19 -> 18, of which waited for: 8 -> 8; matrix products, arithmetic and copies ran while one was open for 0% -> 0% of each run, Pallas kernels for 10% -> 10%
where the time goes in v5:
time: 88.3 us; the launch traced here: 88 us
  blocking collectives  36.3 us (41%)
  starting transfers between devices  20.7 us (23%)
  Pallas kernels  14.2 us (16%)
  waiting for transfers between devices  13.6 us (15%)
  local copies, waits for them, and re-layouts  3.01 us (3%)
    all_to_all x2, blocking collectives, chips(): lax.all_to_all(shaped, CHIP_AXES, split_axis=0, concat_axis=0, tiled=True)  36.3 us
    ppermute x12, starting transfers between devices, shift(): return lax.ppermute(array, axis, [(i, (i + step) % 4) for i in range(4)])  19.7 us
    ppermute x12, waiting for transfers between devices, shift(): return lax.ppermute(array, axis, [(i, (i + step) % 4) for i in range(4)])  12.4 us
    pallas_call x1, Pallas kernels, expert_part(): pl.pallas_call(expert_kernel, out_shape=jax.ShapeDtypeStruct((TILE_ROWS,...  3.62 us
    pallas_call x1, Pallas kernels, carried_part(): pl.pallas_call(carried_kernel, out_shape=jax.ShapeDtypeStruct((64, SHARD)...  3.15 us
    unnamed x20, local copies, waits for them, and re-layouts  3.01 us
    pallas_call x1, Pallas kernels, map_part(): pl.pallas_call(map_kernel, out_shape=(jax.ShapeDtypeStruct((TILE_ROWS, 25...  1.83 us
  transfers between devices with their start and end apart: 18, of which 8 were waited for; matrix products, arithmetic and copies ran while one was open for 0% of the time, Pallas kernels for 10%

profile of v5, /device:TPU:0, one launch (start us, length us, event | category | flops | bytes accessed | tf_op | source)
XLA Modules:
  0.0 88.0 jit_solution(2975500874563398563)
XLA Ops:
  0.0 0.0 collective-permute-start
  0.0 0.0 copy-start.3
  0.0 1.6 %copy-done.3 = bf16[512,2048]{1,0:T(8,128)(2,1)S(1)} copy-done((bf16[512,2048]{1,0:T(8,128)(2,1)S(1)}, bf16[512,2048]{1,0:T(8,128)(2,1)}, u32[]{:S(2)}) %copy-start.3) | copy-done | bytes 2097176
  1.6 0.7 copy-done.7
  2.3 0.4 norm.1
  2.7 0.0 copy-start
  2.7 0.0 copy-start.2
  2.7 0.0 collective-permute-done.other_ref
  2.7 0.7 copy-done.5
  3.4 0.8 project.1
  4.3 2.9 %collective-permute-start.4 = (bf16[256,256]{1,0:T(8,128)(2,1)S(1)}, bf16[256,256]{1,0:T(8,128)(2,1)S(1)}, u32[]{:S(2)}, u32[]{:S(2)}) collective-permute-start(bf16[256,256]{1,0:T(8,128)(2,1)S(1)} %get-tuple-element.35.kv0), channel_id=1, source_target_pairs={{0,96},{32,0},{64,32},{96,64},{1,97},{33,1},{65,33},{97,65},{2,98}... | collective-permute-start | bytes 393224 | tf_op jit(solution)/shard_map/ppermute | solution.py:28
  7.2 0.2 collective-permute-start.1
  7.4 0.0 copy-done
  7.4 3.2 %collective-permute-start.7 = (bf16[64,2048]{1,0:T(8,128)(2,1)S(1)}, bf16[64,2048]{1,0:T(8,128)(2,1)S(1)}, u32[]{:S(2)}, u32[]{:S(2)}) collective-permute-start(bf16[64,2048]{1,0:T(8,128)(2,1)S(1)} %copy-done), channel_id=1, source_target_pairs={{0,4},{2,6},{4,0},{6,2},{1,5},{3,7},{5,1},{7,3},{8,12},{10,14},{12... | collective-permute-start | bytes 786440 | tf_op jit(solution)/shard_map/ppermute | solution.py:28
  10.6 0.7 collective-permute-start.6
  11.3 2.6 %collective-permute-start.8 = (bf16[64,2048]{1,0:T(8,128)(2,1)S(1)}, bf16[64,2048]{1,0:T(8,128)(2,1)S(1)}, u32[]{:S(2)}, u32[]{:S(2)}) collective-permute-start(bf16[64,2048]{1,0:T(8,128)(2,1)S(1)} %copy-done), channel_id=1, source_target_pairs={{0,6},{2,0},{4,2},{6,4},{1,7},{3,1},{5,3},{7,5},{8,14},{10,8},{12,... | collective-permute-start | bytes 786440 | tf_op jit(solution)/shard_map/ppermute | solution.py:28
  13.8 0.0 collective-permute-done.1.q_other_ref
  13.8 0.8 collective-permute-start.3
  14.6 0.0 collective-permute-done.4.kv3
  14.7 0.9 %collective-permute-start.2 = (bf16[256,256]{1,0:T(8,128)(2,1)S(1)}, bf16[256,256]{1,0:T(8,128)(2,1)S(1)}, u32[]{:S(2)}, u32[]{:S(2)}) collective-permute-start(bf16[256,256]{1,0:T(8,128)(2,1)S(1)} %get-tuple-element.35.kv0), channel_id=1, source_target_pairs={{0,32},{32,64},{64,96},{96,0},{1,33},{33,65},{65,97},{97,1},{2,34}... | collective-permute-start | bytes 393224 | tf_op jit(solution)/shard_map/ppermute | solution.py:28
  15.5 0.0 copy-done.2
  15.5 3.2 %carried.1.carried_ref = f32[64,512]{1,0:T(8,128)S(1)} custom-call(f32[64,8256]{1,0:T(8,128)S(1)} %bitcast.15, bf16[128,256]{1,0:T(8,128)(2,1)S(1)} %get-tuple-element.34.q_own_ref, bf16[128,256]{1,0:T(8,128)(2,1)S(1)} %collective-permute-done.1.q_other_ref), custom_call_target="tpu_custom_call" | custom-call | flops 5000000000 | bytes 15000000 | tf_op jit(solution)/shard_map/carried/pallas_call | solution.py:104
  18.7 0.0 copy-start.1
  18.7 2.9 %collective-permute-done.3.kv2 = bf16[256,256]{1,0:T(8,128)(2,1)S(1)} collective-permute-done((bf16[256,256]{1,0:T(8,128)(2,1)S(1)}, bf16[256,256]{1,0:T(8,128)(2,1)S(1)}, u32[]{:S(2)}, u32[]{:S(2)}) %collective-permute-start.3) | collective-permute-done | bytes 131104 | tf_op jit(solution)/shard_map/ppermute | solution.py:28
  21.6 1.4 %collective-permute-done.2.kv1 = bf16[256,256]{1,0:T(8,128)(2,1)S(1)} collective-permute-done((bf16[256,256]{1,0:T(8,128)(2,1)S(1)}, bf16[256,256]{1,0:T(8,128)(2,1)S(1)}, u32[]{:S(2)}, u32[]{:S(2)}) %collective-permute-start.2) | collective-permute-done | bytes 131104 | tf_op jit(solution)/shard_map/ppermute | solution.py:28
  23.0 1.1 %window.1 = (f32[256,128]{1,0:T(8,128)S(1)}, bf16[256,128]{1,0:T(8,128)(2,1)S(1)}) custom-call(bf16[128,256]{1,0:T(8,128)(2,1)S(1)} %get-tuple-element.34.q_own_ref, bf16[128,256]{1,0:T(8,128)(2,1)S(1)} %collective-permute-done.1.q_other_ref, bf16[256,256]{1,0:T(8,128)(2,1)S(1)} %get-tuple-element.35.kv0, bf16[256,256]{1,0:T(8,128)(2,1)S(1)} %collective-permute-done.2.kv1, ...), custom_call_target="tpu_custom_call" | custom-call | flops 2000000000 | bytes 6000000 | tf_op jit(solution)/shard_map/window/pallas_call | solution.py:150
  24.1 0.0 copy-start.4
  24.1 0.1 collective-permute-start.5
  24.2 0.0 collective-permute-done.7.refs_2_
  24.2 0.0 collective-permute-done.6.refs_1_
  24.2 0.0 collective-permute-done.8.refs_3_
  24.2 1.2 %collective-permute-done.5.received_ref = bf16[256,128]{1,0:T(8,128)(2,1)S(1)} collective-permute-done((bf16[256,128]{1,0:T(8,128)(2,1)S(1)}, bf16[256,128]{1,0:T(8,128)(2,1)S(1)}, u32[]{:S(2)}, u32[]{:S(2)}) %collective-permute-start.5) | collective-permute-done | bytes 65568 | tf_op jit(solution)/shard_map/ppermute | solution.py:24
  25.5 0.0 copy-done.1
  25.5 0.2 collective-permute-start.16
  25.6 0.1 pack.1.rest_4_
  25.7 0.4 collective-permute-start.12
  26.1 0.0 copy-done.4
  26.1 0.2 collective-permute-start.17
  26.3 0.1 attend.1
  26.4 0.1 collective-permute-start.9
  26.5 2.0 %collective-permute-start.10 = (bf16[64,128]{1,0:T(8,128)(2,1)S(1)}, bf16[64,128]{1,0:T(8,128)(2,1)S(1)}, u32[]{:S(2)}, u32[]{:S(2)}) collective-permute-start(bf16[64,128]{1,0:T(8,128)(2,1)S(1)} %get-tuple-element.41), channel_id=1, source_target_pairs={{0,4},{2,6},{4,0},{6,2},{1,5},{3,7},{5,1},{7,3},{8,12},{10,14},{12... | collective-permute-start | bytes 49160 | tf_op jit(solution)/shard_map/ppermute | solution.py:28
  28.5 2.9 %collective-permute-done.9.rest_1_ = bf16[64,128]{1,0:T(8,128)(2,1)S(1)} collective-permute-done((bf16[64,128]{1,0:T(8,128)(2,1)S(1)}, bf16[64,128]{1,0:T(8,128)(2,1)S(1)}, u32[]{:S(2)}, u32[]{:S(2)}) %collective-permute-start.9) | collective-permute-done | bytes 16416 | tf_op jit(solution)/shard_map/ppermute | solution.py:28
  31.4 0.0 collective-permute-start.11
  31.4 0.4 collective-permute-done.10.rest_2_
  31.8 3.4 %collective-permute-done.11.rest_3_ = bf16[64,128]{1,0:T(8,128)(2,1)S(1)} collective-permute-done((bf16[64,128]{1,0:T(8,128)(2,1)S(1)}, bf16[64,128]{1,0:T(8,128)(2,1)S(1)}, u32[]{:S(2)}, u32[]{:S(2)}) %collective-permute-start.11) | collective-permute-done | bytes 16416 | tf_op jit(solution)/shard_map/ppermute | solution.py:28
  35.2 0.0 collective-permute-done.12.rest_5_
  35.2 0.8 output.1
  35.9 2.0 %collective-permute-start.13 = (bf16[16,2048]{1,0:T(8,128)(2,1)S(1)}, bf16[16,2048]{1,0:T(8,128)(2,1)S(1)}, u32[]{:S(2)}, u32[]{:S(2)}) collective-permute-start(bf16[16,2048]{1,0:T(8,128)(2,1)S(1)} %get-tuple-element.48), channel_id=1, source_target_pairs={{0,8},{8,16},{16,24},{24,0},{1,9},{9,17},{17,25},{25,1},{2,10},{10... | collective-permute-start | bytes 196616 | tf_op jit(solution)/shard_map/ppermute | solution.py:28
  37.9 3.6 %collective-permute-start.14 = (bf16[16,2048]{1,0:T(8,128)(2,1)S(1)}, bf16[16,2048]{1,0:T(8,128)(2,1)S(1)}, u32[]{:S(2)}, u32[]{:S(2)}) collective-permute-start(bf16[16,2048]{1,0:T(8,128)(2,1)S(1)} %get-tuple-element.49), channel_id=1, source_target_pairs={{0,16},{8,24},{16,0},{24,8},{1,17},{9,25},{17,1},{25,9},{2,18},{10... | collective-permute-start | bytes 196616 | tf_op jit(solution)/shard_map/ppermute | solution.py:28
  41.5 1.0 %collective-permute-start.15 = (bf16[16,2048]{1,0:T(8,128)(2,1)S(1)}, bf16[16,2048]{1,0:T(8,128)(2,1)S(1)}, u32[]{:S(2)}, u32[]{:S(2)}) collective-permute-start(bf16[16,2048]{1,0:T(8,128)(2,1)S(1)} %get-tuple-element.50), channel_id=1, source_target_pairs={{0,24},{8,0},{16,8},{24,16},{1,25},{9,1},{17,9},{25,17},{2,26},{10... | collective-permute-start | bytes 196616 | tf_op jit(solution)/shard_map/ppermute | solution.py:28
  42.5 0.0 copy-done.8
  42.5 0.0 copy-done.9
  42.5 1.8 %maps.1 = (bf16[3072,256]{1,0:T(8,128)(2,1)S(1)}, f32[16,3072]{1,0:T(8,128)S(1)}, f32[1,2048]{1,0:T(1,128)S(1)}) custom-call(s32[8,16]{1,0:T(8,128)S(1)} %bitcast.22, f32[1,2048]{1,0:T(1,128)S(1)} %bitcast.21), custom_call_target="tpu_custom_call" | custom-call | flops 2000000000 | bytes 6000000 | tf_op jit(solution)/shard_map/maps/pallas_call | solution.py:350
  44.4 0.0 collective-permute-done.13.r1
  44.4 0.1 collective-permute-done.14.r2
  44.5 1.3 %collective-permute-done.15.r3 = bf16[16,2048]{1,0:T(8,128)(2,1)S(1)} collective-permute-done((bf16[16,2048]{1,0:T(8,128)(2,1)S(1)}, bf16[16,2048]{1,0:T(8,128)(2,1)S(1)}, u32[]{:S(2)}, u32[]{:S(2)}) %collective-permute-start.15) | collective-permute-done | bytes 65568 | tf_op jit(solution)/shard_map/ppermute | solution.py:28
  45.8 0.0 copy-done.6
  45.8 1.0 %dispatch.1 = (f32[16,2048]{1,0:T(8,128)S(1)}, bf16[3072,128]{1,0:T(8,128)(2,1)S(1)}, f32[16,3072]{1,0:T(8,128)S(1)}) custom-call(bf16[16,2048]{1,0:T(8,128)(2,1)S(1)} %get-tuple-element.32.slab_ref, f32[16,2048]{1,0:T(8,128)S(1)} %get-tuple-element.47.own_ref, bf16[16,2048]{1,0:T(8,128)(2,1)S(1)} %collective-permute-done.13.r1, ...), custom_call_target="tpu_custom_call" | custom-call | flops 1000000000 | bytes 3000000 | tf_op jit(solution)/shard_map/dispatch/pallas_call | solution.py:388
  46.8 18.7 %all_to_all.10 = bf16[64,48,128]{2,1,0:T(8,128)(2,1)S(1)} all-to-all(bf16[64,48,128]{2,1,0:T(8,128)(2,1)S(1)} %bitcast.11), channel_id=1, replica_groups=mesh['x'=4,'z'=4,'y'=4,'c'=2] {'x','z','y'}, dimensions={0} | all-to-all | bytes 1572864 | tf_op jit(solution)/shard_map/all_to_all | solution.py:474
  65.5 0.0 collective-permute-done.17.second_other
  65.5 0.0 collective-permute-done.16.first_other
  65.5 3.6 %experts.1 = bf16[3072,128]{1,0:T(8,128)(2,1)S(1)} custom-call(bf16[3072,128]{1,0:T(8,128)(2,1)S(1)} %bitcast.12, bf16[2,2048,512]{2,1,0:T(8,128)(2,1)S(1)} %copy-done.1, bf16[512,2048]{1,0:T(8,128)(2,1)S(1)} %copy-done.4, bf16[2,2048,512]{2,1,0:T(8,128)(2,1)S(1)} %collective-permute-done.16.first_other, ...), custom_call_target="tpu_custom_call" | custom-call | flops 5000000000 | bytes 15000000 | tf_op jit(solution)/shard_map/experts/pallas_call | solution.py:428
  69.2 17.6 %all_to_all.11 = bf16[64,48,128]{2,1,0:T(8,128)(2,1)S(1)} all-to-all(bf16[64,48,128]{2,1,0:T(8,128)(2,1)S(1)} %bitcast.14), channel_id=1, replica_groups=mesh['x'=4,'z'=4,'y'=4,'c'=2] {'x','z','y'}, dimensions={0} | all-to-all | bytes 1572864 | tf_op jit(solution)/shard_map/all_to_all | solution.py:474
  86.8 1.2 %combine.1 = bf16[16,2048]{1,0:T(8,128)(2,1)} custom-call(f32[16,2048]{1,0:T(8,128)S(1)} %get-tuple-element.54.residual_ref, f32[16,3072]{1,0:T(8,128)S(1)} %get-tuple-element.55.wide_ref, bf16[3072,128]{1,0:T(8,128)(2,1)S(1)} %bitcast.13), custom_call_target="tpu_custom_call" | custom-call | flops 1000000000 | bytes 3000000 | tf_op jit(solution)/shard_map/combine/pallas_call | solution.py:460
  (5 shorter events, 0.0 us)
Async XLA Ops:
  0.0 2.7 %collective-permute-start = (bf16[3,64,2048]{2,1,0:T(8,128)(2,1)}, bf16[3,64,2048]{2,1,0:T(8,128)(2,1)S(1)}, u32[]{:S(2)}, u32[]{:S(2)}) collective-permute-start(bf16[3,64,2048]{2,1,0:T(8,128)(2,1)} %bitcast.17), channel_id=1, source_target_pairs={{0,1},{1,0},{2,3},{3,2},{4,5},{5,4},{6,7},{7,6},{8,9},{9,8},{10,11... | collective-permute-start | bytes 2359304 | tf_op jit(solution)/shard_map/ppermute | solution.py:24
  0.0 1.6 %copy-start.3 = (bf16[512,2048]{1,0:T(8,128)(2,1)S(1)}, bf16[512,2048]{1,0:T(8,128)(2,1)}, u32[]{:S(2)}) copy-start(bf16[512,2048]{1,0:T(8,128)(2,1)} %param.10) | copy-start | bytes 6291460
  1.6 0.7 copy-start.7
  2.3 1.1 %copy-start.5 = (bf16[3,2048,64]{1,2,0:T(8,128)(2,1)S(1)}, bf16[3,2048,64]{1,2,0:T(8,128)(2,1)}, u32[]{:S(2)}) copy-start(bf16[3,2048,64]{1,2,0:T(8,128)(2,1)} %param.12) | copy-start | bytes 2359300
  2.7 4.7 %copy-start = (bf16[64,2048]{1,0:T(8,128)(2,1)S(1)}, bf16[64,2048]{1,0:T(8,128)(2,1)}, u32[]{:S(2)}) copy-start(bf16[64,2048]{1,0:T(8,128)(2,1)} %refs_0_) | copy-start | bytes 786436
  2.7 12.8 %copy-start.2 = (f32[8256,64]{0,1:T(8,128)S(1)}, f32[8256,64]{0,1:T(8,128)}, u32[]{:S(2)}) copy-start(f32[8256,64]{0,1:T(8,128)} %param.13) | copy-start | bytes 6340612
  4.3 10.4 %collective-permute-start.4 = (bf16[256,256]{1,0:T(8,128)(2,1)S(1)}, bf16[256,256]{1,0:T(8,128)(2,1)S(1)}, u32[]{:S(2)}, u32[]{:S(2)}) collective-permute-start(bf16[256,256]{1,0:T(8,128)(2,1)S(1)} %get-tuple-element.35.kv0), channel_id=1, source_target_pairs={{0,96},{32,0},{64,32},{96,64},{1,97},{33,1},{65,33},{97,65},{2,98}... | collective-permute-start | bytes 393224 | tf_op jit(solution)/shard_map/ppermute | solution.py:28
  7.2 6.7 %collective-permute-start.1 = (bf16[128,256]{1,0:T(8,128)(2,1)S(1)}, bf16[128,256]{1,0:T(8,128)(2,1)S(1)}, u32[]{:S(2)}, u32[]{:S(2)}) collective-permute-start(bf16[128,256]{1,0:T(8,128)(2,1)S(1)} %get-tuple-element.34.q_own_ref), channel_id=1, source_target_pairs={{0,1},{1,0},{2,3},{3,2},{4,5},{5,4},{6,7},{7,6},{8,9},{9,8},{10,11... | collective-permute-start | bytes 196616 | tf_op jit(solution)/shard_map/ppermute | solution.py:24
  7.4 16.8 %collective-permute-start.7 = (bf16[64,2048]{1,0:T(8,128)(2,1)S(1)}, bf16[64,2048]{1,0:T(8,128)(2,1)S(1)}, u32[]{:S(2)}, u32[]{:S(2)}) collective-permute-start(bf16[64,2048]{1,0:T(8,128)(2,1)S(1)} %copy-done), channel_id=1, source_target_pairs={{0,4},{2,6},{4,0},{6,2},{1,5},{3,7},{5,1},{7,3},{8,12},{10,14},{12... | collective-permute-start | bytes 786440 | tf_op jit(solution)/shard_map/ppermute | solution.py:28
  10.6 13.6 %collective-permute-start.6 = (bf16[64,2048]{1,0:T(8,128)(2,1)S(1)}, bf16[64,2048]{1,0:T(8,128)(2,1)S(1)}, u32[]{:S(2)}, u32[]{:S(2)}) collective-permute-start(bf16[64,2048]{1,0:T(8,128)(2,1)S(1)} %copy-done), channel_id=1, source_target_pairs={{0,2},{2,4},{4,6},{6,0},{1,3},{3,5},{5,7},{7,1},{8,10},{10,12},{12... | collective-permute-start | bytes 786440 | tf_op jit(solution)/shard_map/ppermute | solution.py:28
  11.3 13.0 %collective-permute-start.8 = (bf16[64,2048]{1,0:T(8,128)(2,1)S(1)}, bf16[64,2048]{1,0:T(8,128)(2,1)S(1)}, u32[]{:S(2)}, u32[]{:S(2)}) collective-permute-start(bf16[64,2048]{1,0:T(8,128)(2,1)S(1)} %copy-done), channel_id=1, source_target_pairs={{0,6},{2,0},{4,2},{6,4},{1,7},{3,1},{5,3},{7,5},{8,14},{10,8},{12,... | collective-permute-start | bytes 786440 | tf_op jit(solution)/shard_map/ppermute | solution.py:28
  13.8 7.8 %collective-permute-start.3 = (bf16[256,256]{1,0:T(8,128)(2,1)S(1)}, bf16[256,256]{1,0:T(8,128)(2,1)S(1)}, u32[]{:S(2)}, u32[]{:S(2)}) collective-permute-start(bf16[256,256]{1,0:T(8,128)(2,1)S(1)} %get-tuple-element.35.kv0), channel_id=1, source_target_pairs={{0,64},{32,96},{64,0},{96,32},{1,65},{33,97},{65,1},{97,33},{2,66}... | collective-permute-start | bytes 393224 | tf_op jit(solution)/shard_map/ppermute | solution.py:28
  14.7 8.4 %collective-permute-start.2 = (bf16[256,256]{1,0:T(8,128)(2,1)S(1)}, bf16[256,256]{1,0:T(8,128)(2,1)S(1)}, u32[]{:S(2)}, u32[]{:S(2)}) collective-permute-start(bf16[256,256]{1,0:T(8,128)(2,1)S(1)} %get-tuple-element.35.kv0), channel_id=1, source_target_pairs={{0,32},{32,64},{64,96},{96,0},{1,33},{33,65},{65,97},{97,1},{2,34}... | collective-permute-start | bytes 393224 | tf_op jit(solution)/shard_map/ppermute | solution.py:28
  18.7 6.8 %copy-start.1 = (bf16[2,2048,512]{2,1,0:T(8,128)(2,1)S(1)}, bf16[2,2048,512]{2,1,0:T(8,128)(2,1)}, u32[]{:S(2)}) copy-start(bf16[2,2048,512]{2,1,0:T(8,128)(2,1)} %first_own.1) | copy-start | bytes 12582916
  24.1 2.0 %copy-start.4 = (bf16[512,2048]{1,0:T(8,128)(2,1)S(1)}, bf16[512,2048]{1,0:T(8,128)(2,1)}, u32[]{:S(2)}) copy-start(bf16[512,2048]{1,0:T(8,128)(2,1)} %second_own.1) | copy-start | bytes 6291460
  24.1 1.3 %collective-permute-start.5 = (bf16[256,128]{1,0:T(8,128)(2,1)S(1)}, bf16[256,128]{1,0:T(8,128)(2,1)S(1)}, u32[]{:S(2)}, u32[]{:S(2)}) collective-permute-start(bf16[256,128]{1,0:T(8,128)(2,1)S(1)} %get-tuple-element.37), channel_id=1, source_target_pairs={{0,1},{1,0},{2,3},{3,2},{4,5},{5,4},{6,7},{7,6},{8,9},{9,8},{10,11... | collective-permute-start | bytes 196616 | tf_op jit(solution)/shard_map/ppermute | solution.py:24
  25.5 40.1 %collective-permute-start.16 = (bf16[2,2048,512]{2,1,0:T(8,128)(2,1)S(1)}, bf16[2,2048,512]{2,1,0:T(8,128)(2,1)S(1)}, u32[]{:S(2)}, u32[]{:S(2)}) collective-permute-start(bf16[2,2048,512]{2,1,0:T(8,128)(2,1)S(1)} %copy-done.1), channel_id=1, source_target_pairs={{0,1},{1,0},{2,3},{3,2},{4,5},{5,4},{6,7},{7,6},{8,9},{9,8},{10,11... | collective-permute-start | bytes 12582920 | tf_op jit(solution)/shard_map/ppermute | solution.py:24
  25.7 9.5 %collective-permute-start.12 = (bf16[256,2048]{1,0:T(8,128)(2,1)S(1)}, bf16[256,2048]{1,0:T(8,128)(2,1)S(1)}, u32[]{:S(2)}, u32[]{:S(2)}) collective-permute-start(bf16[256,2048]{1,0:T(8,128)(2,1)S(1)} %pack.1.rest_4_), channel_id=1, source_target_pairs={{0,1},{1,0},{2,3},{3,2},{4,5},{5,4},{6,7},{7,6},{8,9},{9,8},{10,11... | collective-permute-start | bytes 3145736 | tf_op jit(solution)/shard_map/ppermute | solution.py:24
  26.1 39.4 %collective-permute-start.17 = (bf16[512,2048]{1,0:T(8,128)(2,1)S(1)}, bf16[512,2048]{1,0:T(8,128)(2,1)S(1)}, u32[]{:S(2)}, u32[]{:S(2)}) collective-permute-start(bf16[512,2048]{1,0:T(8,128)(2,1)S(1)} %copy-done.4), channel_id=1, source_target_pairs={{0,1},{1,0},{2,3},{3,2},{4,5},{5,4},{6,7},{7,6},{8,9},{9,8},{10,11... | collective-permute-start | bytes 6291464 | tf_op jit(solution)/shard_map/ppermute | solution.py:24
  26.4 5.0 %collective-permute-start.9 = (bf16[64,128]{1,0:T(8,128)(2,1)S(1)}, bf16[64,128]{1,0:T(8,128)(2,1)S(1)}, u32[]{:S(2)}, u32[]{:S(2)}) collective-permute-start(bf16[64,128]{1,0:T(8,128)(2,1)S(1)} %get-tuple-element.40), channel_id=1, source_target_pairs={{0,2},{2,4},{4,6},{6,0},{1,3},{3,5},{5,7},{7,1},{8,10},{10,12},{12... | collective-permute-start | bytes 49160 | tf_op jit(solution)/shard_map/ppermute | solution.py:28
  26.5 5.3 %collective-permute-start.10 = (bf16[64,128]{1,0:T(8,128)(2,1)S(1)}, bf16[64,128]{1,0:T(8,128)(2,1)S(1)}, u32[]{:S(2)}, u32[]{:S(2)}) collective-permute-start(bf16[64,128]{1,0:T(8,128)(2,1)S(1)} %get-tuple-element.41), channel_id=1, source_target_pairs={{0,4},{2,6},{4,0},{6,2},{1,5},{3,7},{5,1},{7,3},{8,12},{10,14},{12... | collective-permute-start | bytes 49160 | tf_op jit(solution)/shard_map/ppermute | solution.py:28
  31.4 3.7 %collective-permute-start.11 = (bf16[64,128]{1,0:T(8,128)(2,1)S(1)}, bf16[64,128]{1,0:T(8,128)(2,1)S(1)}, u32[]{:S(2)}, u32[]{:S(2)}) collective-permute-start(bf16[64,128]{1,0:T(8,128)(2,1)S(1)} %get-tuple-element.42), channel_id=1, source_target_pairs={{0,6},{2,0},{4,2},{6,4},{1,7},{3,1},{5,3},{7,5},{8,14},{10,8},{12,... | collective-permute-start | bytes 49160 | tf_op jit(solution)/shard_map/ppermute | solution.py:28
  35.2 7.3 %copy-start.8 = (f32[2048]{0:T(1024)S(1)}, f32[2048]{0:T(1024)}, u32[]{:S(2)}) copy-start(f32[2048]{0:T(1024)} %param.15) | copy-start | bytes 24580
  35.2 7.3 %copy-start.9 = (s32[16,8]{0,1:T(8,128)S(1)}, s32[16,8]{0,1:T(8,128)}, u32[]{:S(2)}) copy-start(s32[16,8]{0,1:T(8,128)} %param.17) | copy-start | bytes 1540
  35.9 8.4 %collective-permute-start.13 = (bf16[16,2048]{1,0:T(8,128)(2,1)S(1)}, bf16[16,2048]{1,0:T(8,128)(2,1)S(1)}, u32[]{:S(2)}, u32[]{:S(2)}) collective-permute-start(bf16[16,2048]{1,0:T(8,128)(2,1)S(1)} %get-tuple-element.48), channel_id=1, source_target_pairs={{0,8},{8,16},{16,24},{24,0},{1,9},{9,17},{17,25},{25,1},{2,10},{10... | collective-permute-start | bytes 196616 | tf_op jit(solution)/shard_map/ppermute | solution.py:28
  37.9 6.5 %collective-permute-start.14 = (bf16[16,2048]{1,0:T(8,128)(2,1)S(1)}, bf16[16,2048]{1,0:T(8,128)(2,1)S(1)}, u32[]{:S(2)}, u32[]{:S(2)}) collective-permute-start(bf16[16,2048]{1,0:T(8,128)(2,1)S(1)} %get-tuple-element.49), channel_id=1, source_target_pairs={{0,16},{8,24},{16,0},{24,8},{1,17},{9,25},{17,1},{25,9},{2,18},{10... | collective-permute-start | bytes 196616 | tf_op jit(solution)/shard_map/ppermute | solution.py:28
  41.5 4.3 %collective-permute-start.15 = (bf16[16,2048]{1,0:T(8,128)(2,1)S(1)}, bf16[16,2048]{1,0:T(8,128)(2,1)S(1)}, u32[]{:S(2)}, u32[]{:S(2)}) collective-permute-start(bf16[16,2048]{1,0:T(8,128)(2,1)S(1)} %get-tuple-element.50), channel_id=1, source_target_pairs={{0,24},{8,0},{16,8},{24,16},{1,25},{9,1},{17,9},{25,17},{2,26},{10... | collective-permute-start | bytes 196616 | tf_op jit(solution)/shard_map/ppermute | solution.py:28
  42.5 3.3 %copy-start.6 = (bf16[2048,64]{0,1:T(8,128)(2,1)S(1)}, bf16[2048,64]{0,1:T(8,128)(2,1)}, u32[]{:S(2)}) copy-start(bf16[2048,64]{0,1:T(8,128)(2,1)} %param.16) | copy-start | bytes 786436

commit v6 on v5

--- a/solution.py
+++ b/solution.py
@@ -161,32 +161,32 @@
     )(q_own, q_other, *kvs, carried)
 
 
-def norm_kernel(tokens_ref, gain_ref, out_ref, slab_ref):
+def norm_kernel(tokens_ref, out_ref, slab_ref):
     core = lax.axis_index("c")
     slab_ref[...] = tokens_ref[lax.axis_index("z") * 4 + lax.axis_index("y"), core]
     for k in range(4):
         floats = tokens_ref[4 * k : 4 * k + 4, core].astype(jnp.float32).reshape(64, D)
-        out_ref[64 * k : 64 * k + 64, :] = norm_scaled(floats, gain_ref[...]).astype(jnp.bfloat16)
-
-
-def norm_part(tokens, gain):
+        out_ref[64 * k : 64 * k + 64, :] = norm_scaled(floats, 1.0)
+
+
+def norm_part(tokens):
     return pl.pallas_call(
         norm_kernel,
         out_shape=(
-            jax.ShapeDtypeStruct((HALF, D), jnp.bfloat16),
+            jax.ShapeDtypeStruct((HALF, D), jnp.float32),
             jax.ShapeDtypeStruct((SLAB, D), jnp.bfloat16),
         ),
-        in_specs=[VMEM, VMEM],
+        in_specs=[VMEM],
         out_specs=(VMEM, VMEM),
         compiler_params=room(2),
         cost_estimate=cost(1),
         name="norm",
-    )(tokens.reshape(16, 2, 16, D), gain.reshape(1, D))
-
-
-def project_kernel(normed_ref, own_ref, other_ref, q_ref, kv_ref):
+    )(tokens.reshape(16, 2, 16, D))
+
+
+def project_kernel(normed_ref, gain_ref, own_ref, other_ref, q_ref, kv_ref):
     core = lax.axis_index("c")
-    normed = normed_ref[...]
+    normed = (normed_ref[...] * gain_ref[...]).astype(jnp.bfloat16)
 
     def times(ref):
         return lax.dot_general(
@@ -207,19 +207,19 @@
     kv_ref[192:256, :] = other[128:]
 
 
-def project_part(normed, own, other):
+def project_part(normed, gain, own, other):
     return pl.pallas_call(
         project_kernel,
         out_shape=(
             jax.ShapeDtypeStruct((HD, HALF), jnp.bfloat16),
             jax.ShapeDtypeStruct((2 * HD, HALF), jnp.bfloat16),
         ),
-        in_specs=[VMEM, VMEM, VMEM],
+        in_specs=[VMEM] * 4,
         out_specs=(VMEM, VMEM),
-        compiler_params=room(2),
+        compiler_params=room(4),
         cost_estimate=cost(1),
         name="project",
-    )(normed, own, other)
+    )(normed, gain.reshape(1, D), own, other)
 
 
 def attend_kernel(mine_ref, received_ref, *rest):
@@ -490,10 +490,11 @@
 ):
     own_weights = head_weights.transpose(0, 2, 1)
     other_weights = swap_core(own_weights)
-    output_own = [output_weight] + [shift(output_weight, "y", step) for step in (1, 2, 3)]
-    normed, slab = norm_part(tokens, attention_gain)
-    q_own, kv = project_part(normed, own_weights, other_weights)
+    normed, slab = norm_part(tokens)
+    q_own, kv = project_part(normed, attention_gain, own_weights, other_weights)
     kvs = [kv] + [shift(kv, "x", step) for step in (1, 2, 3)]
+    gathered = {step: shift(output_weight, "y", step) for step in (1, 3, 2)}
+    output_own = [output_weight, gathered[1], gathered[2], gathered[3]]
     q_other = swap_core(q_own)
     rows_map, lanes_map, gain = map_part(expert_index.T, expert_gain)
 

time: 88.3 us -> 87.5 us (level)
  local copies, waits for them, and re-layouts: 3.01 us -> 1.86 us
    unnamed x20, local copies, waits for them, and re-layouts: 3.01 us -> 1.86 us
  transfers between devices with their start and end apart: 18 -> 18, of which waited for: 8 -> 9; matrix products, arithmetic and copies ran while one was open for 0% -> 0% of each run, Pallas kernels for 10% -> 10%
where the time goes in v6:
time: 87.5 us; the launch traced here: 87.3 us
  blocking collectives  36.3 us (41%)
  starting transfers between devices  20.7 us (24%)
  Pallas kernels  14.1 us (16%)
  waiting for transfers between devices  14.1 us (16%)
  local copies, waits for them, and re-layouts  1.86 us (2%)
    all_to_all x2, blocking collectives, chips(): lax.all_to_all(shaped, CHIP_AXES, split_axis=0, concat_axis=0, tiled=True)  36.3 us
    ppermute x12, starting transfers between devices, shift(): return lax.ppermute(array, axis, [(i, (i + step) % 4) for i in range(4)])  19.7 us
    ppermute x12, waiting for transfers between devices, shift(): return lax.ppermute(array, axis, [(i, (i + step) % 4) for i in range(4)])  12.4 us
    pallas_call x1, Pallas kernels, expert_part(): pl.pallas_call(expert_kernel, out_shape=jax.ShapeDtypeStruct((TILE_ROWS,...  3.62 us
    pallas_call x1, Pallas kernels, carried_part(): pl.pallas_call(carried_kernel, out_shape=jax.ShapeDtypeStruct((64, SHARD)...  3.17 us
    unnamed x20, local copies, waits for them, and re-layouts  1.86 us
    pallas_call x1, Pallas kernels, map_part(): pl.pallas_call(map_kernel, out_shape=(jax.ShapeDtypeStruct((TILE_ROWS, 25...  1.83 us
  transfers between devices with their start and end apart: 18, of which 9 were waited for; matrix products, arithmetic and copies ran while one was open for 0% of the time, Pallas kernels for 10%

profile of v6, /device:TPU:0, one launch (start us, length us, event | category | flops | bytes accessed | tf_op | source)
XLA Modules:
  0.0 87.3 jit_solution(5770416007830224931)
XLA Ops:
  0.0 0.0 collective-permute-start
  0.0 0.0 copy-start.3
  0.0 1.6 %copy-done.3 = bf16[512,2048]{1,0:T(8,128)(2,1)S(1)} copy-done((bf16[512,2048]{1,0:T(8,128)(2,1)S(1)}, bf16[512,2048]{1,0:T(8,128)(2,1)}, u32[]{:S(2)}) %copy-start.3) | copy-done | bytes 2097176
  1.6 0.4 norm.1
  2.0 0.0 copy-start
  2.0 0.0 copy-start.2
  2.0 0.5 collective-permute-done.other_ref
  2.5 0.2 copy-done.5
  2.7 0.0 copy-done.7
  2.7 0.8 project.1
  3.6 2.9 %collective-permute-start.4 = (bf16[256,256]{1,0:T(8,128)(2,1)S(1)}, bf16[256,256]{1,0:T(8,128)(2,1)S(1)}, u32[]{:S(2)}, u32[]{:S(2)}) collective-permute-start(bf16[256,256]{1,0:T(8,128)(2,1)S(1)} %get-tuple-element.35.kv0), channel_id=1, source_target_pairs={{0,96},{32,0},{64,32},{96,64},{1,97},{33,1},{65,33},{97,65},{2,98}... | collective-permute-start | bytes 393224 | tf_op jit(solution)/shard_map/ppermute | solution.py:28
  6.5 0.2 collective-permute-start.1
  6.7 0.0 copy-done
  6.7 3.2 %collective-permute-start.7 = (bf16[64,2048]{1,0:T(8,128)(2,1)S(1)}, bf16[64,2048]{1,0:T(8,128)(2,1)S(1)}, u32[]{:S(2)}, u32[]{:S(2)}) collective-permute-start(bf16[64,2048]{1,0:T(8,128)(2,1)S(1)} %copy-done), channel_id=1, source_target_pairs={{0,4},{2,6},{4,0},{6,2},{1,5},{3,7},{5,1},{7,3},{8,12},{10,14},{12... | collective-permute-start | bytes 786440 | tf_op jit(solution)/shard_map/ppermute | solution.py:28
  9.9 0.7 collective-permute-start.6
  10.6 2.6 %collective-permute-start.8 = (bf16[64,2048]{1,0:T(8,128)(2,1)S(1)}, bf16[64,2048]{1,0:T(8,128)(2,1)S(1)}, u32[]{:S(2)}, u32[]{:S(2)}) collective-permute-start(bf16[64,2048]{1,0:T(8,128)(2,1)S(1)} %copy-done), channel_id=1, source_target_pairs={{0,6},{2,0},{4,2},{6,4},{1,7},{3,1},{5,3},{7,5},{8,14},{10,8},{12,... | collective-permute-start | bytes 786440 | tf_op jit(solution)/shard_map/ppermute | solution.py:28
  13.2 0.0 collective-permute-done.1.q_other_ref
  13.2 0.8 collective-permute-start.3
  14.0 0.0 collective-permute-done.4.kv3
  14.0 0.9 %collective-permute-start.2 = (bf16[256,256]{1,0:T(8,128)(2,1)S(1)}, bf16[256,256]{1,0:T(8,128)(2,1)S(1)}, u32[]{:S(2)}, u32[]{:S(2)}) collective-permute-start(bf16[256,256]{1,0:T(8,128)(2,1)S(1)} %get-tuple-element.35.kv0), channel_id=1, source_target_pairs={{0,32},{32,64},{64,96},{96,0},{1,33},{33,65},{65,97},{97,1},{2,34}... | collective-permute-start | bytes 393224 | tf_op jit(solution)/shard_map/ppermute | solution.py:28
  14.8 0.0 copy-done.2
  14.8 3.2 %carried.1.carried_ref = f32[64,512]{1,0:T(8,128)S(1)} custom-call(f32[64,8256]{1,0:T(8,128)S(1)} %bitcast.15, bf16[128,256]{1,0:T(8,128)(2,1)S(1)} %get-tuple-element.34.q_own_ref, bf16[128,256]{1,0:T(8,128)(2,1)S(1)} %collective-permute-done.1.q_other_ref), custom_call_target="tpu_custom_call" | custom-call | flops 5000000000 | bytes 15000000 | tf_op jit(solution)/shard_map/carried/pallas_call | solution.py:104
  18.0 0.0 copy-start.1
  18.0 2.9 %collective-permute-done.3.kv2 = bf16[256,256]{1,0:T(8,128)(2,1)S(1)} collective-permute-done((bf16[256,256]{1,0:T(8,128)(2,1)S(1)}, bf16[256,256]{1,0:T(8,128)(2,1)S(1)}, u32[]{:S(2)}, u32[]{:S(2)}) %collective-permute-start.3) | collective-permute-done | bytes 131104 | tf_op jit(solution)/shard_map/ppermute | solution.py:28
  20.9 1.4 %collective-permute-done.2.kv1 = bf16[256,256]{1,0:T(8,128)(2,1)S(1)} collective-permute-done((bf16[256,256]{1,0:T(8,128)(2,1)S(1)}, bf16[256,256]{1,0:T(8,128)(2,1)S(1)}, u32[]{:S(2)}, u32[]{:S(2)}) %collective-permute-start.2) | collective-permute-done | bytes 131104 | tf_op jit(solution)/shard_map/ppermute | solution.py:28
  22.3 1.1 %window.1 = (f32[256,128]{1,0:T(8,128)S(1)}, bf16[256,128]{1,0:T(8,128)(2,1)S(1)}) custom-call(bf16[128,256]{1,0:T(8,128)(2,1)S(1)} %get-tuple-element.34.q_own_ref, bf16[128,256]{1,0:T(8,128)(2,1)S(1)} %collective-permute-done.1.q_other_ref, bf16[256,256]{1,0:T(8,128)(2,1)S(1)} %get-tuple-element.35.kv0, bf16[256,256]{1,0:T(8,128)(2,1)S(1)} %collective-permute-done.2.kv1, ...), custom_call_target="tpu_custom_call" | custom-call | flops 2000000000 | bytes 6000000 | tf_op jit(solution)/shard_map/window/pallas_call | solution.py:150
  23.4 0.0 copy-start.4
  23.4 0.1 collective-permute-start.5
  23.5 0.0 collective-permute-done.7.refs_2_
  23.5 0.0 collective-permute-done.6.refs_1_
  23.6 0.0 collective-permute-done.8.refs_3_
  23.6 1.2 %collective-permute-done.5.received_ref = bf16[256,128]{1,0:T(8,128)(2,1)S(1)} collective-permute-done((bf16[256,128]{1,0:T(8,128)(2,1)S(1)}, bf16[256,128]{1,0:T(8,128)(2,1)S(1)}, u32[]{:S(2)}, u32[]{:S(2)}) %collective-permute-start.5) | collective-permute-done | bytes 65568 | tf_op jit(solution)/shard_map/ppermute | solution.py:24
  24.8 0.0 copy-done.1
  24.8 0.2 collective-permute-start.16
  24.9 0.1 pack.1.rest_4_
  25.0 0.4 collective-permute-start.12
  25.4 0.0 copy-done.4
  25.4 0.2 collective-permute-start.17
  25.6 0.1 attend.1
  25.7 0.1 collective-permute-start.9
  25.8 2.0 %collective-permute-start.10 = (bf16[64,128]{1,0:T(8,128)(2,1)S(1)}, bf16[64,128]{1,0:T(8,128)(2,1)S(1)}, u32[]{:S(2)}, u32[]{:S(2)}) collective-permute-start(bf16[64,128]{1,0:T(8,128)(2,1)S(1)} %get-tuple-element.41), channel_id=1, source_target_pairs={{0,4},{2,6},{4,0},{6,2},{1,5},{3,7},{5,1},{7,3},{8,12},{10,14},{12... | collective-permute-start | bytes 49160 | tf_op jit(solution)/shard_map/ppermute | solution.py:28
  27.8 3.0 %collective-permute-done.9.rest_1_ = bf16[64,128]{1,0:T(8,128)(2,1)S(1)} collective-permute-done((bf16[64,128]{1,0:T(8,128)(2,1)S(1)}, bf16[64,128]{1,0:T(8,128)(2,1)S(1)}, u32[]{:S(2)}, u32[]{:S(2)}) %collective-permute-start.9) | collective-permute-done | bytes 16416 | tf_op jit(solution)/shard_map/ppermute | solution.py:28
  30.8 0.0 collective-permute-start.11
  30.8 0.4 collective-permute-done.10.rest_2_
  31.1 3.4 %collective-permute-done.11.rest_3_ = bf16[64,128]{1,0:T(8,128)(2,1)S(1)} collective-permute-done((bf16[64,128]{1,0:T(8,128)(2,1)S(1)}, bf16[64,128]{1,0:T(8,128)(2,1)S(1)}, u32[]{:S(2)}, u32[]{:S(2)}) %collective-permute-start.11) | collective-permute-done | bytes 16416 | tf_op jit(solution)/shard_map/ppermute | solution.py:28
  34.5 0.0 collective-permute-done.12.rest_5_
  34.5 0.8 output.1
  35.3 2.0 %collective-permute-start.13 = (bf16[16,2048]{1,0:T(8,128)(2,1)S(1)}, bf16[16,2048]{1,0:T(8,128)(2,1)S(1)}, u32[]{:S(2)}, u32[]{:S(2)}) collective-permute-start(bf16[16,2048]{1,0:T(8,128)(2,1)S(1)} %get-tuple-element.48), channel_id=1, source_target_pairs={{0,8},{8,16},{16,24},{24,0},{1,9},{9,17},{17,25},{25,1},{2,10},{10... | collective-permute-start | bytes 196616 | tf_op jit(solution)/shard_map/ppermute | solution.py:28
  37.2 3.6 %collective-permute-start.14 = (bf16[16,2048]{1,0:T(8,128)(2,1)S(1)}, bf16[16,2048]{1,0:T(8,128)(2,1)S(1)}, u32[]{:S(2)}, u32[]{:S(2)}) collective-permute-start(bf16[16,2048]{1,0:T(8,128)(2,1)S(1)} %get-tuple-element.49), channel_id=1, source_target_pairs={{0,16},{8,24},{16,0},{24,8},{1,17},{9,25},{17,1},{25,9},{2,18},{10... | collective-permute-start | bytes 196616 | tf_op jit(solution)/shard_map/ppermute | solution.py:28
  40.8 1.0 %collective-permute-start.15 = (bf16[16,2048]{1,0:T(8,128)(2,1)S(1)}, bf16[16,2048]{1,0:T(8,128)(2,1)S(1)}, u32[]{:S(2)}, u32[]{:S(2)}) collective-permute-start(bf16[16,2048]{1,0:T(8,128)(2,1)S(1)} %get-tuple-element.50), channel_id=1, source_target_pairs={{0,24},{8,0},{16,8},{24,16},{1,25},{9,1},{17,9},{25,17},{2,26},{10... | collective-permute-start | bytes 196616 | tf_op jit(solution)/shard_map/ppermute | solution.py:28
  41.9 0.0 copy-done.8
  41.9 0.0 copy-done.9
  41.9 1.8 %maps.1 = (bf16[3072,256]{1,0:T(8,128)(2,1)S(1)}, f32[16,3072]{1,0:T(8,128)S(1)}, f32[1,2048]{1,0:T(1,128)S(1)}) custom-call(s32[8,16]{1,0:T(8,128)S(1)} %bitcast.22, f32[1,2048]{1,0:T(1,128)S(1)} %bitcast.21), custom_call_target="tpu_custom_call" | custom-call | flops 2000000000 | bytes 6000000 | tf_op jit(solution)/shard_map/maps/pallas_call | solution.py:350
  43.7 0.0 collective-permute-done.13.r1
  43.7 0.1 collective-permute-done.14.r2
  43.8 1.3 %collective-permute-done.15.r3 = bf16[16,2048]{1,0:T(8,128)(2,1)S(1)} collective-permute-done((bf16[16,2048]{1,0:T(8,128)(2,1)S(1)}, bf16[16,2048]{1,0:T(8,128)(2,1)S(1)}, u32[]{:S(2)}, u32[]{:S(2)}) %collective-permute-start.15) | collective-permute-done | bytes 65568 | tf_op jit(solution)/shard_map/ppermute | solution.py:28
  45.1 0.0 copy-done.6
  45.1 1.1 %dispatch.1 = (f32[16,2048]{1,0:T(8,128)S(1)}, bf16[3072,128]{1,0:T(8,128)(2,1)S(1)}, f32[16,3072]{1,0:T(8,128)S(1)}) custom-call(bf16[16,2048]{1,0:T(8,128)(2,1)S(1)} %get-tuple-element.32.slab_ref, f32[16,2048]{1,0:T(8,128)S(1)} %get-tuple-element.47.own_ref, bf16[16,2048]{1,0:T(8,128)(2,1)S(1)} %collective-permute-done.13.r1, ...), custom_call_target="tpu_custom_call" | custom-call | flops 1000000000 | bytes 3000000 | tf_op jit(solution)/shard_map/dispatch/pallas_call | solution.py:388
  46.2 18.7 %all_to_all.10 = bf16[64,48,128]{2,1,0:T(8,128)(2,1)S(1)} all-to-all(bf16[64,48,128]{2,1,0:T(8,128)(2,1)S(1)} %bitcast.11), channel_id=1, replica_groups=mesh['x'=4,'z'=4,'y'=4,'c'=2] {'x','z','y'}, dimensions={0} | all-to-all | bytes 1572864 | tf_op jit(solution)/shard_map/all_to_all | solution.py:474
  64.8 0.0 collective-permute-done.17.second_other
  64.8 0.0 collective-permute-done.16.first_other
  64.8 3.6 %experts.1 = bf16[3072,128]{1,0:T(8,128)(2,1)S(1)} custom-call(bf16[3072,128]{1,0:T(8,128)(2,1)S(1)} %bitcast.12, bf16[2,2048,512]{2,1,0:T(8,128)(2,1)S(1)} %copy-done.1, bf16[512,2048]{1,0:T(8,128)(2,1)S(1)} %copy-done.4, bf16[2,2048,512]{2,1,0:T(8,128)(2,1)S(1)} %collective-permute-done.16.first_other, ...), custom_call_target="tpu_custom_call" | custom-call | flops 5000000000 | bytes 15000000 | tf_op jit(solution)/shard_map/experts/pallas_call | solution.py:428
  68.5 17.6 %all_to_all.11 = bf16[64,48,128]{2,1,0:T(8,128)(2,1)S(1)} all-to-all(bf16[64,48,128]{2,1,0:T(8,128)(2,1)S(1)} %bitcast.14), channel_id=1, replica_groups=mesh['x'=4,'z'=4,'y'=4,'c'=2] {'x','z','y'}, dimensions={0} | all-to-all | bytes 1572864 | tf_op jit(solution)/shard_map/all_to_all | solution.py:474
  86.1 1.2 %combine.1 = bf16[16,2048]{1,0:T(8,128)(2,1)} custom-call(f32[16,2048]{1,0:T(8,128)S(1)} %get-tuple-element.54.residual_ref, f32[16,3072]{1,0:T(8,128)S(1)} %get-tuple-element.55.wide_ref, bf16[3072,128]{1,0:T(8,128)(2,1)S(1)} %bitcast.13), custom_call_target="tpu_custom_call" | custom-call | flops 1000000000 | bytes 3000000 | tf_op jit(solution)/shard_map/combine/pallas_call | solution.py:460
  (5 shorter events, 0.0 us)
Async XLA Ops:
  0.0 2.5 %collective-permute-start = (bf16[3,64,2048]{2,1,0:T(8,128)(2,1)}, bf16[3,64,2048]{2,1,0:T(8,128)(2,1)S(1)}, u32[]{:S(2)}, u32[]{:S(2)}) collective-permute-start(bf16[3,64,2048]{2,1,0:T(8,128)(2,1)} %bitcast.17), channel_id=1, source_target_pairs={{0,1},{1,0},{2,3},{3,2},{4,5},{5,4},{6,7},{7,6},{8,9},{9,8},{10,11... | collective-permute-start | bytes 2359304 | tf_op jit(solution)/shard_map/ppermute | solution.py:24
  0.0 1.6 %copy-start.3 = (bf16[512,2048]{1,0:T(8,128)(2,1)S(1)}, bf16[512,2048]{1,0:T(8,128)(2,1)}, u32[]{:S(2)}) copy-start(bf16[512,2048]{1,0:T(8,128)(2,1)} %param.10) | copy-start | bytes 6291460
  1.6 1.1 %copy-start.5 = (bf16[3,2048,64]{1,2,0:T(8,128)(2,1)S(1)}, bf16[3,2048,64]{1,2,0:T(8,128)(2,1)}, u32[]{:S(2)}) copy-start(bf16[3,2048,64]{1,2,0:T(8,128)(2,1)} %param.12) | copy-start | bytes 2359300
  1.6 1.1 %copy-start.7 = (f32[2048]{0:T(1024)S(1)}, f32[2048]{0:T(1024)}, u32[]{:S(2)}) copy-start(f32[2048]{0:T(1024)} %param.11) | copy-start | bytes 24580
  2.0 4.8 %copy-start = (bf16[64,2048]{1,0:T(8,128)(2,1)S(1)}, bf16[64,2048]{1,0:T(8,128)(2,1)}, u32[]{:S(2)}) copy-start(bf16[64,2048]{1,0:T(8,128)(2,1)} %refs_0_) | copy-start | bytes 786436
  2.0 12.9 %copy-start.2 = (f32[8256,64]{0,1:T(8,128)S(1)}, f32[8256,64]{0,1:T(8,128)}, u32[]{:S(2)}) copy-start(f32[8256,64]{0,1:T(8,128)} %param.13) | copy-start | bytes 6340612
  3.6 10.4 %collective-permute-start.4 = (bf16[256,256]{1,0:T(8,128)(2,1)S(1)}, bf16[256,256]{1,0:T(8,128)(2,1)S(1)}, u32[]{:S(2)}, u32[]{:S(2)}) collective-permute-start(bf16[256,256]{1,0:T(8,128)(2,1)S(1)} %get-tuple-element.35.kv0), channel_id=1, source_target_pairs={{0,96},{32,0},{64,32},{96,64},{1,97},{33,1},{65,33},{97,65},{2,98}... | collective-permute-start | bytes 393224 | tf_op jit(solution)/shard_map/ppermute | solution.py:28
  6.5 6.7 %collective-permute-start.1 = (bf16[128,256]{1,0:T(8,128)(2,1)S(1)}, bf16[128,256]{1,0:T(8,128)(2,1)S(1)}, u32[]{:S(2)}, u32[]{:S(2)}) collective-permute-start(bf16[128,256]{1,0:T(8,128)(2,1)S(1)} %get-tuple-element.34.q_own_ref), channel_id=1, source_target_pairs={{0,1},{1,0},{2,3},{3,2},{4,5},{5,4},{6,7},{7,6},{8,9},{9,8},{10,11... | collective-permute-start | bytes 196616 | tf_op jit(solution)/shard_map/ppermute | solution.py:24
  6.7 16.8 %collective-permute-start.7 = (bf16[64,2048]{1,0:T(8,128)(2,1)S(1)}, bf16[64,2048]{1,0:T(8,128)(2,1)S(1)}, u32[]{:S(2)}, u32[]{:S(2)}) collective-permute-start(bf16[64,2048]{1,0:T(8,128)(2,1)S(1)} %copy-done), channel_id=1, source_target_pairs={{0,4},{2,6},{4,0},{6,2},{1,5},{3,7},{5,1},{7,3},{8,12},{10,14},{12... | collective-permute-start | bytes 786440 | tf_op jit(solution)/shard_map/ppermute | solution.py:28
  9.9 13.6 %collective-permute-start.6 = (bf16[64,2048]{1,0:T(8,128)(2,1)S(1)}, bf16[64,2048]{1,0:T(8,128)(2,1)S(1)}, u32[]{:S(2)}, u32[]{:S(2)}) collective-permute-start(bf16[64,2048]{1,0:T(8,128)(2,1)S(1)} %copy-done), channel_id=1, source_target_pairs={{0,2},{2,4},{4,6},{6,0},{1,3},{3,5},{5,7},{7,1},{8,10},{10,12},{12... | collective-permute-start | bytes 786440 | tf_op jit(solution)/shard_map/ppermute | solution.py:28
  10.6 13.0 %collective-permute-start.8 = (bf16[64,2048]{1,0:T(8,128)(2,1)S(1)}, bf16[64,2048]{1,0:T(8,128)(2,1)S(1)}, u32[]{:S(2)}, u32[]{:S(2)}) collective-permute-start(bf16[64,2048]{1,0:T(8,128)(2,1)S(1)} %copy-done), channel_id=1, source_target_pairs={{0,6},{2,0},{4,2},{6,4},{1,7},{3,1},{5,3},{7,5},{8,14},{10,8},{12,... | collective-permute-start | bytes 786440 | tf_op jit(solution)/shard_map/ppermute | solution.py:28
  13.2 7.8 %collective-permute-start.3 = (bf16[256,256]{1,0:T(8,128)(2,1)S(1)}, bf16[256,256]{1,0:T(8,128)(2,1)S(1)}, u32[]{:S(2)}, u32[]{:S(2)}) collective-permute-start(bf16[256,256]{1,0:T(8,128)(2,1)S(1)} %get-tuple-element.35.kv0), channel_id=1, source_target_pairs={{0,64},{32,96},{64,0},{96,32},{1,65},{33,97},{65,1},{97,33},{2,66}... | collective-permute-start | bytes 393224 | tf_op jit(solution)/shard_map/ppermute | solution.py:28
  14.0 8.4 %collective-permute-start.2 = (bf16[256,256]{1,0:T(8,128)(2,1)S(1)}, bf16[256,256]{1,0:T(8,128)(2,1)S(1)}, u32[]{:S(2)}, u32[]{:S(2)}) collective-permute-start(bf16[256,256]{1,0:T(8,128)(2,1)S(1)} %get-tuple-element.35.kv0), channel_id=1, source_target_pairs={{0,32},{32,64},{64,96},{96,0},{1,33},{33,65},{65,97},{97,1},{2,34}... | collective-permute-start | bytes 393224 | tf_op jit(solution)/shard_map/ppermute | solution.py:28
  18.0 6.7 %copy-start.1 = (bf16[2,2048,512]{2,1,0:T(8,128)(2,1)S(1)}, bf16[2,2048,512]{2,1,0:T(8,128)(2,1)}, u32[]{:S(2)}) copy-start(bf16[2,2048,512]{2,1,0:T(8,128)(2,1)} %first_own.1) | copy-start | bytes 12582916
  23.4 2.0 %copy-start.4 = (bf16[512,2048]{1,0:T(8,128)(2,1)S(1)}, bf16[512,2048]{1,0:T(8,128)(2,1)}, u32[]{:S(2)}) copy-start(bf16[512,2048]{1,0:T(8,128)(2,1)} %second_own.1) | copy-start | bytes 6291460
  23.4 1.3 %collective-permute-start.5 = (bf16[256,128]{1,0:T(8,128)(2,1)S(1)}, bf16[256,128]{1,0:T(8,128)(2,1)S(1)}, u32[]{:S(2)}, u32[]{:S(2)}) collective-permute-start(bf16[256,128]{1,0:T(8,128)(2,1)S(1)} %get-tuple-element.37), channel_id=1, source_target_pairs={{0,1},{1,0},{2,3},{3,2},{4,5},{5,4},{6,7},{7,6},{8,9},{9,8},{10,11... | collective-permute-start | bytes 196616 | tf_op jit(solution)/shard_map/ppermute | solution.py:24
  24.8 40.1 %collective-permute-start.16 = (bf16[2,2048,512]{2,1,0:T(8,128)(2,1)S(1)}, bf16[2,2048,512]{2,1,0:T(8,128)(2,1)S(1)}, u32[]{:S(2)}, u32[]{:S(2)}) collective-permute-start(bf16[2,2048,512]{2,1,0:T(8,128)(2,1)S(1)} %copy-done.1), channel_id=1, source_target_pairs={{0,1},{1,0},{2,3},{3,2},{4,5},{5,4},{6,7},{7,6},{8,9},{9,8},{10,11... | collective-permute-start | bytes 12582920 | tf_op jit(solution)/shard_map/ppermute | solution.py:24
  25.0 9.5 %collective-permute-start.12 = (bf16[256,2048]{1,0:T(8,128)(2,1)S(1)}, bf16[256,2048]{1,0:T(8,128)(2,1)S(1)}, u32[]{:S(2)}, u32[]{:S(2)}) collective-permute-start(bf16[256,2048]{1,0:T(8,128)(2,1)S(1)} %pack.1.rest_4_), channel_id=1, source_target_pairs={{0,1},{1,0},{2,3},{3,2},{4,5},{5,4},{6,7},{7,6},{8,9},{9,8},{10,11... | collective-permute-start | bytes 3145736 | tf_op jit(solution)/shard_map/ppermute | solution.py:24
  25.4 39.4 %collective-permute-start.17 = (bf16[512,2048]{1,0:T(8,128)(2,1)S(1)}, bf16[512,2048]{1,0:T(8,128)(2,1)S(1)}, u32[]{:S(2)}, u32[]{:S(2)}) collective-permute-start(bf16[512,2048]{1,0:T(8,128)(2,1)S(1)} %copy-done.4), channel_id=1, source_target_pairs={{0,1},{1,0},{2,3},{3,2},{4,5},{5,4},{6,7},{7,6},{8,9},{9,8},{10,11... | collective-permute-start | bytes 6291464 | tf_op jit(solution)/shard_map/ppermute | solution.py:24
  25.7 5.0 %collective-permute-start.9 = (bf16[64,128]{1,0:T(8,128)(2,1)S(1)}, bf16[64,128]{1,0:T(8,128)(2,1)S(1)}, u32[]{:S(2)}, u32[]{:S(2)}) collective-permute-start(bf16[64,128]{1,0:T(8,128)(2,1)S(1)} %get-tuple-element.40), channel_id=1, source_target_pairs={{0,2},{2,4},{4,6},{6,0},{1,3},{3,5},{5,7},{7,1},{8,10},{10,12},{12... | collective-permute-start | bytes 49160 | tf_op jit(solution)/shard_map/ppermute | solution.py:28
  25.8 5.3 %collective-permute-start.10 = (bf16[64,128]{1,0:T(8,128)(2,1)S(1)}, bf16[64,128]{1,0:T(8,128)(2,1)S(1)}, u32[]{:S(2)}, u32[]{:S(2)}) collective-permute-start(bf16[64,128]{1,0:T(8,128)(2,1)S(1)} %get-tuple-element.41), channel_id=1, source_target_pairs={{0,4},{2,6},{4,0},{6,2},{1,5},{3,7},{5,1},{7,3},{8,12},{10,14},{12... | collective-permute-start | bytes 49160 | tf_op jit(solution)/shard_map/ppermute | solution.py:28
  30.8 3.7 %collective-permute-start.11 = (bf16[64,128]{1,0:T(8,128)(2,1)S(1)}, bf16[64,128]{1,0:T(8,128)(2,1)S(1)}, u32[]{:S(2)}, u32[]{:S(2)}) collective-permute-start(bf16[64,128]{1,0:T(8,128)(2,1)S(1)} %get-tuple-element.42), channel_id=1, source_target_pairs={{0,6},{2,0},{4,2},{6,4},{1,7},{3,1},{5,3},{7,5},{8,14},{10,8},{12,... | collective-permute-start | bytes 49160 | tf_op jit(solution)/shard_map/ppermute | solution.py:28
  34.5 7.4 %copy-start.8 = (f32[2048]{0:T(1024)S(1)}, f32[2048]{0:T(1024)}, u32[]{:S(2)}) copy-start(f32[2048]{0:T(1024)} %param.15) | copy-start | bytes 24580
  34.5 7.4 %copy-start.9 = (s32[16,8]{0,1:T(8,128)S(1)}, s32[16,8]{0,1:T(8,128)}, u32[]{:S(2)}) copy-start(s32[16,8]{0,1:T(8,128)} %param.17) | copy-start | bytes 1540
  35.3 8.4 %collective-permute-start.13 = (bf16[16,2048]{1,0:T(8,128)(2,1)S(1)}, bf16[16,2048]{1,0:T(8,128)(2,1)S(1)}, u32[]{:S(2)}, u32[]{:S(2)}) collective-permute-start(bf16[16,2048]{1,0:T(8,128)(2,1)S(1)} %get-tuple-element.48), channel_id=1, source_target_pairs={{0,8},{8,16},{16,24},{24,0},{1,9},{9,17},{17,25},{25,1},{2,10},{10... | collective-permute-start | bytes 196616 | tf_op jit(solution)/shard_map/ppermute | solution.py:28
  37.2 6.5 %collective-permute-start.14 = (bf16[16,2048]{1,0:T(8,128)(2,1)S(1)}, bf16[16,2048]{1,0:T(8,128)(2,1)S(1)}, u32[]{:S(2)}, u32[]{:S(2)}) collective-permute-start(bf16[16,2048]{1,0:T(8,128)(2,1)S(1)} %get-tuple-element.49), channel_id=1, source_target_pairs={{0,16},{8,24},{16,0},{24,8},{1,17},{9,25},{17,1},{25,9},{2,18},{10... | collective-permute-start | bytes 196616 | tf_op jit(solution)/shard_map/ppermute | solution.py:28
  40.8 4.3 %collective-permute-start.15 = (bf16[16,2048]{1,0:T(8,128)(2,1)S(1)}, bf16[16,2048]{1,0:T(8,128)(2,1)S(1)}, u32[]{:S(2)}, u32[]{:S(2)}) collective-permute-start(bf16[16,2048]{1,0:T(8,128)(2,1)S(1)} %get-tuple-element.50), channel_id=1, source_target_pairs={{0,24},{8,0},{16,8},{24,16},{1,25},{9,1},{17,9},{25,17},{2,26},{10... | collective-permute-start | bytes 196616 | tf_op jit(solution)/shard_map/ppermute | solution.py:28
  41.9 3.2 %copy-start.6 = (bf16[2048,64]{0,1:T(8,128)(2,1)S(1)}, bf16[2048,64]{0,1:T(8,128)(2,1)}, u32[]{:S(2)}) copy-start(bf16[2048,64]{0,1:T(8,128)(2,1)} %param.16) | copy-start | bytes 786436

commit v7 on v6

--- a/solution.py
+++ b/solution.py
@@ -22,6 +22,10 @@
 
 def swap_core(array):
     return lax.ppermute(array, "c", [(0, 1), (1, 0)])
+
+
+def pair(array, axis, bits):
+    return lax.ppermute(array, axis, [(i, i ^ bits) for i in range(4)])
 
 
 def shift(array, axis, step):
@@ -136,7 +140,7 @@
         if number == 0:
             weights = jnp.where(allowed, weights, 0.0)
         else:
-            weights = jnp.where(shard >= number, weights, 0.0)
+            weights = jnp.where((shard ^ number) < shard, weights, 0.0)
         total = total + jnp.dot(
             kv[HD:, :], weights.astype(jnp.bfloat16), preferred_element_type=jnp.float32
         )
@@ -222,26 +226,52 @@
     )(normed, gain.reshape(1, D), own, other)
 
 
-def attend_kernel(mine_ref, received_ref, *rest):
-    outs, scratch = rest[:4], rest[4]
+def attend_kernel(mine_ref, received_ref, keep_ref, first_ref, second_ref, scratch):
     raw = (mine_ref[...] + received_ref[...].astype(jnp.float32)) / HD
     scratch[...] = norm_scaled(raw, 1.0).reshape(4, 64, HD)
-    for step, out in enumerate(outs):
-        at = pl.multiple_of(lax.rem(lax.axis_index("y") + step, 4) * SLAB, SLAB)
-        out[...] = scratch[:, pl.ds(at, SLAB), :].reshape(64, HD).astype(jnp.bfloat16)
+
+    def block(bits):
+        at = pl.multiple_of((lax.axis_index("y") ^ bits) * SLAB, SLAB)
+        return scratch[:, pl.ds(at, SLAB), :].reshape(64, HD).astype(jnp.bfloat16)
+
+    keep_ref[...] = block(0)
+    first_ref[:64, :] = block(1)
+    first_ref[64:, :] = block(2)
+    second_ref[...] = block(3)
 
 
 def attend_part(mine, received):
     return pl.pallas_call(
         attend_kernel,
-        out_shape=(jax.ShapeDtypeStruct((64, HD), jnp.bfloat16),) * 4,
+        out_shape=(
+            jax.ShapeDtypeStruct((64, HD), jnp.bfloat16),
+            jax.ShapeDtypeStruct((128, HD), jnp.bfloat16),
+            jax.ShapeDtypeStruct((64, HD), jnp.bfloat16),
+        ),
         in_specs=[VMEM, VMEM],
-        out_specs=(VMEM,) * 4,
+        out_specs=(VMEM,) * 3,
         scratch_shapes=[pltpu.VMEM((4, 64, HD), jnp.float32)],
         compiler_params=room(2),
         cost_estimate=cost(0.7),
         name="attend",
     )(mine, received)
+
+
+def relay_kernel(own_ref, received_ref, out_ref):
+    out_ref[:64, :] = own_ref[...]
+    out_ref[64:, :] = received_ref[64:, :]
+
+
+def relay_part(own, received):
+    return pl.pallas_call(
+        relay_kernel,
+        out_shape=jax.ShapeDtypeStruct((128, HD), jnp.bfloat16),
+        in_specs=[VMEM, VMEM],
+        out_specs=VMEM,
+        compiler_params=room(2),
+        cost_estimate=cost(0.2),
+        name="relay",
+    )(own, received)
 
 
 def pack_kernel(*refs):
@@ -262,8 +292,8 @@
 
 
 def output_kernel(*rest):
-    pieces, own, other, outs, scratch = rest[:4], rest[4], rest[5], rest[6:10], rest[10]
-    loaded = [piece[...] for piece in pieces]
+    pieces, own, other, outs, scratch = rest[:3], rest[3], rest[4], rest[5:9], rest[9]
+    loaded = [pieces[0][...], pieces[1][:64, :], pieces[2][:64, :], pieces[2][64:, :]]
     for at in range(0, D, 512):
         total = jnp.zeros((64, 512), jnp.float32)
         for step in range(4):
@@ -288,7 +318,7 @@
         output_kernel,
         out_shape=(jax.ShapeDtypeStruct((SLAB, D), jnp.float32),)
         + (jax.ShapeDtypeStruct((SLAB, D), jnp.bfloat16),) * 3,
-        in_specs=[VMEM] * 6,
+        in_specs=[VMEM] * 5,
         out_specs=(VMEM,) * 4,
         scratch_shapes=[pltpu.VMEM((64, D), jnp.float32)],
         compiler_params=room(2),
@@ -490,11 +520,12 @@
 ):
     own_weights = head_weights.transpose(0, 2, 1)
     other_weights = swap_core(own_weights)
+    output_near = pair(output_weight, "y", 1)
+    output_own = [output_weight, output_near, pair(output_weight, "y", 3), pair(output_near, "y", 3)]
     normed, slab = norm_part(tokens)
     q_own, kv = project_part(normed, attention_gain, own_weights, other_weights)
-    kvs = [kv] + [shift(kv, "x", step) for step in (1, 2, 3)]
-    gathered = {step: shift(output_weight, "y", step) for step in (1, 3, 2)}
-    output_own = [output_weight, gathered[1], gathered[2], gathered[3]]
+    kv_near = pair(kv, "x", 1)
+    kvs = [kv, kv_near, pair(kv_near, "x", 3), pair(kv, "x", 3)]
     q_other = swap_core(q_own)
     rows_map, lanes_map, gain = map_part(expert_index.T, expert_gain)
 
@@ -504,9 +535,10 @@
     received, output_own = tied[0], pack_part(tied[3:])
     first_other, second_other = swap_core(tied[1]), swap_core(tied[2])
     output_other = swap_core(output_own)
-    pieces = attend_part(mine, received)
-    pieces = [pieces[0]] + [shift(pieces[step], "y", step) for step in (1, 2, 3)]
-    sums = output_part(pieces, output_own, output_other)
+    kept, first, second = attend_part(mine, received)
+    first = pair(first, "y", 1)
+    second = pair(relay_part(second, first), "y", 3)
+    sums = output_part((kept, first, second), output_own, output_other)
     summed = [shift(sums[step], "z", step) for step in (1, 2, 3)]
     residual, outgoing, wide = dispatch_part(
         slab, sums[0], summed, gain, router_weight.T, rows_map, lanes_map

time: 87.5 us -> 88.2 us (level)
  blocking collectives: 36.3 us -> 38 us
  waiting for transfers between devices: 14.1 us -> 13.1 us
    ppermute x12 -> x3, starting transfers between devices: 19.7 us -> 6.58 us  [shift(): return lax.ppermute(array, axis, [(i, (i + step) % 4) for i in range(4)])]
    ppermute x0 -> x8, starting transfers between devices: none -> 12.9 us  [pair(): return lax.ppermute(array, axis, [(i, i ^ bits) for i in range(4)])]
    ppermute x12 -> x3, waiting for transfers between devices: 12.4 us -> 1.4 us  [shift(): return lax.ppermute(array, axis, [(i, (i + step) % 4) for i in range(4)])]
    ppermute x0 -> x8, waiting for transfers between devices: none -> 10.5 us  [pair(): return lax.ppermute(array, axis, [(i, i ^ bits) for i in range(4)])]
    all_to_all x2, blocking collectives: 36.3 us -> 38 us  [chips(): lax.all_to_all(shaped, CHIP_AXES, split_axis=0, concat_axis=0, tiled=True)]
  transfers between devices with their start and end apart: 18 -> 17, of which waited for: 9 -> 8; matrix products, arithmetic and copies ran while one was open for 0% -> 0% of each run, Pallas kernels for 10% -> 11%
where the time goes in v7:
time: 88.2 us; the launch traced here: 88 us
  blocking collectives  38 us (43%)
  starting transfers between devices  20.3 us (23%)
  Pallas kernels  14.2 us (16%)
  waiting for transfers between devices  13.1 us (15%)
  local copies, waits for them, and re-layouts  2.37 us (3%)
    all_to_all x2, blocking collectives, chips(): lax.all_to_all(shaped, CHIP_AXES, split_axis=0, concat_axis=0, tiled=True)  38 us
    ppermute x8, starting transfers between devices, pair(): return lax.ppermute(array, axis, [(i, i ^ bits) for i in range(4)])  12.9 us
    ppermute x8, waiting for transfers between devices, pair(): return lax.ppermute(array, axis, [(i, i ^ bits) for i in range(4)])  10.5 us
    ppermute x3, starting transfers between devices, shift(): return lax.ppermute(array, axis, [(i, (i + step) % 4) for i in range(4)])  6.58 us
    pallas_call x1, Pallas kernels, expert_part(): pl.pallas_call(expert_kernel, out_shape=jax.ShapeDtypeStruct((TILE_ROWS,...  3.62 us
    pallas_call x1, Pallas kernels, carried_part(): pl.pallas_call(carried_kernel, out_shape=jax.ShapeDtypeStruct((64, SHARD)...  3.19 us
    unnamed x20, local copies, waits for them, and re-layouts  2.37 us
    pallas_call x1, Pallas kernels, map_part(): pl.pallas_call(map_kernel, out_shape=(jax.ShapeDtypeStruct((TILE_ROWS, 25...  1.83 us
  transfers between devices with their start and end apart: 17, of which 8 were waited for; matrix products, arithmetic and copies ran while one was open for 0% of the time, Pallas kernels for 11%

profile of v7, /device:TPU:0, one launch (start us, length us, event | category | flops | bytes accessed | tf_op | source)
XLA Modules:
  0.0 88.0 jit_solution(3702954726265185725)
XLA Ops:
  0.0 0.0 collective-permute-start
  0.0 1.7 %collective-permute-start.6 = (bf16[64,2048]{1,0:T(8,128)(2,1)}, bf16[64,2048]{1,0:T(8,128)(2,1)S(1)}, u32[]{:S(2)}, u32[]{:S(2)}) collective-permute-start(bf16[64,2048]{1,0:T(8,128)(2,1)} %refs_0_), channel_id=1, source_target_pairs={{0,2},{2,0},{4,6},{6,4},{1,3},{3,1},{5,7},{7,5},{8,10},{10,8},{12,... | collective-permute-start | bytes 786440 | tf_op jit(solution)/shard_map/ppermute | solution.py:28
  1.7 0.0 copy-start.3
  1.7 1.6 %copy-done.3 = bf16[512,2048]{1,0:T(8,128)(2,1)S(1)} copy-done((bf16[512,2048]{1,0:T(8,128)(2,1)S(1)}, bf16[512,2048]{1,0:T(8,128)(2,1)}, u32[]{:S(2)}) %copy-start.3) | copy-done | bytes 2097176
  3.3 0.0 copy-start.5
  3.3 0.0 copy-start.7
  3.3 0.4 norm.1
  3.6 0.0 copy-start
  3.6 0.0 copy-start.2
  3.6 0.0 collective-permute-done.other_ref
  3.7 0.7 copy-done.5
  4.4 0.0 copy-done.7
  4.4 0.8 project.1
  5.2 1.6 %collective-permute-start.2 = (bf16[256,256]{1,0:T(8,128)(2,1)S(1)}, bf16[256,256]{1,0:T(8,128)(2,1)S(1)}, u32[]{:S(2)}, u32[]{:S(2)}) collective-permute-start(bf16[256,256]{1,0:T(8,128)(2,1)S(1)} %get-tuple-element.34.kv0), channel_id=1, source_target_pairs={{0,32},{32,0},{64,96},{96,64},{1,33},{33,1},{65,97},{97,65},{2,34}... | collective-permute-start | bytes 393224 | tf_op jit(solution)/shard_map/ppermute | solution.py:28
  6.8 0.0 collective-permute-start.1
  6.8 0.0 copy-done
  6.8 2.2 %collective-permute-start.7 = (bf16[64,2048]{1,0:T(8,128)(2,1)S(1)}, bf16[64,2048]{1,0:T(8,128)(2,1)S(1)}, u32[]{:S(2)}, u32[]{:S(2)}) collective-permute-start(bf16[64,2048]{1,0:T(8,128)(2,1)S(1)} %copy-done), channel_id=1, source_target_pairs={{0,6},{2,4},{4,2},{6,0},{1,7},{3,5},{5,3},{7,1},{8,14},{10,12},{12... | collective-permute-start | bytes 786440 | tf_op jit(solution)/shard_map/ppermute | solution.py:28
  9.0 0.0 collective-permute-done.6.refs_1_
  9.0 3.0 %collective-permute-start.8 = (bf16[64,2048]{1,0:T(8,128)(2,1)S(1)}, bf16[64,2048]{1,0:T(8,128)(2,1)S(1)}, u32[]{:S(2)}, u32[]{:S(2)}) collective-permute-start(bf16[64,2048]{1,0:T(8,128)(2,1)S(1)} %collective-permute-done.6.refs_1_), channel_id=1, source_target_pairs={{0,6},{2,4},{4,2},{6,0},{1,7},{3,5},{5,3},{7,1},{8,14},{10,12},{12... | collective-permute-start | bytes 786440 | tf_op jit(solution)/shard_map/ppermute | solution.py:28
  12.0 2.8 %collective-permute-start.4 = (bf16[256,256]{1,0:T(8,128)(2,1)S(1)}, bf16[256,256]{1,0:T(8,128)(2,1)S(1)}, u32[]{:S(2)}, u32[]{:S(2)}) collective-permute-start(bf16[256,256]{1,0:T(8,128)(2,1)S(1)} %get-tuple-element.34.kv0), channel_id=1, source_target_pairs={{0,96},{32,64},{64,32},{96,0},{1,97},{33,65},{65,33},{97,1},{2,98}... | collective-permute-start | bytes 393224 | tf_op jit(solution)/shard_map/ppermute | solution.py:28
  14.8 0.0 collective-permute-done.2.kv1
  14.8 0.5 collective-permute-start.3
  15.3 0.0 collective-permute-done.1.q_other_ref
  15.3 0.0 copy-done.2
  15.3 3.2 %carried.1.carried_ref = f32[64,512]{1,0:T(8,128)S(1)} custom-call(f32[64,8256]{1,0:T(8,128)S(1)} %bitcast.15, bf16[128,256]{1,0:T(8,128)(2,1)S(1)} %get-tuple-element.33.q_own_ref, bf16[128,256]{1,0:T(8,128)(2,1)S(1)} %collective-permute-done.1.q_other_ref), custom_call_target="tpu_custom_call" | custom-call | flops 5000000000 | bytes 15000000 | tf_op jit(solution)/shard_map/carried/pallas_call | solution.py:108
  18.5 0.0 copy-start.1
  18.5 0.2 collective-permute-done.4.kv3
  18.7 2.4 %collective-permute-done.3.kv2 = bf16[256,256]{1,0:T(8,128)(2,1)S(1)} collective-permute-done((bf16[256,256]{1,0:T(8,128)(2,1)S(1)}, bf16[256,256]{1,0:T(8,128)(2,1)S(1)}, u32[]{:S(2)}, u32[]{:S(2)}) %collective-permute-start.3) | collective-permute-done | bytes 131104 | tf_op jit(solution)/shard_map/ppermute | solution.py:28
  21.0 1.1 %window.1 = (f32[256,128]{1,0:T(8,128)S(1)}, bf16[256,128]{1,0:T(8,128)(2,1)S(1)}) custom-call(bf16[128,256]{1,0:T(8,128)(2,1)S(1)} %get-tuple-element.33.q_own_ref, bf16[128,256]{1,0:T(8,128)(2,1)S(1)} %collective-permute-done.1.q_other_ref, bf16[256,256]{1,0:T(8,128)(2,1)S(1)} %get-tuple-element.34.kv0, bf16[256,256]{1,0:T(8,128)(2,1)S(1)} %collective-permute-done.2.kv1, ...), custom_call_target="tpu_custom_call" | custom-call | flops 2000000000 | bytes 6000000 | tf_op jit(solution)/shard_map/window/pallas_call | solution.py:154
  22.1 0.0 copy-start.4
  22.1 0.1 collective-permute-start.5
  22.2 0.0 collective-permute-done.7.refs_2_
  22.3 0.1 collective-permute-done.8.refs_3_
  22.4 1.1 %collective-permute-done.5.received_ref = bf16[256,128]{1,0:T(8,128)(2,1)S(1)} collective-permute-done((bf16[256,128]{1,0:T(8,128)(2,1)S(1)}, bf16[256,128]{1,0:T(8,128)(2,1)S(1)}, u32[]{:S(2)}, u32[]{:S(2)}) %collective-permute-start.5) | collective-permute-done | bytes 65568 | tf_op jit(solution)/shard_map/ppermute | solution.py:24
  23.5 0.0 copy-done.1
  23.5 0.2 collective-permute-start.15
  23.6 0.1 pack.1.rest_3_
  23.7 0.4 collective-permute-start.11
  24.1 0.0 copy-done.4
  24.2 0.2 collective-permute-start.16
  24.3 0.1 attend.1
  24.4 0.2 collective-permute-start.9
  24.7 3.8 %collective-permute-done.9.received_ref.rest_1_ = bf16[128,128]{1,0:T(8,128)(2,1)S(1)} collective-permute-done((bf16[128,128]{1,0:T(8,128)(2,1)S(1)}, bf16[128,128]{1,0:T(8,128)(2,1)S(1)}, u32[]{:S(2)}, u32[]{:S(2)}) %collective-permute-start.9) | collective-permute-done | bytes 32800 | tf_op jit(solution)/shard_map/ppermute | solution.py:28
  28.4 1.0 %collective-permute-start.10 = (bf16[128,128]{1,0:T(8,128)(2,1)S(1)}, bf16[128,128]{1,0:T(8,128)(2,1)S(1)}, u32[]{:S(2)}, u32[]{:S(2)}) collective-permute-start(bf16[128,128]{1,0:T(8,128)(2,1)S(1)} %relay.1), channel_id=1, source_target_pairs={{0,6},{2,4},{4,2},{6,0},{1,7},{3,5},{5,3},{7,1},{8,14},{10,12},{12... | collective-permute-start | bytes 98312 | tf_op jit(solution)/shard_map/ppermute | solution.py:28
  29.5 4.1 %collective-permute-done.10.rest_2_ = bf16[128,128]{1,0:T(8,128)(2,1)S(1)} collective-permute-done((bf16[128,128]{1,0:T(8,128)(2,1)S(1)}, bf16[128,128]{1,0:T(8,128)(2,1)S(1)}, u32[]{:S(2)}, u32[]{:S(2)}) %collective-permute-start.10) | collective-permute-done | bytes 32800 | tf_op jit(solution)/shard_map/ppermute | solution.py:28
  33.6 0.0 collective-permute-done.11.rest_4_
  33.6 0.8 output.1
  34.3 2.0 %collective-permute-start.12 = (bf16[16,2048]{1,0:T(8,128)(2,1)S(1)}, bf16[16,2048]{1,0:T(8,128)(2,1)S(1)}, u32[]{:S(2)}, u32[]{:S(2)}) collective-permute-start(bf16[16,2048]{1,0:T(8,128)(2,1)S(1)} %get-tuple-element.46), channel_id=1, source_target_pairs={{0,8},{8,16},{16,24},{24,0},{1,9},{9,17},{17,25},{25,1},{2,10},{10... | collective-permute-start | bytes 196616 | tf_op jit(solution)/shard_map/ppermute | solution.py:32
  36.3 3.6 %collective-permute-start.13 = (bf16[16,2048]{1,0:T(8,128)(2,1)S(1)}, bf16[16,2048]{1,0:T(8,128)(2,1)S(1)}, u32[]{:S(2)}, u32[]{:S(2)}) collective-permute-start(bf16[16,2048]{1,0:T(8,128)(2,1)S(1)} %get-tuple-element.47), channel_id=1, source_target_pairs={{0,16},{8,24},{16,0},{24,8},{1,17},{9,25},{17,1},{25,9},{2,18},{10... | collective-permute-start | bytes 196616 | tf_op jit(solution)/shard_map/ppermute | solution.py:32
  39.9 1.0 %collective-permute-start.14 = (bf16[16,2048]{1,0:T(8,128)(2,1)S(1)}, bf16[16,2048]{1,0:T(8,128)(2,1)S(1)}, u32[]{:S(2)}, u32[]{:S(2)}) collective-permute-start(bf16[16,2048]{1,0:T(8,128)(2,1)S(1)} %get-tuple-element.48), channel_id=1, source_target_pairs={{0,24},{8,0},{16,8},{24,16},{1,25},{9,1},{17,9},{25,17},{2,26},{10... | collective-permute-start | bytes 196616 | tf_op jit(solution)/shard_map/ppermute | solution.py:32
  40.9 0.0 copy-done.8
  40.9 0.0 copy-done.9
  40.9 1.8 %maps.1 = (bf16[3072,256]{1,0:T(8,128)(2,1)S(1)}, f32[16,3072]{1,0:T(8,128)S(1)}, f32[1,2048]{1,0:T(1,128)S(1)}) custom-call(s32[8,16]{1,0:T(8,128)S(1)} %bitcast.22, f32[1,2048]{1,0:T(1,128)S(1)} %bitcast.21), custom_call_target="tpu_custom_call" | custom-call | flops 2000000000 | bytes 6000000 | tf_op jit(solution)/shard_map/maps/pallas_call | solution.py:380
  42.8 0.0 collective-permute-done.12.r1
  42.8 0.1 collective-permute-done.13.r2
  42.9 1.3 %collective-permute-done.14.r3 = bf16[16,2048]{1,0:T(8,128)(2,1)S(1)} collective-permute-done((bf16[16,2048]{1,0:T(8,128)(2,1)S(1)}, bf16[16,2048]{1,0:T(8,128)(2,1)S(1)}, u32[]{:S(2)}, u32[]{:S(2)}) %collective-permute-start.14) | collective-permute-done | bytes 65568 | tf_op jit(solution)/shard_map/ppermute | solution.py:32
  44.2 0.0 copy-done.6
  44.2 1.0 %dispatch.1 = (f32[16,2048]{1,0:T(8,128)S(1)}, bf16[3072,128]{1,0:T(8,128)(2,1)S(1)}, f32[16,3072]{1,0:T(8,128)S(1)}) custom-call(bf16[16,2048]{1,0:T(8,128)(2,1)S(1)} %get-tuple-element.31.slab_ref, f32[16,2048]{1,0:T(8,128)S(1)} %get-tuple-element.45.own_ref, bf16[16,2048]{1,0:T(8,128)(2,1)S(1)} %collective-permute-done.12.r1, ...), custom_call_target="tpu_custom_call" | custom-call | flops 1000000000 | bytes 3000000 | tf_op jit(solution)/shard_map/dispatch/pallas_call | solution.py:418
  45.2 20.3 %all_to_all.10 = bf16[64,48,128]{2,1,0:T(8,128)(2,1)S(1)} all-to-all(bf16[64,48,128]{2,1,0:T(8,128)(2,1)S(1)} %bitcast.11), channel_id=1, replica_groups=mesh['x'=4,'z'=4,'y'=4,'c'=2] {'x','z','y'}, dimensions={0} | all-to-all | bytes 1572864 | tf_op jit(solution)/shard_map/all_to_all | solution.py:504
  65.6 0.0 collective-permute-done.16.second_other
  65.6 0.0 collective-permute-done.15.first_other
  65.6 3.6 %experts.1 = bf16[3072,128]{1,0:T(8,128)(2,1)S(1)} custom-call(bf16[3072,128]{1,0:T(8,128)(2,1)S(1)} %bitcast.12, bf16[2,2048,512]{2,1,0:T(8,128)(2,1)S(1)} %copy-done.1, bf16[512,2048]{1,0:T(8,128)(2,1)S(1)} %copy-done.4, bf16[2,2048,512]{2,1,0:T(8,128)(2,1)S(1)} %collective-permute-done.15.first_other, ...), custom_call_target="tpu_custom_call" | custom-call | flops 5000000000 | bytes 15000000 | tf_op jit(solution)/shard_map/experts/pallas_call | solution.py:458
  69.2 17.6 %all_to_all.11 = bf16[64,48,128]{2,1,0:T(8,128)(2,1)S(1)} all-to-all(bf16[64,48,128]{2,1,0:T(8,128)(2,1)S(1)} %bitcast.14), channel_id=1, replica_groups=mesh['x'=4,'z'=4,'y'=4,'c'=2] {'x','z','y'}, dimensions={0} | all-to-all | bytes 1572864 | tf_op jit(solution)/shard_map/all_to_all | solution.py:504
  86.8 1.2 %combine.1 = bf16[16,2048]{1,0:T(8,128)(2,1)} custom-call(f32[16,2048]{1,0:T(8,128)S(1)} %get-tuple-element.52.residual_ref, f32[16,3072]{1,0:T(8,128)S(1)} %get-tuple-element.53.wide_ref, bf16[3072,128]{1,0:T(8,128)(2,1)S(1)} %bitcast.13), custom_call_target="tpu_custom_call" | custom-call | flops 1000000000 | bytes 3000000 | tf_op jit(solution)/shard_map/combine/pallas_call | solution.py:490
  (4 shorter events, 0.0 us)
Async XLA Ops:
  0.0 3.6 %collective-permute-start = (bf16[3,64,2048]{2,1,0:T(8,128)(2,1)}, bf16[3,64,2048]{2,1,0:T(8,128)(2,1)S(1)}, u32[]{:S(2)}, u32[]{:S(2)}) collective-permute-start(bf16[3,64,2048]{2,1,0:T(8,128)(2,1)} %bitcast.17), channel_id=1, source_target_pairs={{0,1},{1,0},{2,3},{3,2},{4,5},{5,4},{6,7},{7,6},{8,9},{9,8},{10,11... | collective-permute-start | bytes 2359304 | tf_op jit(solution)/shard_map/ppermute | solution.py:24
  0.0 9.0 %collective-permute-start.6 = (bf16[64,2048]{1,0:T(8,128)(2,1)}, bf16[64,2048]{1,0:T(8,128)(2,1)S(1)}, u32[]{:S(2)}, u32[]{:S(2)}) collective-permute-start(bf16[64,2048]{1,0:T(8,128)(2,1)} %refs_0_), channel_id=1, source_target_pairs={{0,2},{2,0},{4,6},{6,4},{1,3},{3,1},{5,7},{7,5},{8,10},{10,8},{12,... | collective-permute-start | bytes 786440 | tf_op jit(solution)/shard_map/ppermute | solution.py:28
  1.7 1.6 %copy-start.3 = (bf16[512,2048]{1,0:T(8,128)(2,1)S(1)}, bf16[512,2048]{1,0:T(8,128)(2,1)}, u32[]{:S(2)}) copy-start(bf16[512,2048]{1,0:T(8,128)(2,1)} %param.10) | copy-start | bytes 6291460
  3.3 1.1 %copy-start.5 = (bf16[3,2048,64]{1,2,0:T(8,128)(2,1)S(1)}, bf16[3,2048,64]{1,2,0:T(8,128)(2,1)}, u32[]{:S(2)}) copy-start(bf16[3,2048,64]{1,2,0:T(8,128)(2,1)} %param.12) | copy-start | bytes 2359300
  3.3 1.1 %copy-start.7 = (f32[2048]{0:T(1024)S(1)}, f32[2048]{0:T(1024)}, u32[]{:S(2)}) copy-start(f32[2048]{0:T(1024)} %param.11) | copy-start | bytes 24580
  3.6 3.2 %copy-start = (bf16[64,2048]{1,0:T(8,128)(2,1)S(1)}, bf16[64,2048]{1,0:T(8,128)(2,1)}, u32[]{:S(2)}) copy-start(bf16[64,2048]{1,0:T(8,128)(2,1)} %refs_0_) | copy-start | bytes 786436
  3.6 11.6 %copy-start.2 = (f32[8256,64]{0,1:T(8,128)S(1)}, f32[8256,64]{0,1:T(8,128)}, u32[]{:S(2)}) copy-start(f32[8256,64]{0,1:T(8,128)} %param.13) | copy-start | bytes 6340612
  5.2 9.6 %collective-permute-start.2 = (bf16[256,256]{1,0:T(8,128)(2,1)S(1)}, bf16[256,256]{1,0:T(8,128)(2,1)S(1)}, u32[]{:S(2)}, u32[]{:S(2)}) collective-permute-start(bf16[256,256]{1,0:T(8,128)(2,1)S(1)} %get-tuple-element.34.kv0), channel_id=1, source_target_pairs={{0,32},{32,0},{64,96},{96,64},{1,33},{33,1},{65,97},{97,65},{2,34}... | collective-permute-start | bytes 393224 | tf_op jit(solution)/shard_map/ppermute | solution.py:28
  6.8 8.5 %collective-permute-start.1 = (bf16[128,256]{1,0:T(8,128)(2,1)S(1)}, bf16[128,256]{1,0:T(8,128)(2,1)S(1)}, u32[]{:S(2)}, u32[]{:S(2)}) collective-permute-start(bf16[128,256]{1,0:T(8,128)(2,1)S(1)} %get-tuple-element.33.q_own_ref), channel_id=1, source_target_pairs={{0,1},{1,0},{2,3},{3,2},{4,5},{5,4},{6,7},{7,6},{8,9},{9,8},{10,11... | collective-permute-start | bytes 196616 | tf_op jit(solution)/shard_map/ppermute | solution.py:24
  6.8 15.4 %collective-permute-start.7 = (bf16[64,2048]{1,0:T(8,128)(2,1)S(1)}, bf16[64,2048]{1,0:T(8,128)(2,1)S(1)}, u32[]{:S(2)}, u32[]{:S(2)}) collective-permute-start(bf16[64,2048]{1,0:T(8,128)(2,1)S(1)} %copy-done), channel_id=1, source_target_pairs={{0,6},{2,4},{4,2},{6,0},{1,7},{3,5},{5,3},{7,1},{8,14},{10,12},{12... | collective-permute-start | bytes 786440 | tf_op jit(solution)/shard_map/ppermute | solution.py:28
  9.0 13.4 %collective-permute-start.8 = (bf16[64,2048]{1,0:T(8,128)(2,1)S(1)}, bf16[64,2048]{1,0:T(8,128)(2,1)S(1)}, u32[]{:S(2)}, u32[]{:S(2)}) collective-permute-start(bf16[64,2048]{1,0:T(8,128)(2,1)S(1)} %collective-permute-done.6.refs_1_), channel_id=1, source_target_pairs={{0,6},{2,4},{4,2},{6,0},{1,7},{3,5},{5,3},{7,1},{8,14},{10,12},{12... | collective-permute-start | bytes 786440 | tf_op jit(solution)/shard_map/ppermute | solution.py:28
  12.0 6.6 %collective-permute-start.4 = (bf16[256,256]{1,0:T(8,128)(2,1)S(1)}, bf16[256,256]{1,0:T(8,128)(2,1)S(1)}, u32[]{:S(2)}, u32[]{:S(2)}) collective-permute-start(bf16[256,256]{1,0:T(8,128)(2,1)S(1)} %get-tuple-element.34.kv0), channel_id=1, source_target_pairs={{0,96},{32,64},{64,32},{96,0},{1,97},{33,65},{65,33},{97,1},{2,98}... | collective-permute-start | bytes 393224 | tf_op jit(solution)/shard_map/ppermute | solution.py:28
  14.8 6.2 %collective-permute-start.3 = (bf16[256,256]{1,0:T(8,128)(2,1)S(1)}, bf16[256,256]{1,0:T(8,128)(2,1)S(1)}, u32[]{:S(2)}, u32[]{:S(2)}) collective-permute-start(bf16[256,256]{1,0:T(8,128)(2,1)S(1)} %collective-permute-done.2.kv1), channel_id=1, source_target_pairs={{0,96},{32,64},{64,32},{96,0},{1,97},{33,65},{65,33},{97,1},{2,98}... | collective-permute-start | bytes 393224 | tf_op jit(solution)/shard_map/ppermute | solution.py:28
  18.5 5.0 %copy-start.1 = (bf16[2,2048,512]{2,1,0:T(8,128)(2,1)S(1)}, bf16[2,2048,512]{2,1,0:T(8,128)(2,1)}, u32[]{:S(2)}) copy-start(bf16[2,2048,512]{2,1,0:T(8,128)(2,1)} %first_own.1) | copy-start | bytes 12582916
  22.1 2.0 %copy-start.4 = (bf16[512,2048]{1,0:T(8,128)(2,1)S(1)}, bf16[512,2048]{1,0:T(8,128)(2,1)}, u32[]{:S(2)}) copy-start(bf16[512,2048]{1,0:T(8,128)(2,1)} %second_own.1) | copy-start | bytes 6291460
  22.1 1.3 %collective-permute-start.5 = (bf16[256,128]{1,0:T(8,128)(2,1)S(1)}, bf16[256,128]{1,0:T(8,128)(2,1)S(1)}, u32[]{:S(2)}, u32[]{:S(2)}) collective-permute-start(bf16[256,128]{1,0:T(8,128)(2,1)S(1)} %get-tuple-element.36), channel_id=1, source_target_pairs={{0,1},{1,0},{2,3},{3,2},{4,5},{5,4},{6,7},{7,6},{8,9},{9,8},{10,11... | collective-permute-start | bytes 196616 | tf_op jit(solution)/shard_map/ppermute | solution.py:24
  23.5 42.1 %collective-permute-start.15 = (bf16[2,2048,512]{2,1,0:T(8,128)(2,1)S(1)}, bf16[2,2048,512]{2,1,0:T(8,128)(2,1)S(1)}, u32[]{:S(2)}, u32[]{:S(2)}) collective-permute-start(bf16[2,2048,512]{2,1,0:T(8,128)(2,1)S(1)} %copy-done.1), channel_id=1, source_target_pairs={{0,1},{1,0},{2,3},{3,2},{4,5},{5,4},{6,7},{7,6},{8,9},{9,8},{10,11... | collective-permute-start | bytes 12582920 | tf_op jit(solution)/shard_map/ppermute | solution.py:24
  23.7 9.9 %collective-permute-start.11 = (bf16[256,2048]{1,0:T(8,128)(2,1)S(1)}, bf16[256,2048]{1,0:T(8,128)(2,1)S(1)}, u32[]{:S(2)}, u32[]{:S(2)}) collective-permute-start(bf16[256,2048]{1,0:T(8,128)(2,1)S(1)} %pack.1.rest_3_), channel_id=1, source_target_pairs={{0,1},{1,0},{2,3},{3,2},{4,5},{5,4},{6,7},{7,6},{8,9},{9,8},{10,11... | collective-permute-start | bytes 3145736 | tf_op jit(solution)/shard_map/ppermute | solution.py:24
  24.2 41.4 %collective-permute-start.16 = (bf16[512,2048]{1,0:T(8,128)(2,1)S(1)}, bf16[512,2048]{1,0:T(8,128)(2,1)S(1)}, u32[]{:S(2)}, u32[]{:S(2)}) collective-permute-start(bf16[512,2048]{1,0:T(8,128)(2,1)S(1)} %copy-done.4), channel_id=1, source_target_pairs={{0,1},{1,0},{2,3},{3,2},{4,5},{5,4},{6,7},{7,6},{8,9},{9,8},{10,11... | collective-permute-start | bytes 6291464 | tf_op jit(solution)/shard_map/ppermute | solution.py:24
  24.4 4.0 %collective-permute-start.9 = (bf16[128,128]{1,0:T(8,128)(2,1)S(1)}, bf16[128,128]{1,0:T(8,128)(2,1)S(1)}, u32[]{:S(2)}, u32[]{:S(2)}) collective-permute-start(bf16[128,128]{1,0:T(8,128)(2,1)S(1)} %get-tuple-element.39), channel_id=1, source_target_pairs={{0,2},{2,0},{4,6},{6,4},{1,3},{3,1},{5,7},{7,5},{8,10},{10,8},{12,... | collective-permute-start | bytes 98312 | tf_op jit(solution)/shard_map/ppermute | solution.py:28
  28.4 5.1 %collective-permute-start.10 = (bf16[128,128]{1,0:T(8,128)(2,1)S(1)}, bf16[128,128]{1,0:T(8,128)(2,1)S(1)}, u32[]{:S(2)}, u32[]{:S(2)}) collective-permute-start(bf16[128,128]{1,0:T(8,128)(2,1)S(1)} %relay.1), channel_id=1, source_target_pairs={{0,6},{2,4},{4,2},{6,0},{1,7},{3,5},{5,3},{7,1},{8,14},{10,12},{12... | collective-permute-start | bytes 98312 | tf_op jit(solution)/shard_map/ppermute | solution.py:28
  33.6 7.3 %copy-start.8 = (f32[2048]{0:T(1024)S(1)}, f32[2048]{0:T(1024)}, u32[]{:S(2)}) copy-start(f32[2048]{0:T(1024)} %param.15) | copy-start | bytes 24580
  33.6 7.4 %copy-start.9 = (s32[16,8]{0,1:T(8,128)S(1)}, s32[16,8]{0,1:T(8,128)}, u32[]{:S(2)}) copy-start(s32[16,8]{0,1:T(8,128)} %param.17) | copy-start | bytes 1540
  34.3 8.4 %collective-permute-start.12 = (bf16[16,2048]{1,0:T(8,128)(2,1)S(1)}, bf16[16,2048]{1,0:T(8,128)(2,1)S(1)}, u32[]{:S(2)}, u32[]{:S(2)}) collective-permute-start(bf16[16,2048]{1,0:T(8,128)(2,1)S(1)} %get-tuple-element.46), channel_id=1, source_target_pairs={{0,8},{8,16},{16,24},{24,0},{1,9},{9,17},{17,25},{25,1},{2,10},{10... | collective-permute-start | bytes 196616 | tf_op jit(solution)/shard_map/ppermute | solution.py:32
  36.3 6.5 %collective-permute-start.13 = (bf16[16,2048]{1,0:T(8,128)(2,1)S(1)}, bf16[16,2048]{1,0:T(8,128)(2,1)S(1)}, u32[]{:S(2)}, u32[]{:S(2)}) collective-permute-start(bf16[16,2048]{1,0:T(8,128)(2,1)S(1)} %get-tuple-element.47), channel_id=1, source_target_pairs={{0,16},{8,24},{16,0},{24,8},{1,17},{9,25},{17,1},{25,9},{2,18},{10... | collective-permute-start | bytes 196616 | tf_op jit(solution)/shard_map/ppermute | solution.py:32
  39.9 4.3 %collective-permute-start.14 = (bf16[16,2048]{1,0:T(8,128)(2,1)S(1)}, bf16[16,2048]{1,0:T(8,128)(2,1)S(1)}, u32[]{:S(2)}, u32[]{:S(2)}) collective-permute-start(bf16[16,2048]{1,0:T(8,128)(2,1)S(1)} %get-tuple-element.48), channel_id=1, source_target_pairs={{0,24},{8,0},{16,8},{24,16},{1,25},{9,1},{17,9},{25,17},{2,26},{10... | collective-permute-start | bytes 196616 | tf_op jit(solution)/shard_map/ppermute | solution.py:32
  40.9 3.3 %copy-start.6 = (bf16[2048,64]{0,1:T(8,128)(2,1)S(1)}, bf16[2048,64]{0,1:T(8,128)(2,1)}, u32[]{:S(2)}) copy-start(bf16[2048,64]{0,1:T(8,128)(2,1)} %param.16) | copy-start | bytes 786436
